TPU v7x, 32 devices: a whole 2x2x4 slice. The times are simulated.
32 devices in a mesh: grp: 4 (over x, core), mem: 8 (over z, y).
Axes of the slice: x: 2, y: 2, z: 4, core: 2. Of those that a mesh axis runs over, the one named last changes fastest.
Arguments:
- tiles: bfloat16 [4, 32, 64, 4096], P('grp', 'mem'), may hold values from -0.75 to 0.75
- tile_ids: int32 [4, 4, 32], P(None, None, 'mem'), may hold values from 0 to 383, as said below
- occ_blocks: bfloat16 [384, 4096], P('mem'), may hold values from -0.75 to 0.75
- virt_blocks: bfloat16 [384, 2, 4096], P('mem'), may hold values from -0.75 to 0.75
Outputs:
- chi_band: float32 [1024, 768], P(('grp', 'mem'))
Inputs may be any that keep to these rules, and one draw needn't show every extreme that they name: tile_ids[g,0,c] is an RI block of the group, below 4; tile_ids[g,1,c] is the first or the last of the row blocks c // 4 * 48 to (c // 4 + 1) * 48 - 1; tile_ids[g,2,c] differs from tile_ids[g,1,c] by at most one; tile_ids[g,3,c] is 1 for a live slot and 0 for an empty one; the live slots of a device come first, every device has one or more, and some device has all 4 live.
All inputs are finite; a program needn't handle non-finite values.
Results may differ from a plain program's by a relative error of at most 0.006.
Values may be sent and summed in bfloat16 or wider, within the bound.
No kernel may reach another device: no remote copies, remote signals or barrier semaphores. Data moves between devices by JAX's collectives and lax.ppermute only.
A program may use at most 128 MiB of HBM per device.

v0:
```python
import math

import jax
import jax.numpy as jnp
from jax import lax
from jax.sharding import PartitionSpec as P

RIB = 4
NB = 384


def with_halo(block, sides, width):
    for axis, dim in sides:
        count = lax.axis_size(axis)
        forward = [(i, i + 1) for i in range(count - 1)]
        backward = [(target, source) for source, target in forward]
        low = lax.ppermute(
            lax.slice_in_dim(block, block.shape[dim] - width, None, axis=dim), axis, forward
        )
        high = lax.ppermute(lax.slice_in_dim(block, 0, width, axis=dim), axis, backward)
        block = jnp.concatenate([low, block, high], axis=dim)
    return block


def passed_along(block, axis, distance):
    devices = range(lax.axis_size(axis))
    route = [(i - distance, i) for i in devices if i - distance in devices]
    return lax.ppermute(block, axis, route)


def pick_rows(table, wanted):
    chooser = (
        lax.broadcasted_iota(jnp.int32, (wanted.shape[0], table.shape[0]), 1) == wanted[:, None]
    ).astype(table.dtype)
    picked = jnp.dot(chooser, table, preferred_element_type=jnp.float32).astype(table.dtype)
    return picked


def occ_pick(ids, occ_blocks, first_row):
    block_side = math.isqrt(occ_blocks.shape[1])
    picked = pick_rows(occ_blocks, ids[1] - first_row)
    return picked.reshape(ids.shape[1], block_side, block_side)


def virt_three(ids, virt_rim, first_row):
    count = ids.shape[1]
    block_side = math.isqrt(virt_rim.shape[2])
    local_row = ids[2] - first_row + 2
    virt_diag = pick_rows(virt_rim[:, 0], local_row).reshape(count, block_side, block_side)
    keep_up = (ids[2] + 1 < NB).astype(virt_rim.dtype)
    virt_up = pick_rows(virt_rim[:, 1], local_row) * keep_up[:, None]
    virt_up = virt_up.reshape(count, block_side, block_side)
    virt_down = pick_rows(virt_rim[:, 1], local_row - 1).reshape(count, block_side, block_side)
    virt_down = jnp.transpose(virt_down, (0, 2, 1))
    return jnp.stack([virt_down, virt_diag, virt_up], axis=1)


def half_transform(tile_set, occ_set):
    count, block_side = (occ_set.shape[0], occ_set.shape[1])
    four_dim = tile_set.reshape(count, tile_set.shape[1], block_side, block_side)
    return jnp.einsum(
        "tmn,tPnv->tPmv", occ_set, four_dim, preferred_element_type=jnp.float32
    ).astype(jnp.bfloat16)


def full_transform(half_done, virt_set):
    count, rows_per = (half_done.shape[0], half_done.shape[1])
    rows_out = jnp.einsum(
        "tPmv,tjvs->tjPms", half_done, virt_set, preferred_element_type=jnp.float32
    ).astype(jnp.bfloat16)
    return rows_out.reshape(count, 3, rows_per, half_done.shape[2] * half_done.shape[3])


def pair_terms(rows_in, partner, ids_left, ids_right):
    count_left, rows_per = (rows_in.shape[0], rows_in.shape[2])
    count_right = partner.shape[0]
    flat_width = rows_in.shape[3]
    products = lax.dot_general(
        rows_in.reshape(-1, flat_width),
        partner.reshape(-1, flat_width),
        (((1,), (1,)), ((), ())),
        preferred_element_type=jnp.float32,
    )
    products = products.reshape(count_left, 3, rows_per, count_right, rows_per)
    offsets = lax.broadcasted_iota(jnp.int32, (3,), 0) - 1
    live_left = ids_left[3].astype(jnp.float32)
    live_right = ids_right[3].astype(jnp.float32)
    same_row = ids_right[1][None, None, :] == ids_left[1][:, None, None]
    near_col = ids_right[2][None, None, :] == ids_left[2][:, None, None] + offsets[None, :, None]
    matches = (
        (same_row & near_col).astype(jnp.float32)
        * live_left[:, None, None]
        * live_right[None, None, :]
    )
    blocks_range = lax.broadcasted_iota(jnp.int32, (RIB,), 0)
    left_hot = (ids_left[0][:, None] == blocks_range[None, :]).astype(jnp.float32)
    right_hot = (ids_right[0][:, None] == blocks_range[None, :]).astype(jnp.float32)
    result = jnp.einsum("tp,tju,tjPuQ,uq->pPqQ", left_hot, matches, products, right_hot)
    return result.reshape(RIB * rows_per, RIB * rows_per)


def body(tiles, tile_ids, occ_blocks, virt_blocks):
    group_index = lax.axis_index("grp")
    group_count = lax.axis_size("grp")
    mem_index = lax.axis_index("mem")
    first_row = mem_index * occ_blocks.shape[0]
    mine_tiles = tiles[0]
    ids_own = lax.dynamic_index_in_dim(tile_ids, group_index, 0, keepdims=False)
    ids_low = lax.dynamic_index_in_dim(tile_ids, jnp.maximum(group_index - 1, 0), 0, keepdims=False)
    ids_low = ids_low.at[3].multiply((group_index > 0).astype(jnp.int32))
    ids_high = lax.dynamic_index_in_dim(
        tile_ids, jnp.minimum(group_index + 1, group_count - 1), 0, keepdims=False
    )
    ids_high = ids_high.at[3].multiply((group_index < group_count - 1).astype(jnp.int32))
    virt_rim = with_halo(virt_blocks, (("mem", 0),), 2)
    half_done = half_transform(mine_tiles, occ_pick(ids_own, occ_blocks, first_row))
    transformed = full_transform(half_done, virt_three(ids_own, virt_rim, first_row))
    below_tiles = passed_along(mine_tiles, "grp", 1)
    lower_part = pair_terms(transformed, below_tiles, ids_own, ids_low)
    middle_part = pair_terms(transformed, mine_tiles, ids_own, ids_own)
    reduced = lax.psum_scatter(
        jnp.concatenate([lower_part, middle_part], axis=1), "mem", scatter_dimension=0, tiled=True
    )
    upper_part = passed_along(lower_part, "grp", -1).T
    upper_rows = lax.psum_scatter(upper_part, "mem", scatter_dimension=0, tiled=True)
    return jnp.concatenate([reduced, upper_rows], axis=1)


def solution(mesh):
    placed = (
        P("grp", "mem", None, None),
        P(None, None, "mem"),
        P("mem", None),
        P("mem", None, None),
    )
    return jax.shard_map(
        body, mesh=mesh, in_specs=placed, out_specs=P(("grp", "mem"), None), check_vma=False
    )
```

profile of v0, /device:TPU:1, one launch (start us, length us, event | category | flops | bytes accessed | tf_op | source)
XLA Modules:
  0.0 232.3 jit_solution(3505114116312049159)
XLA Ops:
  6.5 1.6 copy.17
  8.2 4.0 %collective-permute-start = (bf16[2,2,4096]{2,0,1:T(2,128)(2,1)S(1)}, bf16[2,2,4096]{2,0,1:T(2,128)(2,1)S(1)}, u32[]{:S(2)}, u32[]{:S(2)}) collective-permute-start(bf16[2,2,4096]{2,0,1:T(2,128)(2,1)S(1)} %get-tuple-element.17), channel_id=1, source_target_pairs={{0,1},{1,2},{2,3},{3,4},{4,5},{5,6},{6,7},{8,9},{9,10},{10,11},{11... | collective-permute-start | bytes 98312 | tf_op jit(solution)/shard_map/ppermute | solution.py:17
  12.2 1.3 collective-permute-start.1
  13.5 4.0 %collective-permute-start.2 = (bf16[4,64,4096]{2,1,0:T(8,128)(2,1)}, bf16[4,64,4096]{2,1,0:T(8,128)(2,1)}, u32[]{:S(2)}, u32[]{:S(2)}) collective-permute-start(bf16[4,64,4096]{2,1,0:T(8,128)(2,1)} %bitcast.109), channel_id=1, source_target_pairs={{0,8},{8,16},{16,24},{1,9},{9,17},{17,25},{2,10},{10,18},{18,26},{... | collective-permute-start | bytes 6291464 | tf_op jit(solution)/shard_map/ppermute | solution.py:28
  17.5 0.7 constant_dynamic-slice_fusion.1
  18.6 0.7 fusion.39
  19.4 6.9 %reshape_squeeze.4 = bf16[4,64,64,64]{3,2,1,0:T(8,128)(2,1)} reshape(bf16[1,4,64,4096]{3,2,1,0:T(8,128)(2,1)} %param.6) | data formatting | bytes 4194304 | tf_op jit(solution)/shard_map/reshape;squeeze | solution.py:60
  28.3 15.5 %convert_bitcast_fusion = bf16[4,3,64,64,64]{3,4,2,1,0:T(8,128)(2,1)} fusion(bf16[4,64,64,64]{3,2,1,0:T(8,128)(2,1)} %reshape_squeeze.4, bf16[4,1,64,64]{2,3,1,0:T(8,128)(2,1)S(1)} %copy.21, bf16[4,1,64,64]{2,3,1,0:T(8,128)(2,1)S(1)} %copy.20, bf16[4,1,64,64]{2,3,1,0:T(8,128)(2,1)S(1)} %bitcast.110, bf16[4,64,64,1]{2,1,0,3:T(8,128)(2,1)S(1)} %reshape.209), kind=kOutput, calls=%fused_computation | convolution fusion | flops 541360128 | bytes 8519680 | tf_op jit(solution)/shard_map/tPmv,tjvs->tjPms/dot_general | solution.py:68
  43.8 16.7 %copy.22 = bf16[4,3,64,64,64]{4,3,2,1,0:T(8,128)(2,1)} copy(bf16[4,3,64,64,64]{3,4,2,1,0:T(8,128)(2,1)} %convert_bitcast_fusion) | data formatting | bytes 12582912 | tf_op jit(solution)/shard_map/convert_element_type | solution.py:70
  60.5 17.2 %reshape.212 = bf16[4,3,64,4096,1]{3,2,1,0,4:T(8,128)(2,1)} reshape(bf16[4,3,64,64,64]{4,3,2,1,0:T(8,128)(2,1)} %copy.22) | data formatting | bytes 12582912 | tf_op jit(solution)/shard_map/dot_general | solution.py:78
  77.7 5.9 %fusion = bf16[4,3,64,4,64]{4,2,3,1,0:T(8,128)(2,1)S(1)} fusion(bf16[4,3,64,4096,1]{3,2,1,0,4:T(8,128)(2,1)} %reshape.212, bf16[1,4,64,4096]{3,2,1,0:T(8,128)(2,1)S(1)} %copy-done.2), kind=kOutput, calls=%fused_computation.1 | convolution fusion | flops 1610612736 | bytes 8781824 | tf_op jit(solution)/shard_map/dot_general | solution.py:78
  83.6 5.0 %fusion.2 = bf16[4,3,64,4,64]{4,2,3,1,0:T(8,128)(2,1)S(1)} fusion(bf16[4,3,64,4096,1]{3,2,1,0,4:T(8,128)(2,1)S(1)} %copy-done.1, bf16[4,64,4096]{2,1,0:T(8,128)(2,1)} %collective-permute-done.2), kind=kOutput, calls=%fused_computation.3 | convolution fusion | flops 1610612736 | bytes 8781824 | tf_op jit(solution)/shard_map/dot_general | solution.py:78
  88.6 0.8 fusion.13
  89.4 0.4 fusion.17
  90.2 0.3 reshape.207
  90.6 1.9 collective-permute-start.3
  92.5 0.8 fusion.11
  93.3 5.0 %collective-permute-done.3 = f32[256,256]{1,0:T(8,128)S(1)} collective-permute-done((f32[256,256]{1,0:T(8,128)S(1)}, f32[256,256]{1,0:T(8,128)S(1)}, u32[]{:S(2)}, u32[]{:S(2)}) %collective-permute-start.3) | collective-permute-done | bytes 262176 | tf_op jit(solution)/shard_map/ppermute | solution.py:28
  98.3 0.8 copy.42
  99.2 0.4 fusion.15
  100.3 0.9 pad_maximum_fusion.1
  101.2 58.4 %reduce-scatter.7.cloned.1.call-done = f32[32,256]{1,0:T(8,128)} async-done(((f32[256,256]{1,0:T(8,128)}), f32[32,256]{1,0:T(8,128)}) %reduce-scatter.7.cloned.1.call-update) | async-done | bytes 32784 | tf_op jit(solution)/shard_map/reduce_scatter | solution.py:125
  159.6 64.3 %reduce-scatter.5.cloned.1.call-done = f32[32,512]{1,0:T(8,128)} async-done(((f32[256,512]{1,0:T(8,128)}), f32[32,512]{1,0:T(8,128)}) %reduce-scatter.5.cloned.1.call-update) | async-done | bytes 65552 | tf_op jit(solution)/shard_map/reduce_scatter | solution.py:121
  223.9 1.5 pad_maximum_fusion.2
  (39 shorter events, 3.7 us)
Async XLA Ops:
  6.5 11.7 %copy-start = (bf16[48,4096]{1,0:T(8,128)(2,1)S(1)}, bf16[48,4096]{1,0:T(8,128)(2,1)}, u32[]{:S(2)}) copy-start(bf16[48,4096]{1,0:T(8,128)(2,1)} %param.8) | copy-start | bytes 1179652
  6.5 153.0 %reduce-scatter.7.cloned.1.call-start = ((), (), s32[]{:S(2)}) async-start(), calls=%async_computation.3 | async-start | bytes 294912 | tf_op jit(solution)/shard_map/reduce_scatter | solution.py:125
  8.2 18.5 %collective-permute-start = (bf16[2,2,4096]{2,0,1:T(2,128)(2,1)S(1)}, bf16[2,2,4096]{2,0,1:T(2,128)(2,1)S(1)}, u32[]{:S(2)}, u32[]{:S(2)}) collective-permute-start(bf16[2,2,4096]{2,0,1:T(2,128)(2,1)S(1)} %get-tuple-element.17), channel_id=1, source_target_pairs={{0,1},{1,2},{2,3},{3,4},{4,5},{5,6},{6,7},{8,9},{9,10},{10,11},{11... | collective-permute-start | bytes 98312 | tf_op jit(solution)/shard_map/ppermute | solution.py:17
  12.2 14.5 %collective-permute-start.1 = (bf16[2,2,4096]{2,0,1:T(2,128)(2,1)S(1)}, bf16[2,2,4096]{2,0,1:T(2,128)(2,1)S(1)}, u32[]{:S(2)}, u32[]{:S(2)}) collective-permute-start(bf16[2,2,4096]{2,0,1:T(2,128)(2,1)S(1)} %get-tuple-element.18), channel_id=1, source_target_pairs={{1,0},{2,1},{3,2},{4,3},{5,4},{6,5},{7,6},{9,8},{10,9},{11,10},{12... | collective-permute-start | bytes 98312 | tf_op jit(solution)/shard_map/ppermute | solution.py:20
  13.5 70.1 %collective-permute-start.2 = (bf16[4,64,4096]{2,1,0:T(8,128)(2,1)}, bf16[4,64,4096]{2,1,0:T(8,128)(2,1)}, u32[]{:S(2)}, u32[]{:S(2)}) collective-permute-start(bf16[4,64,4096]{2,1,0:T(8,128)(2,1)} %bitcast.109), channel_id=1, source_target_pairs={{0,8},{8,16},{16,24},{1,9},{9,17},{17,25},{2,10},{10,18},{18,26},{... | collective-permute-start | bytes 6291464 | tf_op jit(solution)/shard_map/ppermute | solution.py:28
  60.5 17.2 %copy-start.2 = (bf16[1,4,64,4096]{3,2,1,0:T(8,128)(2,1)S(1)}, bf16[1,4,64,4096]{3,2,1,0:T(8,128)(2,1)}, u32[]{:S(2)}) copy-start(bf16[1,4,64,4096]{3,2,1,0:T(8,128)(2,1)} %param.6) | copy-start | bytes 6291460
  77.7 5.9 %copy-start.1 = (bf16[4,3,64,4096,1]{3,2,1,0,4:T(8,128)(2,1)S(1)}, bf16[4,3,64,4096,1]{3,2,1,0,4:T(8,128)(2,1)}, u32[]{:S(2)}) copy-start(bf16[4,3,64,4096,1]{3,2,1,0,4:T(8,128)(2,1)} %reshape.212) | copy-start | bytes 18874372
  90.6 7.7 %collective-permute-start.3 = (f32[256,256]{1,0:T(8,128)S(1)}, f32[256,256]{1,0:T(8,128)S(1)}, u32[]{:S(2)}, u32[]{:S(2)}) collective-permute-start(f32[256,256]{1,0:T(8,128)S(1)} %reshape.207), channel_id=1, source_target_pairs={{8,0},{16,8},{24,16},{9,1},{17,9},{25,17},{10,2},{18,10},{26,18},{... | collective-permute-start | bytes 786440 | tf_op jit(solution)/shard_map/ppermute | solution.py:28
  99.1 124.8 %reduce-scatter.5.cloned.1.call-start = ((), (), s32[]{:S(2)}) async-start(), calls=%async_computation.2 | async-start | bytes 589824 | tf_op jit(solution)/shard_map/reduce_scatter | solution.py:121
Sparse Core Ops, SparseCore 0:
  99.3 60.2 reduce-scatter.6
  162.9 60.9 reduce-scatter.4
where the time goes:
time: 236 us; the launch traced here: 232 us
  waiting for transfers between devices  128 us (54%)
  local copies, waits for them, and re-layouts  45.8 us (19%)
  matrix products  30.3 us (13%)
  between operations  13.6 us (6%)
  starting transfers between devices  11.2 us (5%)
  other arithmetic  3.6 us (2%)
    reduce_scatter x1, waiting for transfers between devices, body(): lax.psum_scatter(jnp.concatenate([lower_part, middle_part], axis=1), 'mem...  64.3 us
    reduce_scatter x1, waiting for transfers between devices, body(): lax.psum_scatter(upper_part, 'mem', scatter_dimension=0, tiled=True)  58.4 us
    dot_general x1, local copies, waits for them, and re-layouts, pair_terms(): lax.dot_general(rows_in.reshape(-1, flat_width), partner.reshape(-1, flat...  17.2 us
    convert_element_type x1, local copies, waits for them, and re-layouts, full_transform(): rows_out = jnp.einsum('tPmv,tjvs->tjPms', half_done, virt_set, preferred_...  16.7 us
    dot_general x1, matrix products, full_transform(): jnp.einsum('tPmv,tjvs->tjPms', half_done, virt_set, preferred_element_typ...  15.5 us
    dot_general x2, matrix products, pair_terms(): lax.dot_general(rows_in.reshape(-1, flat_width), partner.reshape(-1, flat...  10.9 us
    another operation x1, local copies, waits for them, and re-layouts, half_transform(): tile_set.reshape(count, tile_set.shape[1], block_side, block_side)  6.88 us
    ppermute x2, starting transfers between devices, passed_along(): return lax.ppermute(block, axis, route)  5.88 us
  transfers between devices with their start and end apart: 6, of which 3 were waited for; matrix products, arithmetic and copies ran while one was open for 30% of the time, Pallas kernels for 0%

commit v1 on v0

v1 whole, which is shorter than its diff:
```python
import functools
import math

import jax
import jax.numpy as jnp
from jax import lax
from jax.experimental import pallas as pl
from jax.experimental.pallas import tpu as pltpu
from jax.sharding import PartitionSpec as P

RIB = 4
WIDE = 256
HIGH = lax.Precision.HIGHEST
F32 = jnp.float32
BF16 = jnp.bfloat16
VMEM_BYTES = 48 * 1024 * 1024


def is_odd():
    return lax.rem(lax.axis_index("grp"), 2) == 1


def half_kernel(rows, ids, occ, tiles, half, even, odd, rows_in, rows_out, spread, made):
    side, flat = tiles.shape[2], tiles.shape[3]
    lanes = 2 * side
    high = flat // lanes
    cut = even.shape[2]
    slot = pl.program_id(0)
    group = lax.axis_index("grp")
    first = lax.axis_index("mem") * rows
    end = (ids[group, 1, slot] != first).astype(jnp.int32)
    low = lax.broadcasted_iota(jnp.int32, (high, lanes), 1) < side
    for h in range(high):
        rows_in[h * side : (h + 1) * side, :] = tiles[0, 0, :, h * lanes : (h + 1) * lanes].astype(F32)
    for p in range(0, side, 2):
        one = rows_in[pl.ds(p, high, stride=side), :]
        two = rows_in[pl.ds(p + 1, high, stride=side), :]
        at = slice(p * side, (p + 2) * side)
        spread[:high, at] = jnp.where(low, one, pltpu.roll(two, side, 1)).astype(BF16)
        spread[high:, at] = jnp.where(low, pltpu.roll(one, side, 1), two).astype(BF16)
    made[...] = jnp.dot(occ[end], spread[...], preferred_element_type=F32)
    for p in range(0, side, 2):
        at = slice(p * side, (p + 2) * side)
        top, bottom = made[:high, at], made[high:, at]
        rows_out[pl.ds(p, high, stride=side), :] = jnp.where(low, top, pltpu.roll(bottom, side, 1))
        rows_out[pl.ds(p + 1, high, stride=side), :] = jnp.where(low, pltpu.roll(top, side, 1), bottom)
    for h in range(high):
        half[0, :, h * lanes : (h + 1) * lanes] = rows_out[h * side : (h + 1) * side, :].astype(BF16)

    @pl.when(is_odd())
    def _():
        even[0] = half[0, :, cut:]
        odd[0] = tiles[0, 0, :, :cut]

    @pl.when(jnp.logical_not(is_odd()))
    def _():
        even[0] = tiles[0, 0, :, :cut]
        odd[0] = half[0, :, cut:]


def combined(products, slots, side, ids, left, right, left_on, right_on, total):
    width = slots * side
    owner = lax.broadcasted_iota(jnp.int32, (1, width), 1) // side
    total[...] = jnp.zeros_like(total)
    for t in range(slots):
        term = jnp.zeros((side, width), F32)
        for j in range(3):
            mask = jnp.zeros((1, width), F32)
            for u in range(slots):
                same = (
                    (ids[left, 1, t] == ids[right, 1, u])
                    & (ids[right, 2, u] == ids[left, 2, t] + (j - 1))
                    & (ids[left, 3, t] * left_on * ids[right, 3, u] * right_on > 0)
                )
                mask = jnp.where(owner == u, same.astype(F32), mask)
            at = (t * 3 + j) * side
            term = term + products[at : at + side, :] * mask
        total[ids[left, 0, t]] += term
    row = lax.broadcasted_iota(jnp.int32, (width, RIB * side), 0)
    column = lax.broadcasted_iota(jnp.int32, (width, RIB * side), 1)
    target = jnp.zeros((width, RIB * side), jnp.int32)
    for u in range(slots):
        target = jnp.where(row // side == u, ids[right, 0, u] * side + lax.rem(row, side), target)
    place = (target == column).astype(F32)
    return jnp.dot(total[...].reshape(RIB * side, width), place, precision=HIGH, preferred_element_type=F32)


NT = (((1,), (1,)), ((), ()))
NN = (((1,), (0,)), ((), ()))


def prepare_kernel(rows, ids, half, tiles, table, y_low, v_high, middle, y_all, total):
    slots, side, flat = half.shape
    cut = y_low.shape[1]
    group = lax.axis_index("grp")
    first = lax.axis_index("mem") * rows
    count = rows * lax.axis_size("mem")
    copies = WIDE // side
    own = lax.broadcasted_iota(jnp.int32, (WIDE, WIDE), 0) // side
    own = own == lax.broadcasted_iota(jnp.int32, (WIDE, WIDE), 1) // side

    def spread(block):
        row = jnp.concatenate([block] * copies, axis=1)
        return jnp.where(own, jnp.concatenate([row] * copies, axis=0), jnp.zeros((), BF16))

    for t in range(slots):
        a, b = ids[group, 1, t], ids[group, 2, t]
        at = jnp.where(a == first, 2, 6) + b - a
        keep = (b + 1 < count).astype(F32)
        before = spread(table[at - 1, 1])
        here = spread(table[at, 0])
        after = spread((table[at, 1].astype(F32) * keep).astype(BF16))
        x = jnp.concatenate([half[t, :, c : c + WIDE] for c in range(0, flat, WIDE)], axis=0)
        for j, (mat, dims) in enumerate(((before, NT), (here, NN), (after, NN))):
            y = lax.dot_general(x, mat, dims, preferred_element_type=F32).astype(BF16)
            for c in range(0, flat, WIDE):
                block = y[c // WIDE * side : (c // WIDE + 1) * side]
                y_all[(t * 3 + j) * side : (t * 3 + j + 1) * side, c : c + WIDE] = block
                if c < cut:
                    y_low[(t * 3 + j) * side : (t * 3 + j + 1) * side, c : c + WIDE] = block
        x = jnp.concatenate([tiles[0, t, :, c : c + WIDE] for c in range(cut, flat, WIDE)], axis=0)
        for j, (mat, dims) in enumerate(((before, NT), (here, NT), (after, NN))):
            y = lax.dot_general(x, mat, dims, preferred_element_type=F32).astype(BF16)
            for c in range(0, flat - cut, WIDE):
                block = y[c // WIDE * side : (c // WIDE + 1) * side]
                v_high[(t * 3 + j) * side : (t * 3 + j + 1) * side, c : c + WIDE] = block
    products = lax.dot_general(
        y_all[...], tiles[0].reshape(slots * side, flat), NT, preferred_element_type=F32
    )
    middle[...] = combined(products, slots, side, ids, group, group, 1, 1, total)


def pair_kernel(ids, y_low, v_high, even, odd, lower, upper, out_even, out_odd, below, above, total, sem):
    slots, side, _ = even.shape
    group = lax.axis_index("grp")
    last = lax.axis_size("grp") - 1
    has_below = (group > 0).astype(jnp.int32)
    has_above = (group < last).astype(jnp.int32)
    under, over = jnp.maximum(group - 1, 0), jnp.minimum(group + 1, last)

    @pl.when(is_odd())
    def _():
        pltpu.make_async_copy(even, below, sem.at[0]).start()
        pltpu.make_async_copy(odd, above, sem.at[1]).start()

    @pl.when(jnp.logical_not(is_odd()))
    def _():
        pltpu.make_async_copy(odd, below, sem.at[0]).start()
        pltpu.make_async_copy(even, above, sem.at[1]).start()

    pltpu.make_async_copy(even, below, sem.at[0]).wait()
    products = lax.dot_general(
        y_low[...], below[...].reshape(slots * side, -1), NT, preferred_element_type=F32
    )
    lower[...] = combined(products, slots, side, ids, group, under, 1, has_below, total)
    pltpu.make_async_copy(odd, above, sem.at[1]).wait()
    products = lax.dot_general(
        v_high[...], above[...].reshape(slots * side, -1), NT, preferred_element_type=F32
    )
    upper[...] = combined(products, slots, side, ids, group, over, 1, has_above, total)
    to_below = lower[...].T.astype(BF16)
    to_above = upper[...].T.astype(BF16)
    odd_one = is_odd()
    out_even[...] = jnp.where(odd_one, to_below, to_above)
    out_odd[...] = jnp.where(odd_one, to_above, to_below)


def band_kernel(lower, middle, upper, even, odd, band):
    side = lower.shape[1]
    odd_one = is_odd()
    from_even, from_odd = even[...].astype(F32), odd[...].astype(F32)
    band[:, :side] = (lower[...] + jnp.where(odd_one, from_even, from_odd)).astype(BF16)
    band[:, side : 2 * side] = middle[...].astype(BF16)
    band[:, 2 * side :] = (upper[...] + jnp.where(odd_one, from_odd, from_even)).astype(BF16)


def swapped(block, parity):
    count = lax.axis_size("grp")
    pairs = [(i, i + 1) for i in range(parity, count - 1, 2)]
    return lax.ppermute(block, "grp", pairs + [(b, a) for a, b in pairs])


def params(**more):
    return pltpu.CompilerParams(vmem_limit_bytes=VMEM_BYTES, **more)


WHOLE = pl.BlockSpec(memory_space=pltpu.VMEM)
SCALAR = pl.BlockSpec(memory_space=pltpu.SMEM)


def body(tiles, tile_ids, occ_blocks, virt_blocks):
    slots, side, flat = tiles.shape[1:]
    rows = occ_blocks.shape[0]
    members = lax.axis_size("mem")
    cut = flat // 2
    width = RIB * side

    ends = jnp.concatenate([occ_blocks[:1], occ_blocks[rows - 1 :]], axis=0)
    ends = ends.reshape(2, side // 2, 2, side // 2, 2).transpose(0, 2, 1, 4, 3).reshape(2, side, side)
    one_slot = lambda lanes: pl.BlockSpec((1, side, lanes), lambda i: (i, 0, 0))
    half, even, odd = pl.pallas_call(
        functools.partial(half_kernel, rows),
        grid=(slots,),
        in_specs=[SCALAR, WHOLE, pl.BlockSpec((1, 1, side, flat), lambda i: (0, i, 0, 0))],
        out_specs=[one_slot(flat), one_slot(cut), one_slot(cut)],
        out_shape=[
            jax.ShapeDtypeStruct((slots, side, flat), BF16),
            jax.ShapeDtypeStruct((slots, side, cut), BF16),
            jax.ShapeDtypeStruct((slots, side, cut), BF16),
        ],
        scratch_shapes=[
            pltpu.VMEM((flat // 2, 2 * side), F32),
            pltpu.VMEM((flat // 2, 2 * side), F32),
            pltpu.VMEM((side, flat), BF16),
            pltpu.VMEM((side, flat), F32),
        ],
        compiler_params=params(),
    )(tile_ids, ends, tiles)
    got_odd = swapped(odd, 1)
    got_even = swapped(even, 0)

    forward = [(i, i + 1) for i in range(members - 1)]
    backward = [(b, a) for a, b in forward]
    before = lax.ppermute(virt_blocks[rows - 2 :], "mem", forward)
    after = lax.ppermute(virt_blocks[:1], "mem", backward)
    table = jnp.concatenate([before, virt_blocks[:2], virt_blocks[rows - 3 :], after], axis=0)
    table = table.reshape(8, 2, side, side)

    ids = tile_ids
    y_low, v_high, middle = pl.pallas_call(
        functools.partial(prepare_kernel, rows),
        in_specs=[SCALAR, WHOLE, WHOLE, WHOLE],
        out_specs=[WHOLE, WHOLE, WHOLE],
        out_shape=[
            jax.ShapeDtypeStruct((slots * 3 * side, cut), BF16),
            jax.ShapeDtypeStruct((slots * 3 * side, flat - cut), BF16),
            jax.ShapeDtypeStruct((width, width), F32),
        ],
        scratch_shapes=[
            pltpu.VMEM((slots * 3 * side, flat), BF16),
            pltpu.VMEM((RIB, side, slots * side), F32),
        ],
        compiler_params=params(),
    )(ids, half, tiles, table)
    lower, upper, out_even, out_odd = pl.pallas_call(
        pair_kernel,
        in_specs=[SCALAR, WHOLE, WHOLE, pl.BlockSpec(memory_space=pl.ANY), pl.BlockSpec(memory_space=pl.ANY)],
        out_specs=[WHOLE] * 4,
        out_shape=[jax.ShapeDtypeStruct((width, width), F32)] * 2
        + [jax.ShapeDtypeStruct((width, width), BF16)] * 2,
        scratch_shapes=[
            pltpu.VMEM((slots, side, cut), BF16),
            pltpu.VMEM((slots, side, cut), BF16),
            pltpu.VMEM((RIB, side, slots * side), F32),
            pltpu.SemaphoreType.DMA((2,)),
        ],
        compiler_params=params(),
    )(ids, y_low, v_high, got_even, got_odd)
    back_odd = swapped(out_odd, 1)
    back_even = swapped(out_even, 0)
    band = pl.pallas_call(
        band_kernel,
        in_specs=[WHOLE] * 5,
        out_specs=WHOLE,
        out_shape=jax.ShapeDtypeStruct((width, 3 * width), BF16),
        compiler_params=params(),
    )(lower, middle, upper, back_even, back_odd)
    parts = lax.all_to_all(band.reshape(members, width // members, 3 * width), "mem", 0, 0)
    return parts.astype(F32).sum(axis=0)


def solution(mesh):
    placed = (
        P("grp", "mem", None, None),
        P(None, None, "mem"),
        P("mem", None),
        P("mem", None, None),
    )
    return jax.shard_map(
        body, mesh=mesh, in_specs=placed, out_specs=P(("grp", "mem"), None), check_vma=False
    )
```

time: 236 us -> 73.5 us (0.31); the launches traced: 232 us -> 72.4 us
  waiting for transfers between devices: 128 us -> 5.82 us
  local copies, waits for them, and re-layouts: 45.8 us -> 11.5 us
  matrix products: 30.3 us -> 0 us
  Pallas kernels: 0 us -> 26.5 us
  blocking collectives: 0 us -> 13.5 us
  between operations: 13.6 us -> 0.15 us
  starting transfers between devices: 11.2 us -> 14 us
  other arithmetic: 3.6 us -> 0.94 us
    reduce_scatter x2 -> x0, waiting for transfers between devices: 123 us -> none  [the longest x1 64.3 us: body(): lax.psum_scatter(jnp.concatenate([lower_part, middle_part], axis=1), 'mem...]
    dot_general x13 -> x0, matrix products: 30.3 us -> none  [the longest x1 15.5 us: full_transform(): jnp.einsum('tPmv,tjvs->tjPms', half_done, virt_set, preferred_element_typ...]
    pallas_call x0 -> x4, Pallas kernels: none -> 26.5 us  [the longest x1 10.2 us: body(): pl.pallas_call(functools.partial(prepare_kernel, rows), in_specs=[SCALAR,...]
    dot_general x1 -> x0, local copies, waits for them, and re-layouts: 17.2 us -> none  [pair_terms(): lax.dot_general(rows_in.reshape(-1, flat_width), partner.reshape(-1, flat...]
    convert_element_type x1 -> x0, local copies, waits for them, and re-layouts: 16.7 us -> none  [full_transform(): rows_out = jnp.einsum('tPmv,tjvs->tjPms', half_done, virt_set, preferred_...]
    all_to_all x0 -> x1, blocking collectives: none -> 13.5 us  [body(): lax.all_to_all(band.reshape(members, width // members, 3 * width), 'mem',...]
    another operation x5 -> x0, local copies, waits for them, and re-layouts: 7.34 us -> none  [the longest x1 6.88 us: half_transform(): tile_set.reshape(count, tile_set.shape[1], block_side, block_side)]
    unnamed x8 -> x12, local copies, waits for them, and re-layouts: 2.47 us -> 5.5 us
  transfers between devices with their start and end apart: 6 -> 6, of which waited for: 3 -> 2; matrix products, arithmetic and copies ran while one was open for 30% -> 3% of each run, Pallas kernels for 0% -> 14%
where the time goes in v1:
time: 73.5 us; the launch traced here: 72.4 us
  Pallas kernels  26.5 us (36%)
  starting transfers between devices  14 us (19%)
  blocking collectives  13.5 us (18%)
  local copies, waits for them, and re-layouts  11.5 us (16%)
  waiting for transfers between devices  5.82 us (8%)
  other arithmetic  0.94 us (1%)
    all_to_all x1, blocking collectives, body(): lax.all_to_all(band.reshape(members, width // members, 3 * width), 'mem',...  13.5 us
    pallas_call x1, Pallas kernels, body(): pl.pallas_call(functools.partial(prepare_kernel, rows), in_specs=[SCALAR,...  10.2 us
    ppermute x4, starting transfers between devices, swapped(): return lax.ppermute(block, 'grp', pairs + [(b, a) for a, b in pairs])  9.54 us
    pallas_call x1, Pallas kernels, body(): pl.pallas_call(functools.partial(half_kernel, rows), grid=(slots,), in_sp...  9.22 us
    pallas_call x1, Pallas kernels, body(): pl.pallas_call(pair_kernel, in_specs=[SCALAR, WHOLE, WHOLE, pl.BlockSpec(...  6.97 us
    unnamed x12, local copies, waits for them, and re-layouts  5.5 us
    ppermute x1, waiting for transfers between devices, body(): after = lax.ppermute(virt_blocks[:1], 'mem', backward)  3.18 us
    ppermute x1, starting transfers between devices, body(): before = lax.ppermute(virt_blocks[rows - 2:], 'mem', forward)  3.15 us
  transfers between devices with their start and end apart: 6, of which 2 were waited for; matrix products, arithmetic and copies ran while one was open for 3% of the time, Pallas kernels for 14%

profile of v1, /device:TPU:1, one launch (start us, length us, event | category | flops | bytes accessed | tf_op | source)
XLA Modules:
  0.0 72.4 jit_solution(7631888092666683951)
XLA Ops:
  0.0 1.1 %fusion.1 = (bf16[1,4096]{1,0:T(2,128)(2,1)S(1)}, bf16[1,4096]{1,0:T(2,128)(2,1)S(1)}) fusion(bf16[48,4096]{1,0:T(8,128)(2,1)} %param.6), kind=kLoop, calls=%fused_computation.4 | loop fusion | bytes 32768 | tf_op jit(solution)/shard_map/slice | solution.py:198
  1.1 2.2 %reshape.12 = bf16[2,32,2,32,2]{4,3,2,1,0:T(8,128)(2,1)S(1)} reshape(bf16[2,4096]{1,0:T(2,128)(2,1)S(1)} %pad_maximum_fusion.1) | data formatting | bytes 32768 | tf_op jit(solution)/shard_map/reshape | solution.py:199
  3.4 0.8 %copy.6 = bf16[2,2,32,2,32]{4,3,2,1,0:T(2,128)(2,1)S(1)} copy(bf16[2,2,32,2,32]{3,4,1,2,0:T(8,128)(2,1)S(1)} %bitcast.3) | data formatting | bytes 32768 | tf_op jit(solution)/shard_map/transpose | solution.py:199
  4.3 0.7 copy-done.4
  5.0 9.2 %shard_map.46 = (bf16[4,64,4096]{2,1,0:T(8,128)(2,1)S(1)}, bf16[4,64,2048]{2,1,0:T(8,128)(2,1)}, bf16[4,64,2048]{2,1,0:T(8,128)(2,1)}) custom-call(s32[4,4,4]{2,1,0:T(4,128)S(1)} %copy-done.4, bf16[2,64,64]{2,1,0:T(8,128)(2,1)S(1)} %reshape.13.occ, bf16[1,4,64,4096]{3,2,1,0:T(8,128)(2,1)} %tiles.3), custom_call_target="tpu_custom_call" | custom-call | tf_op jit(solution)/shard_map/pallas_call | solution.py:201
  14.2 1.3 %copy-done.2 = bf16[4,64,4096]{2,1,0:T(8,128)(2,1)} copy-done((bf16[4,64,4096]{2,1,0:T(8,128)(2,1)}, bf16[4,64,4096]{2,1,0:T(8,128)(2,1)S(1)}, u32[]{:S(2)}) %copy-start.2) | copy-done | bytes 2097176
  15.6 4.4 %collective-permute-start.3 = (bf16[4,64,2048]{2,1,0:T(8,128)(2,1)}, bf16[4,64,2048]{2,1,0:T(8,128)(2,1)}, u32[]{:S(2)}, u32[]{:S(2)}) collective-permute-start(bf16[4,64,2048]{2,1,0:T(8,128)(2,1)} %get-tuple-element.19), channel_id=1, source_target_pairs={{8,16},{16,8},{9,17},{17,9},{10,18},{18,10},{11,19},{19,11},{12,20... | collective-permute-start | bytes 3145736 | tf_op jit(solution)/shard_map/ppermute | solution.py:180
  20.1 0.8 %fusion = (bf16[2,2,4096]{2,1,0:T(2,128)(2,1)S(1)}, bf16[2,2,4096]{2,1,0:T(2,128)(2,1)S(1)}) fusion(bf16[48,2,4096]{2,1,0:T(2,128)(2,1)} %param.7), kind=kLoop, calls=%fused_computation.3 | loop fusion | bytes 131072 | tf_op jit(solution)/shard_map/slice | solution.py:224
  20.9 3.1 %collective-permute-start = (bf16[2,2,4096]{2,1,0:T(2,128)(2,1)S(1)}, bf16[2,2,4096]{2,1,0:T(2,128)(2,1)S(1)}, u32[]{:S(2)}, u32[]{:S(2)}) collective-permute-start(bf16[2,2,4096]{2,1,0:T(2,128)(2,1)S(1)} %get-tuple-element.25), channel_id=1, source_target_pairs={{0,1},{1,2},{2,3},{3,4},{4,5},{5,6},{6,7},{8,9},{9,10},{10,11},{11... | collective-permute-start | bytes 98312 | tf_op jit(solution)/shard_map/ppermute | solution.py:224
  24.1 0.7 %slice.23 = bf16[1,2,4096]{2,1,0:T(2,128)(2,1)S(1)} slice(bf16[48,2,4096]{2,1,0:T(2,128)(2,1)} %param.7), slice={[0:1], [0:2], [0:4096]} | slice | bytes 32768 | tf_op jit(solution)/shard_map/slice | solution.py:225
  24.8 1.3 %collective-permute-start.1 = (bf16[1,2,4096]{2,1,0:T(2,128)(2,1)S(1)}, bf16[1,2,4096]{2,1,0:T(2,128)(2,1)S(1)}, u32[]{:S(2)}, u32[]{:S(2)}) collective-permute-start(bf16[1,2,4096]{2,1,0:T(2,128)(2,1)S(1)} %slice.23), channel_id=1, source_target_pairs={{1,0},{2,1},{3,2},{4,3},{5,4},{6,5},{7,6},{9,8},{10,9},{11,10},{12... | collective-permute-start | bytes 49160 | tf_op jit(solution)/shard_map/ppermute | solution.py:225
  26.1 3.2 %collective-permute-done.1 = bf16[1,2,4096]{2,1,0:T(2,128)(2,1)S(1)} collective-permute-done((bf16[1,2,4096]{2,1,0:T(2,128)(2,1)S(1)}, bf16[1,2,4096]{2,1,0:T(2,128)(2,1)S(1)}, u32[]{:S(2)}, u32[]{:S(2)}) %collective-permute-start.1) | collective-permute-done | bytes 16416 | tf_op jit(solution)/shard_map/ppermute | solution.py:225
  29.3 0.2 pad_maximum_fusion
  29.5 0.2 reshape.14.table
  29.7 1.6 %copy-done.3 = bf16[4,64,4096]{2,1,0:T(8,128)(2,1)S(1)} copy-done((bf16[4,64,4096]{2,1,0:T(8,128)(2,1)S(1)}, bf16[4,64,4096]{2,1,0:T(8,128)(2,1)}, u32[]{:S(2)}) %copy-start.3) | copy-done | bytes 2097176
  31.3 10.2 %shard_map.47 = (bf16[768,2048]{1,0:T(8,128)(2,1)}, bf16[768,2048]{1,0:T(8,128)(2,1)}, f32[256,256]{1,0:T(8,128)S(1)}) custom-call(s32[4,4,4]{2,1,0:T(4,128)S(1)} %copy-done.5, bf16[4,64,4096]{2,1,0:T(8,128)(2,1)S(1)} %copy-done.3, bf16[1,4,64,4096]{3,2,1,0:T(8,128)(2,1)S(1)} %copy-done, bf16[8,2,64,64]{3,2,1,0:T(8,128)(2,1)S(1)} %reshape.14.table), custom_call_target="tpu_custom_call" | custom-call | tf_op jit(solution)/shard_map/pallas_call | solution.py:230
  41.5 1.9 %copy-done.1 = bf16[768,2048]{1,0:T(8,128)(2,1)S(1)} copy-done((bf16[768,2048]{1,0:T(8,128)(2,1)S(1)}, bf16[768,2048]{1,0:T(8,128)(2,1)}, u32[]{:S(2)}) %copy-start.1) | copy-done | bytes 3145752
  43.4 7.0 %shard_map.48 = (f32[256,256]{1,0:T(8,128)S(1)}, f32[256,256]{1,0:T(8,128)S(1)}, bf16[256,256]{1,0:T(8,128)(2,1)S(1)}, bf16[256,256]{1,0:T(8,128)(2,1)S(1)}) custom-call(s32[4,4,4]{2,1,0:T(4,128)S(1)} %copy-done.5, bf16[768,2048]{1,0:T(8,128)(2,1)S(1)} %copy-done.1, bf16[768,2048]{1,0:T(8,128)(2,1)} %get-tuple-element.17.v_high, ...), custom_call_target="tpu_custom_call" | custom-call | tf_op jit(solution)/shard_map/pallas_call | solution.py:245
  50.4 1.2 %collective-permute-start.4 = (bf16[256,256]{1,0:T(8,128)(2,1)S(1)}, bf16[256,256]{1,0:T(8,128)(2,1)S(1)}, u32[]{:S(2)}, u32[]{:S(2)}) collective-permute-start(bf16[256,256]{1,0:T(8,128)(2,1)S(1)} %get-tuple-element.23), channel_id=1, source_target_pairs={{0,8},{16,24},{8,0},{24,16},{1,9},{17,25},{9,1},{25,17},{2,10},{18... | collective-permute-start | bytes 393224 | tf_op jit(solution)/shard_map/ppermute | solution.py:180
  51.5 3.8 %collective-permute-start.5 = (bf16[256,256]{1,0:T(8,128)(2,1)S(1)}, bf16[256,256]{1,0:T(8,128)(2,1)S(1)}, u32[]{:S(2)}, u32[]{:S(2)}) collective-permute-start(bf16[256,256]{1,0:T(8,128)(2,1)S(1)} %get-tuple-element.24), channel_id=1, source_target_pairs={{8,16},{16,8},{9,17},{17,9},{10,18},{18,10},{11,19},{19,11},{12,20... | collective-permute-start | bytes 393224 | tf_op jit(solution)/shard_map/ppermute | solution.py:180
  55.4 2.6 %collective-permute-done.5.odd = bf16[256,256]{1,0:T(8,128)(2,1)S(1)} collective-permute-done((bf16[256,256]{1,0:T(8,128)(2,1)S(1)}, bf16[256,256]{1,0:T(8,128)(2,1)S(1)}, u32[]{:S(2)}, u32[]{:S(2)}) %collective-permute-start.5) | collective-permute-done | bytes 131104 | tf_op jit(solution)/shard_map/ppermute | solution.py:180
  58.0 0.1 shard_map.49
  58.2 13.5 %all_to_all.5 = bf16[8,32,768]{2,1,0:T(8,128)(2,1)S(1)} all-to-all(bf16[8,32,768]{2,1,0:T(8,128)(2,1)S(1)} %bitcast.2), channel_id=1, replica_groups=mesh['grp'=4,'mem'=8] {'mem'}, dimensions={0} | all-to-all | bytes 786432 | tf_op jit(solution)/shard_map/all_to_all | solution.py:268
  71.7 0.7 convert_reduce_fusion
  (17 shorter events, 0.2 us)
Async XLA Ops:
  0.0 29.7 %copy-start.5 = (s32[4,4,4]{2,1,0:T(4,128)S(1)}, s32[4,4,4]{2,1,0:T(4,128)}, u32[]{:S(2)}) copy-start(s32[4,4,4]{2,1,0:T(4,128)} %ids.5) | copy-start | bytes 772
  0.0 29.7 %copy-start = (bf16[1,4,64,4096]{3,2,1,0:T(8,128)(2,1)S(1)}, bf16[1,4,64,4096]{3,2,1,0:T(8,128)(2,1)}, u32[]{:S(2)}) copy-start(bf16[1,4,64,4096]{3,2,1,0:T(8,128)(2,1)} %tiles.3) | copy-start | bytes 6291460
  0.0 29.3 %slice-start = ((bf16[48,2,4096]{2,1,0:T(2,128)(2,1)}), bf16[3,2,4096]{2,1,0:T(2,128)(2,1)S(1)}, s32[]{:S(2)}) async-start(bf16[48,2,4096]{2,1,0:T(2,128)(2,1)} %param.7), calls=%async_computation.1 | async-start | bytes 98304 | tf_op jit(solution)/shard_map/slice | solution.py:226
  4.3 0.7 copy-start.4
  14.2 1.3 %copy-start.2 = (bf16[4,64,4096]{2,1,0:T(8,128)(2,1)}, bf16[4,64,4096]{2,1,0:T(8,128)(2,1)S(1)}, u32[]{:S(2)}) copy-start(bf16[4,64,4096]{2,1,0:T(8,128)(2,1)S(1)} %get-tuple-element.15.half) | copy-start | bytes 6291460
  15.6 25.9 %collective-permute-start.2 = (bf16[4,64,2048]{2,1,0:T(8,128)(2,1)}, bf16[4,64,2048]{2,1,0:T(8,128)(2,1)S(1)}, u32[]{:S(2)}, u32[]{:S(2)}) collective-permute-start(bf16[4,64,2048]{2,1,0:T(8,128)(2,1)} %get-tuple-element.18), channel_id=1, source_target_pairs={{0,8},{16,24},{8,0},{24,16},{1,9},{17,25},{9,1},{25,17},{2,10},{18... | collective-permute-start | bytes 3145736 | tf_op jit(solution)/shard_map/ppermute | solution.py:180
  15.6 25.9 %collective-permute-start.3 = (bf16[4,64,2048]{2,1,0:T(8,128)(2,1)}, bf16[4,64,2048]{2,1,0:T(8,128)(2,1)}, u32[]{:S(2)}, u32[]{:S(2)}) collective-permute-start(bf16[4,64,2048]{2,1,0:T(8,128)(2,1)} %get-tuple-element.19), channel_id=1, source_target_pairs={{8,16},{16,8},{9,17},{17,9},{10,18},{18,10},{11,19},{19,11},{12,20... | collective-permute-start | bytes 3145736 | tf_op jit(solution)/shard_map/ppermute | solution.py:180
  20.9 8.4 %collective-permute-start = (bf16[2,2,4096]{2,1,0:T(2,128)(2,1)S(1)}, bf16[2,2,4096]{2,1,0:T(2,128)(2,1)S(1)}, u32[]{:S(2)}, u32[]{:S(2)}) collective-permute-start(bf16[2,2,4096]{2,1,0:T(2,128)(2,1)S(1)} %get-tuple-element.25), channel_id=1, source_target_pairs={{0,1},{1,2},{2,3},{3,4},{4,5},{5,6},{6,7},{8,9},{9,10},{10,11},{11... | collective-permute-start | bytes 98312 | tf_op jit(solution)/shard_map/ppermute | solution.py:224
  24.8 4.5 %collective-permute-start.1 = (bf16[1,2,4096]{2,1,0:T(2,128)(2,1)S(1)}, bf16[1,2,4096]{2,1,0:T(2,128)(2,1)S(1)}, u32[]{:S(2)}, u32[]{:S(2)}) collective-permute-start(bf16[1,2,4096]{2,1,0:T(2,128)(2,1)S(1)} %slice.23), channel_id=1, source_target_pairs={{1,0},{2,1},{3,2},{4,3},{5,4},{6,5},{7,6},{9,8},{10,9},{11,10},{12... | collective-permute-start | bytes 49160 | tf_op jit(solution)/shard_map/ppermute | solution.py:225
  29.7 1.6 %copy-start.3 = (bf16[4,64,4096]{2,1,0:T(8,128)(2,1)S(1)}, bf16[4,64,4096]{2,1,0:T(8,128)(2,1)}, u32[]{:S(2)}) copy-start(bf16[4,64,4096]{2,1,0:T(8,128)(2,1)} %copy-done.2) | copy-start | bytes 6291460
  41.5 1.9 %copy-start.1 = (bf16[768,2048]{1,0:T(8,128)(2,1)S(1)}, bf16[768,2048]{1,0:T(8,128)(2,1)}, u32[]{:S(2)}) copy-start(bf16[768,2048]{1,0:T(8,128)(2,1)} %get-tuple-element.16.y_low) | copy-start | bytes 9437188
  50.4 5.0 %collective-permute-start.4 = (bf16[256,256]{1,0:T(8,128)(2,1)S(1)}, bf16[256,256]{1,0:T(8,128)(2,1)S(1)}, u32[]{:S(2)}, u32[]{:S(2)}) collective-permute-start(bf16[256,256]{1,0:T(8,128)(2,1)S(1)} %get-tuple-element.23), channel_id=1, source_target_pairs={{0,8},{16,24},{8,0},{24,16},{1,9},{17,25},{9,1},{25,17},{2,10},{18... | collective-permute-start | bytes 393224 | tf_op jit(solution)/shard_map/ppermute | solution.py:180
  51.5 6.5 %collective-permute-start.5 = (bf16[256,256]{1,0:T(8,128)(2,1)S(1)}, bf16[256,256]{1,0:T(8,128)(2,1)S(1)}, u32[]{:S(2)}, u32[]{:S(2)}) collective-permute-start(bf16[256,256]{1,0:T(8,128)(2,1)S(1)} %get-tuple-element.24), channel_id=1, source_target_pairs={{8,16},{16,8},{9,17},{17,9},{10,18},{18,10},{11,19},{19,11},{12,20... | collective-permute-start | bytes 393224 | tf_op jit(solution)/shard_map/ppermute | solution.py:180

commit v2 on v1

v2 whole, which is shorter than its diff:
```python
import functools

import jax
import jax.numpy as jnp
from jax import lax
from jax.experimental import pallas as pl
from jax.experimental.pallas import tpu as pltpu
from jax.sharding import PartitionSpec as P

RIB = 4
WIDE = 256
F32 = jnp.float32
BF16 = jnp.bfloat16


def is_odd():
    return lax.rem(lax.axis_index("grp"), 2) == 1


def half_kernel(
    occ_in, ids_in, tiles, virt, half, even, odd, send_up, send_down, held, made, to_even, to_odd,
    occ, ids, green, rows_in, rows_out, sem, out_sem
):
    slots, side, flat = held.shape
    lanes, cut = 2 * side, even.shape[2]
    high = flat // lanes
    pitch = rows_in.shape[0] // high
    rows = occ.shape[0]
    first_in = pltpu.make_async_copy(occ_in, occ, sem.at[slots + 2])
    ids_copy = pltpu.make_async_copy(ids_in, ids, sem.at[slots + 3])
    first_in.start()
    ids_copy.start()
    fetch = [pltpu.make_async_copy(tiles.at[0, t], held.at[t], sem.at[t]) for t in range(slots)]
    for copy in fetch:
        copy.start()
    up = pltpu.make_async_copy(virt.at[pl.ds(rows - 2, 2)], send_up, sem.at[slots])
    down = pltpu.make_async_copy(virt.at[pl.ds(0, 1)], send_down, sem.at[slots + 1])
    up.start()
    down.start()
    group = lax.axis_index("grp")
    first = lax.axis_index("mem") * rows
    odd_one = is_odd()
    source = lax.broadcasted_iota(jnp.int32, (lanes, side), 0)
    target = lax.broadcasted_iota(jnp.int32, (lanes, side), 1)
    mu = lax.rem(source, side)
    first_in.wait()
    for end, row in enumerate((0, rows - 1)):
        line = occ[row : row + 1, :].astype(F32)
        block = jnp.concatenate([line[:, h * lanes : (h + 1) * lanes] for h in range(high)], axis=0)
        for parity in range(2):
            other = (lax.rem(mu, 2) != parity).astype(jnp.int32)
            pick = (source // side == parity) & (target == mu // 2 + other * high)
            green[end, parity * high : (parity + 1) * high, :] = jnp.dot(
                block.astype(BF16), pick.astype(BF16), preferred_element_type=F32
            ).astype(BF16)
    low = lax.broadcasted_iota(jnp.int32, (high, lanes), 1) < side
    ids_copy.wait()
    results = []
    for t in range(slots):
        fetch[t].wait()
        block = green[(ids[group, 1, t] != first).astype(jnp.int32)]
        for h in range(high):
            rows_in[h * pitch : h * pitch + side, :] = held[t, :, h * lanes : (h + 1) * lanes].astype(F32)
        for p in range(0, side, 2):
            one = rows_in[pl.ds(p, high, stride=pitch), :]
            two = rows_in[pl.ds(p + 1, high, stride=pitch), :]
            crossed = [pltpu.roll(one, side, 1), pltpu.roll(two, side, 1)]
            x = jnp.concatenate(
                [jnp.concatenate([one, two], axis=1), jnp.concatenate(crossed, axis=1)], axis=0
            )
            y = jnp.dot(block, x.astype(BF16), preferred_element_type=F32)
            rows_out[pl.ds(p, high, stride=pitch), :] = jnp.where(low, y[:high, :lanes], y[high:, :lanes])
            rows_out[pl.ds(p + 1, high, stride=pitch), :] = jnp.where(low, y[:high, lanes:], y[high:, lanes:])
        for h in range(high):
            at = slice(h * lanes, (h + 1) * lanes)
            done = rows_out[h * pitch : h * pitch + side, :].astype(BF16)
            made[t, :, at] = done
            if h * lanes >= cut:
                raw = held[t, :, h * lanes - cut : (h + 1) * lanes - cut]
                to = slice(h * lanes - cut, (h + 1) * lanes - cut)
                to_even[t, :, to] = jnp.where(odd_one, done, raw)
                to_odd[t, :, to] = jnp.where(odd_one, raw, done)
        for k, (source, target) in enumerate(((to_even, even), (to_odd, odd), (made, half))):
            copy = pltpu.make_async_copy(source.at[t], target.at[t], out_sem.at[t, k])
            copy.start()
            results.append(copy)
    for copy in results + [up, down]:
        copy.wait()


def combined(products, slots, side, ids, left, right, left_on, right_on, total):
    width = slots * side

    def spread(values, owner):
        out = jnp.full(owner.shape, values[0], jnp.int32)
        for u in range(1, slots):
            out = jnp.where(owner == u, values[u], out)
        return out

    owner = lax.broadcasted_iota(jnp.int32, (1, width), 1) // side
    live = [ids[right, 3, u] * right_on for u in range(slots)]
    row_block = spread([jnp.where(live[u] > 0, ids[right, 1, u], -1) for u in range(slots)], owner)
    col_block = spread([ids[right, 2, u] for u in range(slots)], owner)
    total[...] = jnp.zeros_like(total)
    for t in range(slots):
        same = row_block == jnp.where(ids[left, 3, t] * left_on > 0, ids[left, 1, t], -2)
        term = jnp.zeros((side, width), F32)
        for j in range(3):
            at = (t * 3 + j) * side
            match = (same & (col_block == ids[left, 2, t] + (j - 1))).astype(F32)
            term = term + products[at : at + side, :] * match
        total[ids[left, 0, t]] += term
    row = lax.broadcasted_iota(jnp.int32, (width, 1), 0)
    target = spread([ids[right, 0, u] for u in range(slots)], row // side) * side + lax.rem(row, side)
    place = (target == lax.broadcasted_iota(jnp.int32, (width, RIB * side), 1)).astype(F32).astype(BF16)
    summed = total[...].reshape(RIB * side, width)
    coarse = summed.astype(BF16)
    fine = (summed - coarse.astype(F32)).astype(BF16)
    return jnp.dot(coarse, place, preferred_element_type=F32) + jnp.dot(
        fine, place, preferred_element_type=F32
    )


NT = (((1,), (1,)), ((), ()))
NN = (((1,), (0,)), ((), ()))


def prepare_kernel(rows, ids, half, tiles, table, y_all, v_high, middle, total, products):
    slots, side, flat = half.shape
    cut = flat - v_high.shape[1]
    group = lax.axis_index("grp")
    first = lax.axis_index("mem") * rows
    count = rows * lax.axis_size("mem")
    copies = WIDE // side
    own = lax.broadcasted_iota(jnp.int32, (WIDE, WIDE), 0) // side
    own = own == lax.broadcasted_iota(jnp.int32, (WIDE, WIDE), 1) // side

    def spread(block):
        row = jnp.concatenate([block] * copies, axis=1)
        return jnp.where(own, jnp.concatenate([row] * copies, axis=0), jnp.zeros((), BF16))

    for t in range(slots):
        a, b = ids[group, 1, t], ids[group, 2, t]
        at = jnp.where(a == first, 2, 6) + b - a
        keep = (b + 1 < count).astype(F32)
        before = spread(table[at - 1, 1])
        here = spread(table[at, 0])
        after = spread((table[at, 1].astype(F32) * keep).astype(BF16))
        x = jnp.concatenate([half[t, :, c : c + WIDE] for c in range(0, flat, WIDE)], axis=0)
        for j, (mat, dims) in enumerate(((before, NT), (here, NN), (after, NN))):
            y = lax.dot_general(x, mat, dims, preferred_element_type=F32).astype(BF16)
            for c in range(0, flat, WIDE):
                block = y[c // WIDE * side : (c // WIDE + 1) * side]
                y_all[(t * 3 + j) * side : (t * 3 + j + 1) * side, c : c + WIDE] = block
        x = jnp.concatenate([tiles[0, t, :, c : c + WIDE] for c in range(cut, flat, WIDE)], axis=0)
        for j, (mat, dims) in enumerate(((before, NT), (here, NT), (after, NN))):
            y = lax.dot_general(x, mat, dims, preferred_element_type=F32).astype(BF16)
            for c in range(0, flat - cut, WIDE):
                block = y[c // WIDE * side : (c // WIDE + 1) * side]
                v_high[(t * 3 + j) * side : (t * 3 + j + 1) * side, c : c + WIDE] = block
    products[...] = lax.dot_general(
        y_all[...], tiles[0].reshape(slots * side, flat), NT, preferred_element_type=F32
    )
    middle[...] = combined(products, slots, side, ids, group, group, 1, 1, total)


def pair_kernel(ids, y_all, v_high, even, odd, lower, upper, out_even, out_odd, total, products):
    slots, side, _ = even.shape
    group = lax.axis_index("grp")
    last = lax.axis_size("grp") - 1
    has_below = (group > 0).astype(jnp.int32)
    has_above = (group < last).astype(jnp.int32)
    under, over = jnp.maximum(group - 1, 0), jnp.minimum(group + 1, last)

    odd_one = is_odd()
    cut = even.shape[2]
    from_even = even[...].reshape(slots * side, cut)
    from_odd = odd[...].reshape(slots * side, cut)
    products[...] = lax.dot_general(
        y_all[:, :cut], jnp.where(odd_one, from_even, from_odd), NT, preferred_element_type=F32
    )
    lower[...] = combined(products, slots, side, ids, group, under, 1, has_below, total)
    products[...] = lax.dot_general(
        v_high[...], jnp.where(odd_one, from_odd, from_even), NT, preferred_element_type=F32
    )
    upper[...] = combined(products, slots, side, ids, group, over, 1, has_above, total)
    to_below = lower[...].T.astype(BF16)
    to_above = upper[...].T.astype(BF16)
    out_even[...] = jnp.where(odd_one, to_below, to_above)
    out_odd[...] = jnp.where(odd_one, to_above, to_below)


def band_kernel(lower, middle, upper, even, odd, band):
    side = lower.shape[1]
    odd_one = is_odd()
    from_even, from_odd = even[...].astype(F32), odd[...].astype(F32)
    band[:, :side] = (lower[...] + jnp.where(odd_one, from_even, from_odd)).astype(BF16)
    band[:, side : 2 * side] = middle[...].astype(BF16)
    band[:, 2 * side :] = (upper[...] + jnp.where(odd_one, from_odd, from_even)).astype(BF16)


def swapped(block, parity):
    count = lax.axis_size("grp")
    pairs = [(i, i + 1) for i in range(parity, count - 1, 2)]
    return lax.ppermute(block, "grp", pairs + [(b, a) for a, b in pairs])


def params(mib):
    return pltpu.CompilerParams(vmem_limit_bytes=mib * 1024 * 1024)


def in_hbm(x):
    return pltpu.with_memory_space_constraint(x, pltpu.HBM)


def in_vmem(x):
    return pltpu.with_memory_space_constraint(x, pltpu.VMEM)


WHOLE = pl.BlockSpec(memory_space=pltpu.VMEM)
SCALAR = pl.BlockSpec(memory_space=pltpu.SMEM)


def body(tiles, tile_ids, occ_blocks, virt_blocks):
    slots, side, flat = tiles.shape[1:]
    rows = occ_blocks.shape[0]
    members = lax.axis_size("mem")
    cut = flat // 2
    width = RIB * side

    anywhere = pl.BlockSpec(memory_space=pltpu.HBM)
    pitch = side + 8
    half, even, odd, send_up, send_down = pl.pallas_call(
        half_kernel,
        in_specs=[anywhere] * 4,
        out_specs=[anywhere] * 5,
        out_shape=[
            pltpu.HBM((slots, side, flat), BF16),
            pltpu.HBM((slots, side, cut), BF16),
            pltpu.HBM((slots, side, cut), BF16),
            jax.ShapeDtypeStruct((2, 2, flat), BF16),
            jax.ShapeDtypeStruct((1, 2, flat), BF16),
        ],
        scratch_shapes=[
            pltpu.VMEM((slots, side, flat), BF16),
            pltpu.VMEM((slots, side, flat), BF16),
            pltpu.VMEM((slots, side, cut), BF16),
            pltpu.VMEM((slots, side, cut), BF16),
            pltpu.VMEM(occ_blocks.shape, BF16),
            pltpu.SMEM(tile_ids.shape, jnp.int32),
            pltpu.VMEM((2, side, side), BF16),
            pltpu.VMEM((flat // (2 * side) * pitch, 2 * side), F32),
            pltpu.VMEM((flat // (2 * side) * pitch, 2 * side), F32),
            pltpu.SemaphoreType.DMA((slots + 4,)),
            pltpu.SemaphoreType.DMA((slots, 3)),
        ],
        compiler_params=params(16),
    )(*(in_hbm(x) for x in (occ_blocks, tile_ids, tiles, virt_blocks)))
    got_odd = swapped(odd, 1)
    got_even = swapped(even, 0)

    forward = [(i, i + 1) for i in range(members - 1)]
    backward = [(b, a) for a, b in forward]
    before = lax.ppermute(send_up, "mem", forward)
    after = lax.ppermute(send_down, "mem", backward)
    table = jnp.concatenate([before, virt_blocks[:2], virt_blocks[rows - 3 :], after], axis=0)
    table = table.reshape(8, 2, side, side)

    y_all, v_high, middle = pl.pallas_call(
        functools.partial(prepare_kernel, rows),
        in_specs=[SCALAR, WHOLE, WHOLE, WHOLE],
        out_specs=[WHOLE, WHOLE, WHOLE],
        out_shape=[
            pltpu.VMEM((slots * 3 * side, flat), BF16),
            pltpu.VMEM((slots * 3 * side, flat - cut), BF16),
            pltpu.VMEM((width, width), F32),
        ],
        scratch_shapes=[pltpu.VMEM((RIB, side, slots * side), F32),
            pltpu.VMEM((slots * 3 * side, slots * side), F32),
        ],
        compiler_params=params(24),
    )(tile_ids, half, tiles, table)
    lower, upper, out_even, out_odd = pl.pallas_call(
        pair_kernel,
        in_specs=[SCALAR] + [WHOLE] * 4,
        out_specs=[WHOLE] * 4,
        out_shape=[jax.ShapeDtypeStruct((width, width), F32)] * 2
        + [jax.ShapeDtypeStruct((width, width), BF16)] * 2,
        scratch_shapes=[pltpu.VMEM((RIB, side, slots * side), F32),
            pltpu.VMEM((slots * 3 * side, slots * side), F32),
        ],
        compiler_params=params(24),
    )(tile_ids, in_vmem(y_all), in_vmem(v_high), in_vmem(got_even), in_vmem(got_odd))
    back_odd = swapped(out_odd, 1)
    back_even = swapped(out_even, 0)
    band = pl.pallas_call(
        band_kernel,
        in_specs=[WHOLE] * 5,
        out_specs=WHOLE,
        out_shape=jax.ShapeDtypeStruct((width, 3 * width), BF16),
        compiler_params=params(8),
    )(lower, middle, upper, back_even, back_odd)
    parts = lax.all_to_all(band.reshape(members, width // members, 3 * width), "mem", 0, 0)
    return parts.astype(F32).sum(axis=0)


def solution(mesh):
    placed = (
        P("grp", "mem", None, None),
        P(None, None, "mem"),
        P("mem", None),
        P("mem", None, None),
    )
    return jax.shard_map(
        body, mesh=mesh, in_specs=placed, out_specs=P(("grp", "mem"), None), check_vma=False
    )
```

time: 73.5 us -> 54.8 us (0.75)
  local copies, waits for them, and re-layouts: 11.5 us -> 1.81 us
  Pallas kernels: 26.5 us -> 18.7 us
  starting transfers between devices: 14 us -> 13.1 us
    pallas_call x2, Pallas kernels: 16.2 us -> 10.5 us  [the longest x1 5.28 us: body(): pl.pallas_call(half_kernel, in_specs=[anywhere] * 4, out_specs=[anywhere]...]
    unnamed x12 -> x6, local copies, waits for them, and re-layouts: 5.5 us -> 1.59 us
    slice x3 -> x2, local copies, waits for them, and re-layouts: 2.61 us -> 0.01 us  [body(): virt_blocks[:2]]
    reshape x2 -> x0, local copies, waits for them, and re-layouts: 2.35 us -> none  [body(): ends.reshape(2, side // 2, 2, side // 2, 2).transpose(0, 2, 1, 4, 3)]
    pallas_call x1, Pallas kernels: 10.2 us -> 8 us  [body(): pl.pallas_call(functools.partial(prepare_kernel, rows), in_specs=[SCALAR,...]
    ppermute x4, starting transfers between devices: 9.54 us -> 8.61 us  [swapped(): return lax.ppermute(block, 'grp', pairs + [(b, a) for a, b in pairs])]
    transpose x1 -> x0, local copies, waits for them, and re-layouts: 0.83 us -> none  [body(): ends.reshape(2, side // 2, 2, side // 2, 2).transpose(0, 2, 1, 4, 3)]
  transfers between devices with their start and end apart: 6 -> 6, of which waited for: 2 -> 2; matrix products, arithmetic and copies ran while one was open for 3% -> 1% of each run, Pallas kernels for 14% -> 15%
where the time goes in v2:
time: 54.8 us; the launch traced here: 53.9 us
  Pallas kernels  18.7 us (34%)
  blocking collectives  13.6 us (25%)
  starting transfers between devices  13.1 us (24%)
  waiting for transfers between devices  5.82 us (11%)
  local copies, waits for them, and re-layouts  1.81 us (3%)
  other arithmetic  0.9 us (2%)
    all_to_all x1, blocking collectives, body(): lax.all_to_all(band.reshape(members, width // members, 3 * width), 'mem',...  13.6 us
    ppermute x4, starting transfers between devices, swapped(): return lax.ppermute(block, 'grp', pairs + [(b, a) for a, b in pairs])  8.61 us
    pallas_call x1, Pallas kernels, body(): pl.pallas_call(functools.partial(prepare_kernel, rows), in_specs=[SCALAR,...  8 us
    pallas_call x1, Pallas kernels, body(): pl.pallas_call(half_kernel, in_specs=[anywhere] * 4, out_specs=[anywhere]...  5.28 us
    pallas_call x1, Pallas kernels, body(): pl.pallas_call(pair_kernel, in_specs=[SCALAR] + [WHOLE] * 4, out_specs=[W...  5.26 us
    ppermute x1, waiting for transfers between devices, body(): after = lax.ppermute(send_down, 'mem', backward)  3.18 us
    ppermute x1, starting transfers between devices, body(): before = lax.ppermute(send_up, 'mem', forward)  3.16 us
    ppermute x4, waiting for transfers between devices, swapped(): return lax.ppermute(block, 'grp', pairs + [(b, a) for a, b in pairs])  2.63 us
  transfers between devices with their start and end apart: 6, of which 2 were waited for; matrix products, arithmetic and copies ran while one was open for 1% of the time, Pallas kernels for 15%

profile of v2, /device:TPU:1, one launch (start us, length us, event | category | flops | bytes accessed | tf_op | source)
XLA Modules:
  0.0 53.9 jit_solution(11713503376819830046)
XLA Ops:
  0.0 0.0 copy-start
  0.0 5.3 %shard_map.46 = (bf16[4,64,4096]{2,1,0:T(8,128)(2,1)}, bf16[4,64,2048]{2,1,0:T(8,128)(2,1)}, bf16[4,64,2048]{2,1,0:T(8,128)(2,1)}, bf16[2,2,4096]{2,1,0:T(2,128)(2,1)S(1)}, bf16[1,2,4096]{2,1,0:T(2,128)(2,1)S(1)}) custom-call(bf16[48,4096]{1,0:T(8,128)(2,1)} %occ_in.1, s32[4,4,4]{2,1,0:T(4,128)} %ids.3, bf16[1,4,64,4096]{3,2,1,0:T(8,128)(2,1)} %tiles.3, ...), custom_call_target="tpu_custom_call" | custom-call | tf_op jit(solution)/shard_map/pallas_call | solution.py:233
  5.3 0.1 collective-permute-start.2
  5.4 4.4 %collective-permute-start.3 = (bf16[4,64,2048]{2,1,0:T(8,128)(2,1)}, bf16[4,64,2048]{2,1,0:T(8,128)(2,1)}, u32[]{:S(2)}, u32[]{:S(2)}) collective-permute-start(bf16[4,64,2048]{2,1,0:T(8,128)(2,1)} %get-tuple-element.23), channel_id=1, source_target_pairs={{8,16},{16,8},{9,17},{17,9},{10,18},{18,10},{11,19},{19,11},{12,20... | collective-permute-start | bytes 3145736 | tf_op jit(solution)/shard_map/ppermute | solution.py:205
  9.9 3.2 %collective-permute-start = (bf16[2,2,4096]{2,1,0:T(2,128)(2,1)S(1)}, bf16[2,2,4096]{2,1,0:T(2,128)(2,1)S(1)}, u32[]{:S(2)}, u32[]{:S(2)}) collective-permute-start(bf16[2,2,4096]{2,1,0:T(2,128)(2,1)S(1)} %get-tuple-element.18), channel_id=1, source_target_pairs={{0,1},{1,2},{2,3},{3,4},{4,5},{5,6},{6,7},{8,9},{9,10},{10,11},{11... | collective-permute-start | bytes 98312 | tf_op jit(solution)/shard_map/ppermute | solution.py:264
  13.1 1.3 %collective-permute-start.1 = (bf16[1,2,4096]{2,1,0:T(2,128)(2,1)S(1)}, bf16[1,2,4096]{2,1,0:T(2,128)(2,1)S(1)}, u32[]{:S(2)}, u32[]{:S(2)}) collective-permute-start(bf16[1,2,4096]{2,1,0:T(2,128)(2,1)S(1)} %get-tuple-element.19), channel_id=1, source_target_pairs={{1,0},{2,1},{3,2},{4,3},{5,4},{6,5},{7,6},{9,8},{10,9},{11,10},{12... | collective-permute-start | bytes 49160 | tf_op jit(solution)/shard_map/ppermute | solution.py:265
  14.4 3.2 %collective-permute-done.1 = bf16[1,2,4096]{2,1,0:T(2,128)(2,1)S(1)} collective-permute-done((bf16[1,2,4096]{2,1,0:T(2,128)(2,1)S(1)}, bf16[1,2,4096]{2,1,0:T(2,128)(2,1)S(1)}, u32[]{:S(2)}, u32[]{:S(2)}) %collective-permute-start.1) | collective-permute-done | bytes 16416 | tf_op jit(solution)/shard_map/ppermute | solution.py:265
  17.5 0.0 collective-permute-done
  17.5 0.0 slice-done
  17.5 0.0 slice-done.1
  17.6 0.2 pad_maximum_fusion
  17.8 0.2 reshape.6.table
  18.0 1.6 %copy-done.1 = bf16[4,64,4096]{2,1,0:T(8,128)(2,1)S(1)} copy-done((bf16[4,64,4096]{2,1,0:T(8,128)(2,1)S(1)}, bf16[4,64,4096]{2,1,0:T(8,128)(2,1)}, u32[]{:S(2)}) %copy-start.1) | copy-done | bytes 2097176
  19.6 8.0 %shard_map.47 = (bf16[768,4096]{1,0:T(8,128)(2,1)S(1)}, bf16[768,2048]{1,0:T(8,128)(2,1)S(1)}, f32[256,256]{1,0:T(8,128)S(1)}) custom-call(s32[4,4,4]{2,1,0:T(4,128)S(1)} %copy-done.2, bf16[4,64,4096]{2,1,0:T(8,128)(2,1)S(1)} %copy-done.1, bf16[1,4,64,4096]{3,2,1,0:T(8,128)(2,1)S(1)} %copy-done, bf16[8,2,64,64]{3,2,1,0:T(8,128)(2,1)S(1)} %reshape.6.table), custom_call_target="tpu_custom_call" | custom-call | tf_op jit(solution)/shard_map/pallas_call | solution.py:269
  27.6 0.0 collective-permute-done.2.even
  27.6 0.0 collective-permute-done.3.odd
  27.6 5.3 %shard_map.48 = (f32[256,256]{1,0:T(8,128)S(1)}, f32[256,256]{1,0:T(8,128)S(1)}, bf16[256,256]{1,0:T(8,128)(2,1)S(1)}, bf16[256,256]{1,0:T(8,128)(2,1)S(1)}) custom-call(s32[4,4,4]{2,1,0:T(4,128)S(1)} %copy-done.2, bf16[768,4096]{1,0:T(8,128)(2,1)S(1)} %get-tuple-element.20.y_all, bf16[768,2048]{1,0:T(8,128)(2,1)S(1)} %get-tuple-element.21.v_high, ...), custom_call_target="tpu_custom_call" | custom-call | tf_op jit(solution)/shard_map/pallas_call | solution.py:283
  32.9 0.1 collective-permute-start.4
  33.0 3.9 %collective-permute-start.5 = (bf16[256,256]{1,0:T(8,128)(2,1)S(1)}, bf16[256,256]{1,0:T(8,128)(2,1)S(1)}, u32[]{:S(2)}, u32[]{:S(2)}) collective-permute-start(bf16[256,256]{1,0:T(8,128)(2,1)S(1)} %get-tuple-element.28), channel_id=1, source_target_pairs={{8,16},{16,8},{9,17},{17,9},{10,18},{18,10},{11,19},{19,11},{12,20... | collective-permute-start | bytes 393224 | tf_op jit(solution)/shard_map/ppermute | solution.py:205
  36.9 0.0 collective-permute-done.4.even
  36.9 2.6 %collective-permute-done.5.odd = bf16[256,256]{1,0:T(8,128)(2,1)S(1)} collective-permute-done((bf16[256,256]{1,0:T(8,128)(2,1)S(1)}, bf16[256,256]{1,0:T(8,128)(2,1)S(1)}, u32[]{:S(2)}, u32[]{:S(2)}) %collective-permute-start.5) | collective-permute-done | bytes 131104 | tf_op jit(solution)/shard_map/ppermute | solution.py:205
  39.6 0.1 shard_map.49
  39.7 13.6 %all_to_all.5 = bf16[8,32,768]{2,1,0:T(8,128)(2,1)S(1)} all-to-all(bf16[8,32,768]{2,1,0:T(8,128)(2,1)S(1)} %bitcast.1), channel_id=1, replica_groups=mesh['grp'=4,'mem'=8] {'mem'}, dimensions={0} | all-to-all | bytes 786432 | tf_op jit(solution)/shard_map/all_to_all | solution.py:303
  53.3 0.7 %convert_reduce_fusion = f32[32,768]{1,0:T(8,128)} fusion(bf16[8,32,768]{2,1,0:T(8,128)(2,1)S(1)} %all_to_all.5), kind=kLoop, calls=%fused_computation | loop fusion | flops 368640 | bytes 491520 | tf_op jit(solution)/shard_map/reduce_sum | solution.py:304
  (6 shorter events, 0.0 us)
Async XLA Ops:
  0.0 17.5 %slice-start = ((bf16[48,2,4096]{2,1,0:T(2,128)(2,1)}), bf16[2,2,4096]{2,1,0:T(2,128)(2,1)S(1)}, s32[]{:S(2)}) async-start(bf16[48,2,4096]{2,1,0:T(2,128)(2,1)} %virt.1), calls=%async_computation.1 | async-start | bytes 65536 | tf_op jit(solution)/shard_map/slice | solution.py:266
  0.0 17.5 %slice-start.1 = ((bf16[48,2,4096]{2,1,0:T(2,128)(2,1)}), bf16[3,2,4096]{2,1,0:T(2,128)(2,1)S(1)}, s32[]{:S(2)}) async-start(bf16[48,2,4096]{2,1,0:T(2,128)(2,1)} %virt.1), calls=%async_computation.2 | async-start | bytes 98304 | tf_op jit(solution)/shard_map/slice | solution.py:266
  0.0 18.0 %copy-start.2 = (s32[4,4,4]{2,1,0:T(4,128)S(1)}, s32[4,4,4]{2,1,0:T(4,128)}, u32[]{:S(2)}) copy-start(s32[4,4,4]{2,1,0:T(4,128)} %ids.3) | copy-start | bytes 772
  0.0 18.0 %copy-start = (bf16[1,4,64,4096]{3,2,1,0:T(8,128)(2,1)S(1)}, bf16[1,4,64,4096]{3,2,1,0:T(8,128)(2,1)}, u32[]{:S(2)}) copy-start(bf16[1,4,64,4096]{3,2,1,0:T(8,128)(2,1)} %tiles.3) | copy-start | bytes 6291460
  5.3 22.3 %collective-permute-start.2 = (bf16[4,64,2048]{2,1,0:T(8,128)(2,1)}, bf16[4,64,2048]{2,1,0:T(8,128)(2,1)S(1)}, u32[]{:S(2)}, u32[]{:S(2)}) collective-permute-start(bf16[4,64,2048]{2,1,0:T(8,128)(2,1)} %get-tuple-element.22), channel_id=1, source_target_pairs={{0,8},{16,24},{8,0},{24,16},{1,9},{17,25},{9,1},{25,17},{2,10},{18... | collective-permute-start | bytes 3145736 | tf_op jit(solution)/shard_map/ppermute | solution.py:205
  5.4 22.2 %collective-permute-start.3 = (bf16[4,64,2048]{2,1,0:T(8,128)(2,1)}, bf16[4,64,2048]{2,1,0:T(8,128)(2,1)}, u32[]{:S(2)}, u32[]{:S(2)}) collective-permute-start(bf16[4,64,2048]{2,1,0:T(8,128)(2,1)} %get-tuple-element.23), channel_id=1, source_target_pairs={{8,16},{16,8},{9,17},{17,9},{10,18},{18,10},{11,19},{19,11},{12,20... | collective-permute-start | bytes 3145736 | tf_op jit(solution)/shard_map/ppermute | solution.py:205
  9.9 7.7 %collective-permute-start = (bf16[2,2,4096]{2,1,0:T(2,128)(2,1)S(1)}, bf16[2,2,4096]{2,1,0:T(2,128)(2,1)S(1)}, u32[]{:S(2)}, u32[]{:S(2)}) collective-permute-start(bf16[2,2,4096]{2,1,0:T(2,128)(2,1)S(1)} %get-tuple-element.18), channel_id=1, source_target_pairs={{0,1},{1,2},{2,3},{3,4},{4,5},{5,6},{6,7},{8,9},{9,10},{10,11},{11... | collective-permute-start | bytes 98312 | tf_op jit(solution)/shard_map/ppermute | solution.py:264
  13.1 4.5 %collective-permute-start.1 = (bf16[1,2,4096]{2,1,0:T(2,128)(2,1)S(1)}, bf16[1,2,4096]{2,1,0:T(2,128)(2,1)S(1)}, u32[]{:S(2)}, u32[]{:S(2)}) collective-permute-start(bf16[1,2,4096]{2,1,0:T(2,128)(2,1)S(1)} %get-tuple-element.19), channel_id=1, source_target_pairs={{1,0},{2,1},{3,2},{4,3},{5,4},{6,5},{7,6},{9,8},{10,9},{11,10},{12... | collective-permute-start | bytes 49160 | tf_op jit(solution)/shard_map/ppermute | solution.py:265
  18.0 1.6 %copy-start.1 = (bf16[4,64,4096]{2,1,0:T(8,128)(2,1)S(1)}, bf16[4,64,4096]{2,1,0:T(8,128)(2,1)}, u32[]{:S(2)}) copy-start(bf16[4,64,4096]{2,1,0:T(8,128)(2,1)} %get-tuple-element.17.half) | copy-start | bytes 6291460
  32.9 4.0 %collective-permute-start.4 = (bf16[256,256]{1,0:T(8,128)(2,1)S(1)}, bf16[256,256]{1,0:T(8,128)(2,1)S(1)}, u32[]{:S(2)}, u32[]{:S(2)}) collective-permute-start(bf16[256,256]{1,0:T(8,128)(2,1)S(1)} %get-tuple-element.27), channel_id=1, source_target_pairs={{0,8},{16,24},{8,0},{24,16},{1,9},{17,25},{9,1},{25,17},{2,10},{18... | collective-permute-start | bytes 393224 | tf_op jit(solution)/shard_map/ppermute | solution.py:205
  33.0 6.6 %collective-permute-start.5 = (bf16[256,256]{1,0:T(8,128)(2,1)S(1)}, bf16[256,256]{1,0:T(8,128)(2,1)S(1)}, u32[]{:S(2)}, u32[]{:S(2)}) collective-permute-start(bf16[256,256]{1,0:T(8,128)(2,1)S(1)} %get-tuple-element.28), channel_id=1, source_target_pairs={{8,16},{16,8},{9,17},{17,9},{10,18},{18,10},{11,19},{19,11},{12,20... | collective-permute-start | bytes 393224 | tf_op jit(solution)/shard_map/ppermute | solution.py:205

commit v3 on v2

v3 whole, which is shorter than its diff:
```python
import functools

import jax
import jax.numpy as jnp
from jax import lax
from jax.experimental import pallas as pl
from jax.experimental.pallas import tpu as pltpu
from jax.sharding import PartitionSpec as P

RIB = 4
WIDE = 256
F32 = jnp.float32
BF16 = jnp.bfloat16


def is_odd():
    return lax.rem(lax.axis_index("grp"), 2) == 1


def go_rows(block, source, rows_in, rows_out, result):
    side = source.shape[0]
    lanes = 2 * side
    high = source.shape[1] // lanes
    some = block.shape[0] // 2
    pitch = rows_in.shape[0] // high
    low = lax.broadcasted_iota(jnp.int32, (some, lanes), 1) < side
    for h in range(high):
        rows_in[h * pitch : h * pitch + side, :] = source[:, h * lanes : (h + 1) * lanes].astype(F32)
    for p in range(0, side, 2):
        one = rows_in[pl.ds(p, high, stride=pitch), :]
        two = rows_in[pl.ds(p + 1, high, stride=pitch), :]
        crossed = [pltpu.roll(one, side, 1), pltpu.roll(two, side, 1)]
        x = jnp.concatenate(
            [jnp.concatenate([one, two], axis=1), jnp.concatenate(crossed, axis=1)], axis=0
        )
        y = jnp.dot(block, x.astype(BF16), preferred_element_type=F32)
        rows_out[pl.ds(p, some, stride=pitch), :] = jnp.where(low, y[:some, :lanes], y[some:, :lanes])
        rows_out[pl.ds(p + 1, some, stride=pitch), :] = jnp.where(low, y[:some, lanes:], y[some:, lanes:])
    for h in range(some):
        result(slice(h * lanes, (h + 1) * lanes), rows_out[h * pitch : h * pitch + side, :].astype(BF16))


def send_kernel(
    occ_in, ids_in, tiles, virt, even, odd, send_up, send_down, near, far, green, held, to_even, to_odd,
    occ, ids, rows_in, rows_out, sem, out_sem
):
    slots, side, flat = held.shape
    lanes, cut = 2 * side, even.shape[2]
    high = flat // lanes
    rows = occ.shape[0]
    first_in = pltpu.make_async_copy(occ_in, occ, sem.at[slots + 2])
    ids_copy = pltpu.make_async_copy(ids_in, ids, sem.at[slots + 3])
    first_in.start()
    ids_copy.start()
    fetch = [pltpu.make_async_copy(tiles.at[0, t], held.at[t], sem.at[t]) for t in range(slots)]
    for copy in fetch:
        copy.start()
    up = pltpu.make_async_copy(virt.at[pl.ds(rows - 2, 2)], send_up, sem.at[slots])
    down = pltpu.make_async_copy(virt.at[pl.ds(0, 1)], send_down, sem.at[slots + 1])
    near_copy = pltpu.make_async_copy(virt.at[pl.ds(0, 2)], near, sem.at[slots + 4])
    far_copy = pltpu.make_async_copy(virt.at[pl.ds(rows - 3, 3)], far, sem.at[slots + 5])
    edges = [up, down, near_copy, far_copy]
    for copy in edges:
        copy.start()
    group = lax.axis_index("grp")
    first = lax.axis_index("mem") * rows
    odd_one = is_odd()
    source = lax.broadcasted_iota(jnp.int32, (lanes, side), 0)
    target = lax.broadcasted_iota(jnp.int32, (lanes, side), 1)
    mu = lax.rem(source, side)
    some = high // 2
    first_in.wait()
    for end, row in enumerate((0, rows - 1)):
        line = occ[row : row + 1, :].astype(F32)
        block = jnp.concatenate([line[:, h * lanes : (h + 1) * lanes] for h in range(high)], axis=0)
        for parity in range(2):
            other = (lax.rem(mu, 2) != parity).astype(jnp.int32)
            pick = (source // side == parity) & (target == mu // 2 + other * high)
            chosen = jnp.dot(
                block.astype(BF16), pick.astype(BF16), preferred_element_type=F32
            ).astype(BF16)
            for part in range(2):
                green[end, part, parity * some : (parity + 1) * some, :] = chosen[part * some : (part + 1) * some]
    ids_copy.wait()
    results = []
    for t in range(slots):
        fetch[t].wait()
        block = green[(ids[group, 1, t] != first).astype(jnp.int32), 1]

        def result(at, done):
            raw = held[t, :, at]
            to_even[t, :, at] = jnp.where(odd_one, done, raw)
            to_odd[t, :, at] = jnp.where(odd_one, raw, done)

        go_rows(block, held.at[t], rows_in, rows_out, result)
        for k, (source, target) in enumerate(((to_odd, odd), (to_even, even))):
            copy = pltpu.make_async_copy(source.at[t], target.at[t], out_sem.at[t, k])
            copy.start()
            results.append(copy)
    for copy in results + edges:
        copy.wait()


def half_kernel(rows, ids, green, tiles, even, odd, half, rows_in, rows_out, sem):
    slots, side, flat = half.shape
    cut = even.shape[2]
    group = lax.axis_index("grp")
    first = lax.axis_index("mem") * rows
    high_part = half.at[:, :, pl.ds(cut, flat - cut)]

    @pl.when(is_odd())
    def _():
        pltpu.make_async_copy(even, high_part, sem.at[0]).start()

    @pl.when(jnp.logical_not(is_odd()))
    def _():
        pltpu.make_async_copy(odd, high_part, sem.at[0]).start()

    for t in range(slots):
        block = green[(ids[group, 1, t] != first).astype(jnp.int32), 0]

        def result(at, done):
            half[t, :, at] = done

        go_rows(block, tiles.at[0, t], rows_in, rows_out, result)
    pltpu.make_async_copy(even, high_part, sem.at[0]).wait()


def combined(products, slots, side, ids, left, right, left_on, right_on, total):
    width = slots * side

    def spread(values, owner):
        out = jnp.full(owner.shape, values[0], jnp.int32)
        for u in range(1, slots):
            out = jnp.where(owner == u, values[u], out)
        return out

    owner = lax.broadcasted_iota(jnp.int32, (1, width), 1) // side
    live = [ids[right, 3, u] * right_on for u in range(slots)]
    row_block = spread([jnp.where(live[u] > 0, ids[right, 1, u], -1) for u in range(slots)], owner)
    col_block = spread([ids[right, 2, u] for u in range(slots)], owner)
    total[...] = jnp.zeros_like(total)
    for t in range(slots):
        same = row_block == jnp.where(ids[left, 3, t] * left_on > 0, ids[left, 1, t], -2)
        term = jnp.zeros((side, width), F32)
        for j in range(3):
            at = (t * 3 + j) * side
            match = (same & (col_block == ids[left, 2, t] + (j - 1))).astype(F32)
            term = term + products[at : at + side, :] * match
        total[ids[left, 0, t]] += term
    ahead = lax.broadcasted_iota(jnp.int32, (side, RIB * side), 1)
    ahead = ahead - lax.broadcasted_iota(jnp.int32, (side, RIB * side), 0)
    place = [(ahead == ids[right, 0, u] * side).astype(F32).astype(BF16) for u in range(slots)]
    place = jnp.concatenate(place, axis=0)
    summed = total[...].reshape(RIB * side, width)
    coarse = summed.astype(BF16)
    fine = (summed - coarse.astype(F32)).astype(BF16)
    return jnp.dot(coarse, place, preferred_element_type=F32) + jnp.dot(
        fine, place, preferred_element_type=F32
    )


NT = (((1,), (1,)), ((), ()))
NN = (((1,), (0,)), ((), ()))


def prepare_kernel(rows, ids, before, near, far, after, half, tiles, y_all, v_high, table, mats):
    slots, side, flat = half.shape
    cut = flat - v_high.shape[1]
    group = lax.axis_index("grp")
    first = lax.axis_index("mem") * rows
    count = rows * lax.axis_size("mem")
    copies = WIDE // side
    own = lax.broadcasted_iota(jnp.int32, (WIDE, WIDE), 0) // side
    own = own == lax.broadcasted_iota(jnp.int32, (WIDE, WIDE), 1) // side
    own = own.astype(F32).astype(BF16)

    at = 0
    for source in (before, near, far, after):
        for k in range(source.shape[0]):
            table[at : at + 2, :] = source[k].astype(F32)
            at += 2
    lanes = 2 * side
    pairs = side // 2
    line_of = lax.broadcasted_iota(jnp.int32, (side, pairs), 0) // 2
    line_of = (line_of == lax.broadcasted_iota(jnp.int32, (side, pairs), 1)).astype(F32).astype(BF16)
    even_row = lax.rem(lax.broadcasted_iota(jnp.int32, (side, lanes), 0), 2) == 0
    straight = even_row == (lax.broadcasted_iota(jnp.int32, (side, lanes), 1) < side)

    def spread(row, keep=None):
        line = table[pl.ds(row, 1), :]
        if keep is not None:
            line = line * keep
        block = jnp.concatenate([line[:, h * lanes : (h + 1) * lanes] for h in range(pairs)], axis=0)
        block = jnp.dot(line_of, block.astype(BF16), preferred_element_type=F32)
        block = jnp.where(straight, block, pltpu.roll(block, side, 1)).astype(BF16)
        row = jnp.concatenate([block] * (copies // 2), axis=1)
        return jnp.concatenate([row] * copies, axis=0) * own

    for t in range(slots):
        a, b = ids[group, 1, t], ids[group, 2, t]
        at = jnp.where(a == first, 2, 6) + b - a
        keep = (b + 1 < count).astype(F32)
        mats[t * 3] = spread(2 * at - 1)
        mats[t * 3 + 1] = spread(2 * at)
        mats[t * 3 + 2] = spread(2 * at + 1, keep)

    def transform(source, low, result, dims):
        lanes = result.shape[1]
        for t in range(slots):
            x = [source[t, :, c : c + WIDE] for c in range(low, low + lanes, WIDE)]
            x = jnp.concatenate(x, axis=0)
            for j in range(3):
                y = lax.dot_general(x, mats[t * 3 + j], dims[j], preferred_element_type=F32).astype(BF16)
                at = slice((t * 3 + j) * side, (t * 3 + j + 1) * side)
                for k in range(lanes // WIDE):
                    result[at, k * WIDE : (k + 1) * WIDE] = y[k * side : (k + 1) * side]

    transform(half, 0, y_all, (NT, NN, NN))
    transform(tiles.at[0], cut, v_high, (NT, NT, NN))


def middle_kernel(ids, y_all, tiles, after, middle, total, products):
    slots, side, flat = tiles.shape[1:]
    group = lax.axis_index("grp")
    products[...] = lax.dot_general(
        y_all[...], tiles[0].reshape(slots * side, flat), NT, preferred_element_type=F32
    )
    middle[...] = combined(products, slots, side, ids, group, group, 1, 1, total)


def pair_kernel(odd_is_upper_group, ids, y_all, v_high, other, part, send, total, products):
    slots, side, cut = other.shape
    group = lax.axis_index("grp")
    last = lax.axis_size("grp") - 1
    odd_one = is_odd()
    below = odd_one if odd_is_upper_group else jnp.logical_not(odd_one)
    right = jnp.where(below, jnp.maximum(group - 1, 0), jnp.minimum(group + 1, last))
    right_on = jnp.where(below, group > 0, group < last).astype(jnp.int32)

    @pl.when(below)
    def _():
        products[...] = lax.dot_general(
            y_all[:, :cut], other[...].reshape(slots * side, cut), NT, preferred_element_type=F32
        )

    @pl.when(jnp.logical_not(below))
    def _():
        products[...] = lax.dot_general(
            v_high[...], other[...].reshape(slots * side, cut), NT, preferred_element_type=F32
        )

    mine = combined(products, slots, side, ids, group, right, 1, right_on, total)
    part[...] = mine
    send[...] = mine.T.astype(BF16)


def band_kernel(middle, even, odd, got_even, got_odd, band):
    side = middle.shape[1]
    odd_one = is_odd()
    with_even = (even[...] + got_even[...].astype(F32)).astype(BF16)
    with_odd = (odd[...] + got_odd[...].astype(F32)).astype(BF16)
    band[:, :side] = jnp.where(odd_one, with_even, with_odd)
    band[:, side : 2 * side] = middle[...].astype(BF16)
    band[:, 2 * side :] = jnp.where(odd_one, with_odd, with_even)


def swapped(block, parity):
    count = lax.axis_size("grp")
    pairs = [(i, i + 1) for i in range(parity, count - 1, 2)]
    return lax.ppermute(block, "grp", pairs + [(b, a) for a, b in pairs])


def params(mib):
    return pltpu.CompilerParams(vmem_limit_bytes=mib * 1024 * 1024)


def in_hbm(x):
    return pltpu.with_memory_space_constraint(x, pltpu.HBM)


def in_vmem(x):
    return pltpu.with_memory_space_constraint(x, pltpu.VMEM)


WHOLE = pl.BlockSpec(memory_space=pltpu.VMEM)
SCALAR = pl.BlockSpec(memory_space=pltpu.SMEM)


def body(tiles, tile_ids, occ_blocks, virt_blocks):
    slots, side, flat = tiles.shape[1:]
    rows = occ_blocks.shape[0]
    members = lax.axis_size("mem")
    cut = flat // 2
    width = RIB * side

    anywhere = pl.BlockSpec(memory_space=pltpu.HBM)
    pitch = side + 8
    strided = [pltpu.VMEM((flat // (2 * side) * pitch, 2 * side), F32)] * 2
    even, odd, send_up, send_down, near, far, green = pl.pallas_call(
        send_kernel,
        in_specs=[anywhere] * 4,
        out_specs=[anywhere] * 6 + [WHOLE],
        out_shape=[
            pltpu.HBM((slots, side, cut), BF16),
            pltpu.HBM((slots, side, cut), BF16),
            jax.ShapeDtypeStruct((2, 2, flat), BF16),
            jax.ShapeDtypeStruct((1, 2, flat), BF16),
            jax.ShapeDtypeStruct((2, 2, flat), BF16),
            jax.ShapeDtypeStruct((3, 2, flat), BF16),
            jax.ShapeDtypeStruct((2, 2, side // 2, side), BF16),
        ],
        scratch_shapes=[
            pltpu.VMEM((slots, side, flat), BF16),
            pltpu.VMEM((slots, side, cut), BF16),
            pltpu.VMEM((slots, side, cut), BF16),
            pltpu.VMEM(occ_blocks.shape, BF16),
            pltpu.SMEM(tile_ids.shape, jnp.int32),
            *strided,
            pltpu.SemaphoreType.DMA((slots + 6,)),
            pltpu.SemaphoreType.DMA((slots, 2)),
        ],
        compiler_params=params(16),
    )(*(in_hbm(x) for x in (occ_blocks, tile_ids, tiles, virt_blocks)))
    got_odd = swapped(odd, 1)
    got_even = swapped(even, 0)

    macs = slots * slots * 3 * side * side * flat
    half = pl.pallas_call(
        functools.partial(half_kernel, rows),
        in_specs=[SCALAR, WHOLE, WHOLE, anywhere, anywhere],
        out_specs=WHOLE,
        out_shape=pltpu.VMEM((slots, side, flat), BF16),
        scratch_shapes=[*strided, pltpu.SemaphoreType.DMA((1,))],
        compiler_params=params(12),
        cost_estimate=pl.CostEstimate(flops=2 * macs, bytes_accessed=4 * slots * side * flat, transcendentals=0),
    )(tile_ids, green, tiles, in_hbm(even), in_hbm(odd))
    forward = [(i, i + 1) for i in range(members - 1)]
    backward = [(b, a) for a, b in forward]
    before = lax.ppermute(send_up, "mem", forward)
    after = lax.ppermute(send_down, "mem", backward)
    y_all, v_high = pl.pallas_call(
        functools.partial(prepare_kernel, rows),
        in_specs=[SCALAR] + [WHOLE] * 6,
        out_specs=[WHOLE, WHOLE],
        out_shape=[
            pltpu.VMEM((slots * 3 * side, flat), BF16),
            pltpu.VMEM((slots * 3 * side, flat - cut), BF16),
        ],
        scratch_shapes=[pltpu.VMEM((16, flat), F32), pltpu.VMEM((slots * 3, WIDE, WIDE), BF16)],
        compiler_params=params(20),
        cost_estimate=pl.CostEstimate(flops=3 * macs, bytes_accessed=10 * slots * side * flat, transcendentals=0),
    )(tile_ids, before, near, far, after, half, tiles)
    found = [
        pltpu.VMEM((RIB, side, slots * side), F32),
        pltpu.VMEM((slots * 3 * side, slots * side), F32),
    ]

    def coupled(got, odd_is_upper_group):
        return pl.pallas_call(
            functools.partial(pair_kernel, odd_is_upper_group),
            in_specs=[SCALAR] + [WHOLE] * 3,
            out_specs=[WHOLE] * 2,
            out_shape=[pltpu.VMEM((width, width), F32), pltpu.VMEM((width, width), BF16)],
            scratch_shapes=found,
            compiler_params=params(20),
            cost_estimate=pl.CostEstimate(flops=macs, bytes_accessed=8 * slots * side * flat, transcendentals=0),
        )(tile_ids, y_all, v_high, got)

    part_even, out_even = coupled(got_even, True)
    back_even = swapped(out_even, 0)
    part_odd, out_odd = coupled(got_odd, False)
    back_odd = swapped(out_odd, 1)
    middle = pl.pallas_call(
        middle_kernel,
        in_specs=[SCALAR, WHOLE, WHOLE, pl.BlockSpec(memory_space=pl.ANY)],
        out_specs=WHOLE,
        out_shape=pltpu.VMEM((width, width), F32),
        scratch_shapes=found,
        compiler_params=params(20),
        cost_estimate=pl.CostEstimate(flops=2 * macs, bytes_accessed=8 * slots * side * flat, transcendentals=0),
    )(tile_ids, y_all, tiles, out_odd)
    band = pl.pallas_call(
        band_kernel,
        in_specs=[WHOLE] * 5,
        out_specs=WHOLE,
        out_shape=jax.ShapeDtypeStruct((width, 3 * width), BF16),
        compiler_params=params(8),
    )(middle, part_even, part_odd, back_even, back_odd)
    parts = lax.all_to_all(band.reshape(members, width // members, 3 * width), "mem", 0, 0)
    return parts.astype(F32).sum(axis=0)


def solution(mesh):
    placed = (
        P("grp", "mem", None, None),
        P(None, None, "mem"),
        P("mem", None),
        P("mem", None, None),
    )
    return jax.shard_map(
        body, mesh=mesh, in_specs=placed, out_specs=P(("grp", "mem"), None), check_vma=False
    )
```

time: 54.8 us -> 48 us (0.88); the launches traced: 53.9 us -> 47.8 us
  waiting for transfers between devices: 5.82 us -> 0.62 us
  blocking collectives: 13.6 us -> 16.2 us
  local copies, waits for them, and re-layouts: 1.81 us -> 0.01 us
  Pallas kernels: 18.7 us -> 17.4 us
    ppermute x1, waiting for transfers between devices: 3.18 us -> 0.01 us  [body(): after = lax.ppermute(send_down, 'mem', backward)]
    all_to_all x1, blocking collectives: 13.6 us -> 16.2 us  [body(): lax.all_to_all(band.reshape(members, width // members, 3 * width), 'mem',...]
    ppermute x4, waiting for transfers between devices: 2.63 us -> 0.62 us  [swapped(): return lax.ppermute(block, 'grp', pairs + [(b, a) for a, b in pairs])]
    unnamed x6 -> x4, local copies, waits for them, and re-layouts: 1.59 us -> 0.01 us
    pallas_call x3 -> x6, Pallas kernels: 18.5 us -> 17.3 us  [the longest x1 4.37 us: body(): pl.pallas_call(send_kernel, in_specs=[anywhere] * 4, out_specs=[anywhere]...]
    ppermute x4, starting transfers between devices: 8.61 us -> 7.49 us  [swapped(): return lax.ppermute(block, 'grp', pairs + [(b, a) for a, b in pairs])]
    ppermute x1, starting transfers between devices: 3.16 us -> 3.99 us  [body(): before = lax.ppermute(send_up, 'mem', forward)]
  transfers between devices with their start and end apart: 6 -> 6, of which waited for: 2 -> 1; matrix products, arithmetic and copies ran while one was open for 1% -> 0% of each run, Pallas kernels for 15% -> 27%
where the time goes in v3:
time: 48 us; the launch traced here: 47.8 us
  Pallas kernels  17.4 us (36%)
  blocking collectives  16.2 us (34%)
  starting transfers between devices  12.8 us (27%)
  other arithmetic  0.69 us (1%)
  waiting for transfers between devices  0.62 us (1%)
    all_to_all x1, blocking collectives, body(): lax.all_to_all(band.reshape(members, width // members, 3 * width), 'mem',...  16.2 us
    ppermute x4, starting transfers between devices, swapped(): return lax.ppermute(block, 'grp', pairs + [(b, a) for a, b in pairs])  7.49 us
    pallas_call x1, Pallas kernels, body(): pl.pallas_call(send_kernel, in_specs=[anywhere] * 4, out_specs=[anywhere]...  4.37 us
    pallas_call x2, Pallas kernels, coupled(): pl.pallas_call(functools.partial(pair_kernel, odd_is_upper_group), in_spe...  4.16 us
    ppermute x1, starting transfers between devices, body(): before = lax.ppermute(send_up, 'mem', forward)  3.99 us
    pallas_call x1, Pallas kernels, body(): pl.pallas_call(functools.partial(prepare_kernel, rows), in_specs=[SCALAR]...  3.62 us
    pallas_call x1, Pallas kernels, body(): pl.pallas_call(middle_kernel, in_specs=[SCALAR, WHOLE, WHOLE, pl.BlockSpe...  2.81 us
    pallas_call x1, Pallas kernels, body(): pl.pallas_call(functools.partial(half_kernel, rows), in_specs=[SCALAR, WH...  2.32 us
  transfers between devices with their start and end apart: 6, of which 1 were waited for; matrix products, arithmetic and copies ran while one was open for 0% of the time, Pallas kernels for 27%

profile of v3, /device:TPU:1, one launch (start us, length us, event | category | flops | bytes accessed | tf_op | source)
XLA Modules:
  0.0 47.8 jit_solution(8351648558257805357)
XLA Ops:
  0.0 0.0 copy-start.1
  0.0 4.4 %shard_map.46 = (bf16[4,64,2048]{2,1,0:T(8,128)(2,1)}, bf16[4,64,2048]{2,1,0:T(8,128)(2,1)}, bf16[2,2,4096]{2,1,0:T(2,128)(2,1)S(1)}, bf16[1,2,4096]{2,1,0:T(2,1...) custom-call(bf16[48,4096]{1,0:T(8,128)(2,1)} %occ_in.1, ...), custom_call_target="tpu_custom_call" | custom-call | tf_op jit(solution)/shard_map/pallas_call | solution.py:300
  4.4 0.1 collective-permute-start.3
  4.5 4.5 %collective-permute-start.2 = (bf16[4,64,2048]{2,1,0:T(8,128)(2,1)}, bf16[4,64,2048]{2,1,0:T(8,128)(2,1)S(1)}, u32[]{:S(2)}, u32[]{:S(2)}) collective-permute-start(bf16[4,64,2048]{2,1,0:T(8,128)(2,1)} %get-tuple-element.24.odd), channel_id=1, source_target_pairs={{8,16},{16,8},{9,17},{17,9},{10,18},{18,10},{11,19},{19,11},{12,20... | collective-permute-start | bytes 3145736 | tf_op jit(solution)/shard_map/ppermute | solution.py:271
  9.0 1.3 %collective-permute-start.1 = (bf16[1,2,4096]{2,1,0:T(2,128)(2,1)S(1)}, bf16[1,2,4096]{2,1,0:T(2,128)(2,1)S(1)}, u32[]{:S(2)}, u32[]{:S(2)}) collective-permute-start(bf16[1,2,4096]{2,1,0:T(2,128)(2,1)S(1)} %get-tuple-element.21), channel_id=1, source_target_pairs={{1,0},{2,1},{3,2},{4,3},{5,4},{6,5},{7,6},{9,8},{10,9},{11,10},{12... | collective-permute-start | bytes 49160 | tf_op jit(solution)/shard_map/ppermute | solution.py:341
  10.3 4.0 %collective-permute-start = (bf16[2,2,4096]{2,1,0:T(2,128)(2,1)S(1)}, bf16[2,2,4096]{2,1,0:T(2,128)(2,1)S(1)}, u32[]{:S(2)}, u32[]{:S(2)}) collective-permute-start(bf16[2,2,4096]{2,1,0:T(2,128)(2,1)S(1)} %get-tuple-element.18), channel_id=1, source_target_pairs={{0,1},{1,2},{2,3},{3,4},{4,5},{5,6},{6,7},{8,9},{9,10},{10,11},{11... | collective-permute-start | bytes 98312 | tf_op jit(solution)/shard_map/ppermute | solution.py:340
  14.3 0.0 copy-done.1
  14.3 0.0 copy-done
  14.3 2.3 %shard_map.47.half = bf16[4,64,4096]{2,1,0:T(8,128)(2,1)S(1)} custom-call(s32[4,4,4]{2,1,0:T(4,128)S(1)} %copy-done.1, bf16[2,2,32,64]{3,2,1,0:T(8,128)(2,1)S(1)} %get-tuple-element.22.green, bf16[1,4,64,4096]{3,2,1,0:T(8,128)(2,1)S(1)} %copy-done, bf16[4,64,2048]{2,1,0:T(8,128)(2,1)} %get-tuple-element.23.even, bf16[4,64,2048]{2,1,0:T(8,128)(2,1)} %get-tuple-element.24.odd), custom_call_target="tpu_custom_call" | custom-call | flops 1610612736 | bytes 4194304 | tf_op jit(solution)/shard_map/pallas_call | solution.py:329
  16.6 0.0 collective-permute-done.1.after
  16.6 0.0 collective-permute-done.before
  16.6 3.6 %shard_map.48 = (bf16[768,4096]{1,0:T(8,128)(2,1)S(1)}, bf16[768,2048]{1,0:T(8,128)(2,1)S(1)}) custom-call(s32[4,4,4]{2,1,0:T(4,128)S(1)} %copy-done.1, bf16[2,2,4096]{2,1,0:T(2,128)(2,1)S(1)} %collective-permute-done.before, bf16[2,2,4096]{2,1,0:T(2,128)(2,1)S(1)} %get-tuple-element.19.near, bf16[3,2,4096]{2,1,0:T(2,128)(2,1)S(1)} %get-tuple-element.20.far, ...), custom_call_target="tpu_custom_call" | custom-call | flops 2415919104 | bytes 10485760 | tf_op jit(solution)/shard_map/pallas_call | solution.py:342
  20.3 0.0 collective-permute-done.3.other
  20.3 2.1 %shard_map.51 = (f32[256,256]{1,0:T(8,128)S(1)}, bf16[256,256]{1,0:T(8,128)(2,1)S(1)}) custom-call(s32[4,4,4]{2,1,0:T(4,128)S(1)} %copy-done.1, bf16[768,4096]{1,0:T(8,128)(2,1)S(1)} %get-tuple-element.25.y_all, bf16[768,2048]{1,0:T(8,128)(2,1)S(1)} %get-tuple-element.26.v_high, bf16[4,64,2048]{2,1,0:T(8,128)(2,1)S(1)} %collective-permute-done.3.other), custom_call_target="tpu_custom_call" | custom-call | flops 805306368 | bytes 8388608 | tf_op jit(solution)/shard_map/pallas_call | solution.py:360
  22.4 0.1 collective-permute-start.4
  22.5 0.0 collective-permute-done.2.other
  22.5 2.1 %shard_map.49 = (f32[256,256]{1,0:T(8,128)S(1)}, bf16[256,256]{1,0:T(8,128)(2,1)S(1)}) custom-call(s32[4,4,4]{2,1,0:T(4,128)S(1)} %copy-done.1, bf16[768,4096]{1,0:T(8,128)(2,1)S(1)} %get-tuple-element.25.y_all, bf16[768,2048]{1,0:T(8,128)(2,1)S(1)} %get-tuple-element.26.v_high, bf16[4,64,2048]{2,1,0:T(8,128)(2,1)S(1)} %collective-permute-done.2.other), custom_call_target="tpu_custom_call" | custom-call | flops 805306368 | bytes 8388608 | tf_op jit(solution)/shard_map/pallas_call | solution.py:360
  24.6 2.8 %collective-permute-start.5 = (bf16[256,256]{1,0:T(8,128)(2,1)S(1)}, bf16[256,256]{1,0:T(8,128)(2,1)S(1)}, u32[]{:S(2)}, u32[]{:S(2)}) collective-permute-start(bf16[256,256]{1,0:T(8,128)(2,1)S(1)} %get-tuple-element.27.after), channel_id=1, source_target_pairs={{8,16},{16,8},{9,17},{17,9},{10,18},{18,10},{11,19},{19,11},{12,20... | collective-permute-start | bytes 393224 | tf_op jit(solution)/shard_map/ppermute | solution.py:271
  27.4 2.8 %shard_map.50.middle = f32[256,256]{1,0:T(8,128)S(1)} custom-call(s32[4,4,4]{2,1,0:T(4,128)S(1)} %copy-done.1, bf16[768,4096]{1,0:T(8,128)(2,1)S(1)} %get-tuple-element.25.y_all, bf16[1,4,64,4096]{3,2,1,0:T(8,128)(2,1)S(1)} %copy-done, bf16[256,256]{1,0:T(8,128)(2,1)S(1)} %get-tuple-element.27.after), custom_call_target="tpu_custom_call" | custom-call | flops 1610612736 | bytes 8388608 | tf_op jit(solution)/shard_map/pallas_call | solution.py:374
  30.2 0.0 collective-permute-done.4.got_even
  30.2 0.6 %collective-permute-done.5.got_odd = bf16[256,256]{1,0:T(8,128)(2,1)S(1)} collective-permute-done((bf16[256,256]{1,0:T(8,128)(2,1)S(1)}, bf16[256,256]{1,0:T(8,128)(2,1)S(1)}, u32[]{:S(2)}, u32[]{:S(2)}) %collective-permute-start.5) | collective-permute-done | bytes 131104 | tf_op jit(solution)/shard_map/ppermute | solution.py:271
  30.8 0.1 shard_map.52
  30.9 16.2 %all_to_all.5 = bf16[8,32,768]{2,1,0:T(8,128)(2,1)S(1)} all-to-all(bf16[8,32,768]{2,1,0:T(8,128)(2,1)S(1)} %bitcast.1), channel_id=1, replica_groups=mesh['grp'=4,'mem'=8] {'mem'}, dimensions={0} | all-to-all | bytes 786432 | tf_op jit(solution)/shard_map/all_to_all | solution.py:390
  47.1 0.7 %convert_reduce_fusion = f32[32,768]{1,0:T(8,128)} fusion(bf16[8,32,768]{2,1,0:T(8,128)(2,1)S(1)} %all_to_all.5), kind=kLoop, calls=%fused_computation | loop fusion | flops 368640 | bytes 491520 | tf_op jit(solution)/shard_map/reduce_sum | solution.py:391
  (1 shorter events, 0.0 us)
Async XLA Ops:
  0.0 14.3 %copy-start.1 = (s32[4,4,4]{2,1,0:T(4,128)S(1)}, s32[4,4,4]{2,1,0:T(4,128)}, u32[]{:S(2)}) copy-start(s32[4,4,4]{2,1,0:T(4,128)} %ids.9) | copy-start | bytes 772
  0.0 14.3 %copy-start = (bf16[1,4,64,4096]{3,2,1,0:T(8,128)(2,1)S(1)}, bf16[1,4,64,4096]{3,2,1,0:T(8,128)(2,1)}, u32[]{:S(2)}) copy-start(bf16[1,4,64,4096]{3,2,1,0:T(8,128)(2,1)} %tiles.7) | copy-start | bytes 6291460
  4.4 15.9 %collective-permute-start.3 = (bf16[4,64,2048]{2,1,0:T(8,128)(2,1)}, bf16[4,64,2048]{2,1,0:T(8,128)(2,1)S(1)}, u32[]{:S(2)}, u32[]{:S(2)}) collective-permute-start(bf16[4,64,2048]{2,1,0:T(8,128)(2,1)} %get-tuple-element.23.even), channel_id=1, source_target_pairs={{0,8},{16,24},{8,0},{24,16},{1,9},{17,25},{9,1},{25,17},{2,10},{18... | collective-permute-start | bytes 3145736 | tf_op jit(solution)/shard_map/ppermute | solution.py:271
  4.5 17.9 %collective-permute-start.2 = (bf16[4,64,2048]{2,1,0:T(8,128)(2,1)}, bf16[4,64,2048]{2,1,0:T(8,128)(2,1)S(1)}, u32[]{:S(2)}, u32[]{:S(2)}) collective-permute-start(bf16[4,64,2048]{2,1,0:T(8,128)(2,1)} %get-tuple-element.24.odd), channel_id=1, source_target_pairs={{8,16},{16,8},{9,17},{17,9},{10,18},{18,10},{11,19},{19,11},{12,20... | collective-permute-start | bytes 3145736 | tf_op jit(solution)/shard_map/ppermute | solution.py:271
  9.0 7.7 %collective-permute-start.1 = (bf16[1,2,4096]{2,1,0:T(2,128)(2,1)S(1)}, bf16[1,2,4096]{2,1,0:T(2,128)(2,1)S(1)}, u32[]{:S(2)}, u32[]{:S(2)}) collective-permute-start(bf16[1,2,4096]{2,1,0:T(2,128)(2,1)S(1)} %get-tuple-element.21), channel_id=1, source_target_pairs={{1,0},{2,1},{3,2},{4,3},{5,4},{6,5},{7,6},{9,8},{10,9},{11,10},{12... | collective-permute-start | bytes 49160 | tf_op jit(solution)/shard_map/ppermute | solution.py:341
  10.3 6.4 %collective-permute-start = (bf16[2,2,4096]{2,1,0:T(2,128)(2,1)S(1)}, bf16[2,2,4096]{2,1,0:T(2,128)(2,1)S(1)}, u32[]{:S(2)}, u32[]{:S(2)}) collective-permute-start(bf16[2,2,4096]{2,1,0:T(2,128)(2,1)S(1)} %get-tuple-element.18), channel_id=1, source_target_pairs={{0,1},{1,2},{2,3},{3,4},{4,5},{5,6},{6,7},{8,9},{9,10},{10,11},{11... | collective-permute-start | bytes 98312 | tf_op jit(solution)/shard_map/ppermute | solution.py:340
  22.4 7.8 %collective-permute-start.4 = (bf16[256,256]{1,0:T(8,128)(2,1)S(1)}, bf16[256,256]{1,0:T(8,128)(2,1)S(1)}, u32[]{:S(2)}, u32[]{:S(2)}) collective-permute-start(bf16[256,256]{1,0:T(8,128)(2,1)S(1)} %get-tuple-element.30), channel_id=1, source_target_pairs={{0,8},{16,24},{8,0},{24,16},{1,9},{17,25},{9,1},{25,17},{2,10},{18... | collective-permute-start | bytes 393224 | tf_op jit(solution)/shard_map/ppermute | solution.py:271
  24.6 6.3 %collective-permute-start.5 = (bf16[256,256]{1,0:T(8,128)(2,1)S(1)}, bf16[256,256]{1,0:T(8,128)(2,1)S(1)}, u32[]{:S(2)}, u32[]{:S(2)}) collective-permute-start(bf16[256,256]{1,0:T(8,128)(2,1)S(1)} %get-tuple-element.27.after), channel_id=1, source_target_pairs={{8,16},{16,8},{9,17},{17,9},{10,18},{18,10},{11,19},{19,11},{12,20... | collective-permute-start | bytes 393224 | tf_op jit(solution)/shard_map/ppermute | solution.py:271

commit v4 on v3

--- a/solution.py
+++ b/solution.py
@@ -41,8 +41,8 @@
 
 
 def send_kernel(
-    occ_in, ids_in, tiles, virt, even, odd, send_up, send_down, near, far, green, held, to_even, to_odd,
-    occ, ids, rows_in, rows_out, sem, out_sem
+    occ_in, ids_in, tiles, virt, even, odd, send_up, send_down, near, far, green, held,
+    occ, ids, rows_in, rows_out, sem
 ):
     slots, side, flat = held.shape
     lanes, cut = 2 * side, even.shape[2]
@@ -82,22 +82,17 @@
             for part in range(2):
                 green[end, part, parity * some : (parity + 1) * some, :] = chosen[part * some : (part + 1) * some]
     ids_copy.wait()
-    results = []
     for t in range(slots):
         fetch[t].wait()
         block = green[(ids[group, 1, t] != first).astype(jnp.int32), 1]
 
         def result(at, done):
             raw = held[t, :, at]
-            to_even[t, :, at] = jnp.where(odd_one, done, raw)
-            to_odd[t, :, at] = jnp.where(odd_one, raw, done)
+            even[t, :, at] = jnp.where(odd_one, done, raw)
+            odd[t, :, at] = jnp.where(odd_one, raw, done)
 
         go_rows(block, held.at[t], rows_in, rows_out, result)
-        for k, (source, target) in enumerate(((to_odd, odd), (to_even, even))):
-            copy = pltpu.make_async_copy(source.at[t], target.at[t], out_sem.at[t, k])
-            copy.start()
-            results.append(copy)
-    for copy in results + edges:
+    for copy in edges:
         copy.wait()
 
 
@@ -300,10 +295,10 @@
     even, odd, send_up, send_down, near, far, green = pl.pallas_call(
         send_kernel,
         in_specs=[anywhere] * 4,
-        out_specs=[anywhere] * 6 + [WHOLE],
+        out_specs=[WHOLE] * 2 + [anywhere] * 4 + [WHOLE],
         out_shape=[
-            pltpu.HBM((slots, side, cut), BF16),
-            pltpu.HBM((slots, side, cut), BF16),
+            jax.ShapeDtypeStruct((slots, side, cut), BF16),
+            jax.ShapeDtypeStruct((slots, side, cut), BF16),
             jax.ShapeDtypeStruct((2, 2, flat), BF16),
             jax.ShapeDtypeStruct((1, 2, flat), BF16),
             jax.ShapeDtypeStruct((2, 2, flat), BF16),
@@ -312,13 +307,10 @@
         ],
         scratch_shapes=[
             pltpu.VMEM((slots, side, flat), BF16),
-            pltpu.VMEM((slots, side, cut), BF16),
-            pltpu.VMEM((slots, side, cut), BF16),
             pltpu.VMEM(occ_blocks.shape, BF16),
             pltpu.SMEM(tile_ids.shape, jnp.int32),
             *strided,
             pltpu.SemaphoreType.DMA((slots + 6,)),
-            pltpu.SemaphoreType.DMA((slots, 2)),
         ],
         compiler_params=params(16),
     )(*(in_hbm(x) for x in (occ_blocks, tile_ids, tiles, virt_blocks)))
@@ -328,13 +320,13 @@
     macs = slots * slots * 3 * side * side * flat
     half = pl.pallas_call(
         functools.partial(half_kernel, rows),
-        in_specs=[SCALAR, WHOLE, WHOLE, anywhere, anywhere],
+        in_specs=[SCALAR, WHOLE, WHOLE] + [pl.BlockSpec(memory_space=pl.ANY)] * 2,
         out_specs=WHOLE,
         out_shape=pltpu.VMEM((slots, side, flat), BF16),
         scratch_shapes=[*strided, pltpu.SemaphoreType.DMA((1,))],
         compiler_params=params(12),
         cost_estimate=pl.CostEstimate(flops=2 * macs, bytes_accessed=4 * slots * side * flat, transcendentals=0),
-    )(tile_ids, green, tiles, in_hbm(even), in_hbm(odd))
+    )(tile_ids, green, tiles, even, odd)
     forward = [(i, i + 1) for i in range(members - 1)]
     backward = [(b, a) for a, b in forward]
     before = lax.ppermute(send_up, "mem", forward)

time: 48 us -> 47.2 us (0.983)
  Pallas kernels: 17.4 us -> 16.6 us
    pallas_call x1, Pallas kernels: 4.37 us -> 3.52 us  [body(): pl.pallas_call(send_kernel, in_specs=[anywhere] * 4, out_specs=[WHOLE] *...]
  transfers between devices with their start and end apart: 6 -> 6, of which waited for: 1 -> 1; matrix products, arithmetic and copies ran while one was open for 0% -> 0% of each run, Pallas kernels for 27% -> 28%
where the time goes in v4:
time: 47.2 us; the launch traced here: 47 us
  Pallas kernels  16.6 us (35%)
  blocking collectives  16.1 us (34%)
  starting transfers between devices  12.5 us (26%)
  waiting for transfers between devices  0.84 us (2%)
  other arithmetic  0.69 us (1%)
    all_to_all x1, blocking collectives, body(): lax.all_to_all(band.reshape(members, width // members, 3 * width), 'mem',...  16.1 us
    ppermute x4, starting transfers between devices, swapped(): return lax.ppermute(block, 'grp', pairs + [(b, a) for a, b in pairs])  7.27 us
    pallas_call x2, Pallas kernels, coupled(): pl.pallas_call(functools.partial(pair_kernel, odd_is_upper_group), in_spe...  4.16 us
    ppermute x1, starting transfers between devices, body(): before = lax.ppermute(send_up, 'mem', forward)  3.99 us
    pallas_call x1, Pallas kernels, body(): pl.pallas_call(functools.partial(prepare_kernel, rows), in_specs=[SCALAR]...  3.62 us
    pallas_call x1, Pallas kernels, body(): pl.pallas_call(send_kernel, in_specs=[anywhere] * 4, out_specs=[WHOLE] *...  3.52 us
    pallas_call x1, Pallas kernels, body(): pl.pallas_call(middle_kernel, in_specs=[SCALAR, WHOLE, WHOLE, pl.BlockSpe...  2.82 us
    pallas_call x1, Pallas kernels, body(): pl.pallas_call(functools.partial(half_kernel, rows), in_specs=[SCALAR, WH...  2.43 us
  transfers between devices with their start and end apart: 6, of which 1 were waited for; matrix products, arithmetic and copies ran while one was open for 0% of the time, Pallas kernels for 28%

profile of v4, /device:TPU:1, one launch (start us, length us, event | category | flops | bytes accessed | tf_op | source)
XLA Modules:
  0.0 47.0 jit_solution(3184719242398316222)
XLA Ops:
  0.0 0.0 copy-start.1
  0.0 3.5 %shard_map.46 = (bf16[4,64,2048]{2,1,0:T(8,128)(2,1)S(1)}, bf16[4,64,2048]{2,1,0:T(8,128)(2,1)S(1)}, bf16[2,2,4096]{2,1,0:T(2,128)(2,1)S(1)}, bf16[1,2,4096]{2,1...) custom-call(bf16[48,4096]{1,0:T(8,128)(2,1)} %occ_in.1, ...), custom_call_target="tpu_custom_call" | custom-call | tf_op jit(solution)/shard_map/pallas_call | solution.py:295
  3.5 0.1 collective-permute-start.3
  3.7 4.5 %collective-permute-start.2 = (bf16[4,64,2048]{2,1,0:T(8,128)(2,1)S(1)}, bf16[4,64,2048]{2,1,0:T(8,128)(2,1)S(1)}, u32[]{:S(2)}, u32[]{:S(2)}) collective-permute-start(bf16[4,64,2048]{2,1,0:T(8,128)(2,1)S(1)} %get-tuple-element.24.odd), channel_id=1, source_target_pairs={{8,16},{16,8},{9,17},{17,9},{10,18},{18,10},{11,19},{19,11},{12,20... | collective-permute-start | bytes 3145736 | tf_op jit(solution)/shard_map/ppermute | solution.py:266
  8.1 1.3 %collective-permute-start.1 = (bf16[1,2,4096]{2,1,0:T(2,128)(2,1)S(1)}, bf16[1,2,4096]{2,1,0:T(2,128)(2,1)S(1)}, u32[]{:S(2)}, u32[]{:S(2)}) collective-permute-start(bf16[1,2,4096]{2,1,0:T(2,128)(2,1)S(1)} %get-tuple-element.21), channel_id=1, source_target_pairs={{1,0},{2,1},{3,2},{4,3},{5,4},{6,5},{7,6},{9,8},{10,9},{11,10},{12... | collective-permute-start | bytes 49160 | tf_op jit(solution)/shard_map/ppermute | solution.py:333
  9.4 4.0 %collective-permute-start = (bf16[2,2,4096]{2,1,0:T(2,128)(2,1)S(1)}, bf16[2,2,4096]{2,1,0:T(2,128)(2,1)S(1)}, u32[]{:S(2)}, u32[]{:S(2)}) collective-permute-start(bf16[2,2,4096]{2,1,0:T(2,128)(2,1)S(1)} %get-tuple-element.18), channel_id=1, source_target_pairs={{0,1},{1,2},{2,3},{3,4},{4,5},{5,6},{6,7},{8,9},{9,10},{10,11},{11... | collective-permute-start | bytes 98312 | tf_op jit(solution)/shard_map/ppermute | solution.py:332
  13.4 0.0 copy-done.1
  13.4 0.0 copy-done
  13.4 2.4 %shard_map.47.half = bf16[4,64,4096]{2,1,0:T(8,128)(2,1)S(1)} custom-call(s32[4,4,4]{2,1,0:T(4,128)S(1)} %copy-done.1, bf16[2,2,32,64]{3,2,1,0:T(8,128)(2,1)S(1)} %get-tuple-element.22.green, bf16[1,4,64,4096]{3,2,1,0:T(8,128)(2,1)S(1)} %copy-done, bf16[4,64,2048]{2,1,0:T(8,128)(2,1)S(1)} %get-tuple-element.23.even, ...), custom_call_target="tpu_custom_call" | custom-call | flops 1610612736 | bytes 4194304 | tf_op jit(solution)/shard_map/pallas_call | solution.py:321
  15.9 0.0 collective-permute-done.1.after
  15.9 0.0 collective-permute-done.before
  15.9 3.6 %shard_map.48 = (bf16[768,4096]{1,0:T(8,128)(2,1)S(1)}, bf16[768,2048]{1,0:T(8,128)(2,1)S(1)}) custom-call(s32[4,4,4]{2,1,0:T(4,128)S(1)} %copy-done.1, bf16[2,2,4096]{2,1,0:T(2,128)(2,1)S(1)} %collective-permute-done.before, bf16[2,2,4096]{2,1,0:T(2,128)(2,1)S(1)} %get-tuple-element.19.near, bf16[3,2,4096]{2,1,0:T(2,128)(2,1)S(1)} %get-tuple-element.20.far, ...), custom_call_target="tpu_custom_call" | custom-call | flops 2415919104 | bytes 10485760 | tf_op jit(solution)/shard_map/pallas_call | solution.py:334
  19.5 0.0 collective-permute-done.3.other
  19.6 2.1 %shard_map.51 = (f32[256,256]{1,0:T(8,128)S(1)}, bf16[256,256]{1,0:T(8,128)(2,1)S(1)}) custom-call(s32[4,4,4]{2,1,0:T(4,128)S(1)} %copy-done.1, bf16[768,4096]{1,0:T(8,128)(2,1)S(1)} %get-tuple-element.25.y_all, bf16[768,2048]{1,0:T(8,128)(2,1)S(1)} %get-tuple-element.26.v_high, bf16[4,64,2048]{2,1,0:T(8,128)(2,1)S(1)} %collective-permute-done.3.other), custom_call_target="tpu_custom_call" | custom-call | flops 805306368 | bytes 8388608 | tf_op jit(solution)/shard_map/pallas_call | solution.py:352
  21.6 0.1 collective-permute-start.4
  21.7 0.0 collective-permute-done.2.other
  21.7 2.1 %shard_map.49 = (f32[256,256]{1,0:T(8,128)S(1)}, bf16[256,256]{1,0:T(8,128)(2,1)S(1)}) custom-call(s32[4,4,4]{2,1,0:T(4,128)S(1)} %copy-done.1, bf16[768,4096]{1,0:T(8,128)(2,1)S(1)} %get-tuple-element.25.y_all, bf16[768,2048]{1,0:T(8,128)(2,1)S(1)} %get-tuple-element.26.v_high, bf16[4,64,2048]{2,1,0:T(8,128)(2,1)S(1)} %collective-permute-done.2.other), custom_call_target="tpu_custom_call" | custom-call | flops 805306368 | bytes 8388608 | tf_op jit(solution)/shard_map/pallas_call | solution.py:352
  23.8 2.6 %collective-permute-start.5 = (bf16[256,256]{1,0:T(8,128)(2,1)S(1)}, bf16[256,256]{1,0:T(8,128)(2,1)S(1)}, u32[]{:S(2)}, u32[]{:S(2)}) collective-permute-start(bf16[256,256]{1,0:T(8,128)(2,1)S(1)} %get-tuple-element.27.after), channel_id=1, source_target_pairs={{8,16},{16,8},{9,17},{17,9},{10,18},{18,10},{11,19},{19,11},{12,20... | collective-permute-start | bytes 393224 | tf_op jit(solution)/shard_map/ppermute | solution.py:266
  26.4 2.8 %shard_map.50.middle = f32[256,256]{1,0:T(8,128)S(1)} custom-call(s32[4,4,4]{2,1,0:T(4,128)S(1)} %copy-done.1, bf16[768,4096]{1,0:T(8,128)(2,1)S(1)} %get-tuple-element.25.y_all, bf16[1,4,64,4096]{3,2,1,0:T(8,128)(2,1)S(1)} %copy-done, bf16[256,256]{1,0:T(8,128)(2,1)S(1)} %get-tuple-element.27.after), custom_call_target="tpu_custom_call" | custom-call | flops 1610612736 | bytes 8388608 | tf_op jit(solution)/shard_map/pallas_call | solution.py:366
  29.3 0.0 collective-permute-done.4.got_even
  29.3 0.8 %collective-permute-done.5.got_odd = bf16[256,256]{1,0:T(8,128)(2,1)S(1)} collective-permute-done((bf16[256,256]{1,0:T(8,128)(2,1)S(1)}, bf16[256,256]{1,0:T(8,128)(2,1)S(1)}, u32[]{:S(2)}, u32[]{:S(2)}) %collective-permute-start.5) | collective-permute-done | bytes 131104 | tf_op jit(solution)/shard_map/ppermute | solution.py:266
  30.1 0.1 shard_map.52
  30.2 16.1 %all_to_all.5 = bf16[8,32,768]{2,1,0:T(8,128)(2,1)S(1)} all-to-all(bf16[8,32,768]{2,1,0:T(8,128)(2,1)S(1)} %bitcast.1), channel_id=1, replica_groups=mesh['grp'=4,'mem'=8] {'mem'}, dimensions={0} | all-to-all | bytes 786432 | tf_op jit(solution)/shard_map/all_to_all | solution.py:382
  46.3 0.7 %convert_reduce_fusion = f32[32,768]{1,0:T(8,128)} fusion(bf16[8,32,768]{2,1,0:T(8,128)(2,1)S(1)} %all_to_all.5), kind=kLoop, calls=%fused_computation | loop fusion | flops 368640 | bytes 491520 | tf_op jit(solution)/shard_map/reduce_sum | solution.py:383
  (1 shorter events, 0.0 us)
Async XLA Ops:
  0.0 13.4 %copy-start.1 = (s32[4,4,4]{2,1,0:T(4,128)S(1)}, s32[4,4,4]{2,1,0:T(4,128)}, u32[]{:S(2)}) copy-start(s32[4,4,4]{2,1,0:T(4,128)} %ids.9) | copy-start | bytes 772
  0.0 13.4 %copy-start = (bf16[1,4,64,4096]{3,2,1,0:T(8,128)(2,1)S(1)}, bf16[1,4,64,4096]{3,2,1,0:T(8,128)(2,1)}, u32[]{:S(2)}) copy-start(bf16[1,4,64,4096]{3,2,1,0:T(8,128)(2,1)} %tiles.7) | copy-start | bytes 6291460
  3.5 16.0 %collective-permute-start.3 = (bf16[4,64,2048]{2,1,0:T(8,128)(2,1)S(1)}, bf16[4,64,2048]{2,1,0:T(8,128)(2,1)S(1)}, u32[]{:S(2)}, u32[]{:S(2)}) collective-permute-start(bf16[4,64,2048]{2,1,0:T(8,128)(2,1)S(1)} %get-tuple-element.23.even), channel_id=1, source_target_pairs={{0,8},{16,24},{8,0},{24,16},{1,9},{17,25},{9,1},{25,17},{2,10},{18... | collective-permute-start | bytes 3145736 | tf_op jit(solution)/shard_map/ppermute | solution.py:266
  3.7 18.1 %collective-permute-start.2 = (bf16[4,64,2048]{2,1,0:T(8,128)(2,1)S(1)}, bf16[4,64,2048]{2,1,0:T(8,128)(2,1)S(1)}, u32[]{:S(2)}, u32[]{:S(2)}) collective-permute-start(bf16[4,64,2048]{2,1,0:T(8,128)(2,1)S(1)} %get-tuple-element.24.odd), channel_id=1, source_target_pairs={{8,16},{16,8},{9,17},{17,9},{10,18},{18,10},{11,19},{19,11},{12,20... | collective-permute-start | bytes 3145736 | tf_op jit(solution)/shard_map/ppermute | solution.py:266
  8.1 7.8 %collective-permute-start.1 = (bf16[1,2,4096]{2,1,0:T(2,128)(2,1)S(1)}, bf16[1,2,4096]{2,1,0:T(2,128)(2,1)S(1)}, u32[]{:S(2)}, u32[]{:S(2)}) collective-permute-start(bf16[1,2,4096]{2,1,0:T(2,128)(2,1)S(1)} %get-tuple-element.21), channel_id=1, source_target_pairs={{1,0},{2,1},{3,2},{4,3},{5,4},{6,5},{7,6},{9,8},{10,9},{11,10},{12... | collective-permute-start | bytes 49160 | tf_op jit(solution)/shard_map/ppermute | solution.py:333
  9.4 6.5 %collective-permute-start = (bf16[2,2,4096]{2,1,0:T(2,128)(2,1)S(1)}, bf16[2,2,4096]{2,1,0:T(2,128)(2,1)S(1)}, u32[]{:S(2)}, u32[]{:S(2)}) collective-permute-start(bf16[2,2,4096]{2,1,0:T(2,128)(2,1)S(1)} %get-tuple-element.18), channel_id=1, source_target_pairs={{0,1},{1,2},{2,3},{3,4},{4,5},{5,6},{6,7},{8,9},{9,10},{10,11},{11... | collective-permute-start | bytes 98312 | tf_op jit(solution)/shard_map/ppermute | solution.py:332
  21.6 7.6 %collective-permute-start.4 = (bf16[256,256]{1,0:T(8,128)(2,1)S(1)}, bf16[256,256]{1,0:T(8,128)(2,1)S(1)}, u32[]{:S(2)}, u32[]{:S(2)}) collective-permute-start(bf16[256,256]{1,0:T(8,128)(2,1)S(1)} %get-tuple-element.30), channel_id=1, source_target_pairs={{0,8},{16,24},{8,0},{24,16},{1,9},{17,25},{9,1},{25,17},{2,10},{18... | collective-permute-start | bytes 393224 | tf_op jit(solution)/shard_map/ppermute | solution.py:266
  23.8 6.3 %collective-permute-start.5 = (bf16[256,256]{1,0:T(8,128)(2,1)S(1)}, bf16[256,256]{1,0:T(8,128)(2,1)S(1)}, u32[]{:S(2)}, u32[]{:S(2)}) collective-permute-start(bf16[256,256]{1,0:T(8,128)(2,1)S(1)} %get-tuple-element.27.after), channel_id=1, source_target_pairs={{8,16},{16,8},{9,17},{17,9},{10,18},{18,10},{11,19},{19,11},{12,20... | collective-permute-start | bytes 393224 | tf_op jit(solution)/shard_map/ppermute | solution.py:266

commit v5 on v4

--- a/solution.py
+++ b/solution.py
@@ -15,6 +15,10 @@
 
 def is_odd():
     return lax.rem(lax.axis_index("grp"), 2) == 1
+
+
+def sends_up():
+    return lax.rem(lax.axis_index("grp") + lax.axis_index("mem"), 2) == 0
 
 
 def go_rows(block, source, rows_in, rows_out, result):
@@ -41,7 +45,7 @@
 
 
 def send_kernel(
-    occ_in, ids_in, tiles, virt, even, odd, send_up, send_down, near, far, green, held,
+    occ_in, ids_in, tiles, virt, even, odd, send_row, near, far, green, held,
     occ, ids, rows_in, rows_out, sem
 ):
     slots, side, flat = held.shape
@@ -55,11 +59,11 @@
     fetch = [pltpu.make_async_copy(tiles.at[0, t], held.at[t], sem.at[t]) for t in range(slots)]
     for copy in fetch:
         copy.start()
-    up = pltpu.make_async_copy(virt.at[pl.ds(rows - 2, 2)], send_up, sem.at[slots])
-    down = pltpu.make_async_copy(virt.at[pl.ds(0, 1)], send_down, sem.at[slots + 1])
+    start = jnp.where(sends_up(), rows - 2, 0)
+    row_copy = pltpu.make_async_copy(virt.at[pl.ds(start, 2)], send_row, sem.at[slots])
     near_copy = pltpu.make_async_copy(virt.at[pl.ds(0, 2)], near, sem.at[slots + 4])
     far_copy = pltpu.make_async_copy(virt.at[pl.ds(rows - 3, 3)], far, sem.at[slots + 5])
-    edges = [up, down, near_copy, far_copy]
+    edges = [row_copy, near_copy, far_copy]
     for copy in edges:
         copy.start()
     group = lax.axis_index("grp")
@@ -159,7 +163,7 @@
 NN = (((1,), (0,)), ((), ()))
 
 
-def prepare_kernel(rows, ids, before, near, far, after, half, tiles, y_all, v_high, table, mats):
+def prepare_kernel(rows, ids, fetched, passed, near, far, half, tiles, y_all, v_high, table, mats):
     slots, side, flat = half.shape
     cut = flat - v_high.shape[1]
     group = lax.axis_index("grp")
@@ -170,11 +174,15 @@
     own = own == lax.broadcasted_iota(jnp.int32, (WIDE, WIDE), 1) // side
     own = own.astype(F32).astype(BF16)
 
-    at = 0
-    for source in (before, near, far, after):
-        for k in range(source.shape[0]):
-            table[at : at + 2, :] = source[k].astype(F32)
-            at += 2
+    from_above = sends_up()
+    for k in range(2):
+        one, two = fetched[k].astype(F32), passed[k].astype(F32)
+        table[2 * k : 2 * k + 2, :] = jnp.where(from_above, two, one)
+        table[2 * k + 4 : 2 * k + 6, :] = near[k].astype(F32)
+        if k == 0:
+            table[14:16, :] = jnp.where(from_above, one, two)
+    for k in range(3):
+        table[2 * k + 8 : 2 * k + 10, :] = far[k].astype(F32)
     lanes = 2 * side
     pairs = side // 2
     line_of = lax.broadcasted_iota(jnp.int32, (side, pairs), 0) // 2
@@ -292,15 +300,14 @@
     anywhere = pl.BlockSpec(memory_space=pltpu.HBM)
     pitch = side + 8
     strided = [pltpu.VMEM((flat // (2 * side) * pitch, 2 * side), F32)] * 2
-    even, odd, send_up, send_down, near, far, green = pl.pallas_call(
+    even, odd, send_row, near, far, green = pl.pallas_call(
         send_kernel,
         in_specs=[anywhere] * 4,
-        out_specs=[WHOLE] * 2 + [anywhere] * 4 + [WHOLE],
+        out_specs=[WHOLE] * 2 + [anywhere] * 3 + [WHOLE],
         out_shape=[
             jax.ShapeDtypeStruct((slots, side, cut), BF16),
             jax.ShapeDtypeStruct((slots, side, cut), BF16),
             jax.ShapeDtypeStruct((2, 2, flat), BF16),
-            jax.ShapeDtypeStruct((1, 2, flat), BF16),
             jax.ShapeDtypeStruct((2, 2, flat), BF16),
             jax.ShapeDtypeStruct((3, 2, flat), BF16),
             jax.ShapeDtypeStruct((2, 2, side // 2, side), BF16),
@@ -327,10 +334,26 @@
         compiler_params=params(12),
         cost_estimate=pl.CostEstimate(flops=2 * macs, bytes_accessed=4 * slots * side * flat, transcendentals=0),
     )(tile_ids, green, tiles, even, odd)
+    route = []
+    for g in range(lax.axis_size("grp")):
+        for m in range(g % 2, members - 1, 2):
+            a, b = g * members + m, g * members + m + 1
+            route += [(a, b), (b, a)]
+    fetched = lax.ppermute(send_row, ("grp", "mem"), route)
+    macs = slots * slots * 3 * side * side * flat
+    half = pl.pallas_call(
+        functools.partial(half_kernel, rows),
+        in_specs=[SCALAR, WHOLE, WHOLE] + [pl.BlockSpec(memory_space=pl.ANY)] * 2,
+        out_specs=WHOLE,
+        out_shape=pltpu.VMEM((slots, side, flat), BF16),
+        scratch_shapes=[*strided, pltpu.SemaphoreType.DMA((1,))],
+        compiler_params=params(12),
+        cost_estimate=pl.CostEstimate(flops=2 * macs, bytes_accessed=4 * slots * side * flat, transcendentals=0),
+    )(tile_ids, green, tiles, even, odd)
     forward = [(i, i + 1) for i in range(members - 1)]
     backward = [(b, a) for a, b in forward]
-    before = lax.ppermute(send_up, "mem", forward)
-    after = lax.ppermute(send_down, "mem", backward)
+    fetched, half = lax.optimization_barrier((fetched, half))
+    passed = swapped(fetched, 0)
     y_all, v_high = pl.pallas_call(
         functools.partial(prepare_kernel, rows),
         in_specs=[SCALAR] + [WHOLE] * 6,
@@ -342,7 +365,7 @@
         scratch_shapes=[pltpu.VMEM((16, flat), F32), pltpu.VMEM((slots * 3, WIDE, WIDE), BF16)],
         compiler_params=params(20),
         cost_estimate=pl.CostEstimate(flops=3 * macs, bytes_accessed=10 * slots * side * flat, transcendentals=0),
-    )(tile_ids, before, near, far, after, half, tiles)
+    )(tile_ids, fetched, passed, near, far, half, tiles)
     found = [
         pltpu.VMEM((RIB, side, slots * side), F32),
         pltpu.VMEM((slots * 3 * side, slots * side), F32),

time: 47.2 us -> 45.3 us (0.960)
  starting transfers between devices: 12.5 us -> 9.87 us
  waiting for transfers between devices: 0.84 us -> 2.63 us
  blocking collectives: 16.1 us -> 15.2 us
    ppermute x2 -> x1, starting transfers between devices: 5.28 us -> 0.66 us  [body(): fetched = lax.ppermute(send_row, ('grp', 'mem'), route)]
    ppermute x4 -> x5, starting transfers between devices: 7.27 us -> 9.21 us  [swapped(): return lax.ppermute(block, 'grp', pairs + [(b, a) for a, b in pairs])]
    ppermute x4 -> x5, waiting for transfers between devices: 0.84 us -> 2.63 us  [swapped(): return lax.ppermute(block, 'grp', pairs + [(b, a) for a, b in pairs])]
    all_to_all x1, blocking collectives: 16.1 us -> 15.2 us  [body(): lax.all_to_all(band.reshape(members, width // members, 3 * width), 'mem',...]
  transfers between devices with their start and end apart: 6 -> 6, of which waited for: 1 -> 2; matrix products, arithmetic and copies ran while one was open for 0% -> 0% of each run, Pallas kernels for 28% -> 29%
where the time goes in v5:
time: 45.3 us; the launch traced here: 45.1 us
  Pallas kernels  16.6 us (37%)
  blocking collectives  15.2 us (34%)
  starting transfers between devices  9.87 us (22%)
  waiting for transfers between devices  2.63 us (6%)
  other arithmetic  0.69 us (2%)
    all_to_all x1, blocking collectives, body(): lax.all_to_all(band.reshape(members, width // members, 3 * width), 'mem',...  15.2 us
    ppermute x5, starting transfers between devices, swapped(): return lax.ppermute(block, 'grp', pairs + [(b, a) for a, b in pairs])  9.21 us
    pallas_call x2, Pallas kernels, coupled(): pl.pallas_call(functools.partial(pair_kernel, odd_is_upper_group), in_spe...  4.16 us
    pallas_call x1, Pallas kernels, body(): pl.pallas_call(functools.partial(prepare_kernel, rows), in_specs=[SCALAR]...  3.62 us
    pallas_call x1, Pallas kernels, body(): pl.pallas_call(send_kernel, in_specs=[anywhere] * 4, out_specs=[WHOLE] *...  3.52 us
    pallas_call x1, Pallas kernels, body(): pl.pallas_call(middle_kernel, in_specs=[SCALAR, WHOLE, WHOLE, pl.BlockSpe...  2.82 us
    ppermute x5, waiting for transfers between devices, swapped(): return lax.ppermute(block, 'grp', pairs + [(b, a) for a, b in pairs])  2.63 us
    pallas_call x1, Pallas kernels, body(): pl.pallas_call(functools.partial(half_kernel, rows), in_specs=[SCALAR, WH...  2.44 us
  transfers between devices with their start and end apart: 6, of which 2 were waited for; matrix products, arithmetic and copies ran while one was open for 0% of the time, Pallas kernels for 29%

profile of v5, /device:TPU:1, one launch (start us, length us, event | category | flops | bytes accessed | tf_op | source)
XLA Modules:
  0.0 45.1 jit_solution(15866796209425898532)
XLA Ops:
  0.0 0.0 copy-start.1
  0.0 3.5 %shard_map.46 = (bf16[4,64,2048]{2,1,0:T(8,128)(2,1)S(1)}, bf16[4,64,2048]{2,1,0:T(8,128)(2,1)S(1)}, bf16[2,2,4096]{2,1,0:T(2,128)(2,1)S(1)}, bf16[2,2,4096]{2,1...) custom-call(bf16[48,4096]{1,0:T(8,128)(2,1)} %occ_in.1, s32[4,4,4]{2,1,0:T(4,128)} %ids.9, ...), custom_call_target="tpu_custom_call" | custom-call | tf_op jit(solution)/shard_map/pallas_call | solution.py:303
  3.5 0.1 collective-permute-start.3
  3.7 4.5 %collective-permute-start.2 = (bf16[4,64,2048]{2,1,0:T(8,128)(2,1)S(1)}, bf16[4,64,2048]{2,1,0:T(8,128)(2,1)S(1)}, u32[]{:S(2)}, u32[]{:S(2)}) collective-permute-start(bf16[4,64,2048]{2,1,0:T(8,128)(2,1)S(1)} %get-tuple-element.22.odd), channel_id=1, source_target_pairs={{8,16},{16,8},{9,17},{17,9},{10,18},{18,10},{11,19},{19,11},{12,20... | collective-permute-start | bytes 3145736 | tf_op jit(solution)/shard_map/ppermute | solution.py:274
  8.1 0.7 %collective-permute-start = (bf16[2,2,4096]{2,1,0:T(2,128)(2,1)S(1)}, bf16[2,2,4096]{2,1,0:T(2,128)(2,1)S(1)}, u32[]{:S(2)}, u32[]{:S(2)}) collective-permute-start(bf16[2,2,4096]{2,1,0:T(2,128)(2,1)S(1)} %get-tuple-element.19), channel_id=1, source_target_pairs={{0,1},{1,0},{2,3},{3,2},{4,5},{5,4},{6,7},{7,6},{9,10},{10,9},{11,... | collective-permute-start | bytes 98312 | tf_op jit(solution)/shard_map/ppermute | solution.py:342
  8.8 0.0 copy-done.1
  8.8 0.0 copy-done
  8.8 2.4 %shard_map.47.half = bf16[4,64,4096]{2,1,0:T(8,128)(2,1)S(1)} custom-call(s32[4,4,4]{2,1,0:T(4,128)S(1)} %copy-done.1, bf16[2,2,32,64]{3,2,1,0:T(8,128)(2,1)S(1)} %get-tuple-element.20.green, bf16[1,4,64,4096]{3,2,1,0:T(8,128)(2,1)S(1)} %copy-done, bf16[4,64,2048]{2,1,0:T(8,128)(2,1)S(1)} %get-tuple-element.21.even, ...), custom_call_target="tpu_custom_call" | custom-call | flops 1610612736 | bytes 4194304 | tf_op jit(solution)/shard_map/pallas_call | solution.py:344
  11.3 0.0 collective-permute-done.fetched
  11.3 0.6 %collective-permute-start.1 = (bf16[2,2,4096]{2,1,0:T(2,128)(2,1)S(1)}, bf16[2,2,4096]{2,1,0:T(2,128)(2,1)S(1)}, u32[]{:S(2)}, u32[]{:S(2)}) collective-permute-start(bf16[2,2,4096]{2,1,0:T(2,128)(2,1)S(1)} %collective-permute-done.fetched), channel_id=1, source_target_pairs={{0,8},{16,24},{8,0},{24,16},{1,9},{17,25},{9,1},{25,17},{2,10},{18... | collective-permute-start | bytes 98312 | tf_op jit(solution)/shard_map/ppermute | solution.py:274
  11.8 0.9 %collective-permute-done.1.passed = bf16[2,2,4096]{2,1,0:T(2,128)(2,1)S(1)} collective-permute-done((bf16[2,2,4096]{2,1,0:T(2,128)(2,1)S(1)}, bf16[2,2,4096]{2,1,0:T(2,128)(2,1)S(1)}, u32[]{:S(2)}, u32[]{:S(2)}) %collective-permute-start.1) | collective-permute-done | bytes 32800 | tf_op jit(solution)/shard_map/ppermute | solution.py:274
  12.7 3.6 %shard_map.48 = (bf16[768,4096]{1,0:T(8,128)(2,1)S(1)}, bf16[768,2048]{1,0:T(8,128)(2,1)S(1)}) custom-call(s32[4,4,4]{2,1,0:T(4,128)S(1)} %copy-done.1, bf16[2,2,4096]{2,1,0:T(2,128)(2,1)S(1)} %collective-permute-done.fetched, bf16[2,2,4096]{2,1,0:T(2,128)(2,1)S(1)} %collective-permute-done.1.passed, bf16[2,2,4096]{2,1,0:T(2,128)(2,1)S(1)} %get-tuple-element.24.near, ...), custom_call_target="tpu_custom_call" | custom-call | flops 2415919104 | bytes 10485760 | tf_op jit(solution)/shard_map/pallas_call | solution.py:357
  16.3 0.0 collective-permute-done.3.other
  16.3 2.1 %shard_map.51 = (f32[256,256]{1,0:T(8,128)S(1)}, bf16[256,256]{1,0:T(8,128)(2,1)S(1)}) custom-call(s32[4,4,4]{2,1,0:T(4,128)S(1)} %copy-done.1, bf16[768,4096]{1,0:T(8,128)(2,1)S(1)} %get-tuple-element.27.y_all, bf16[768,2048]{1,0:T(8,128)(2,1)S(1)} %get-tuple-element.28.v_high, bf16[4,64,2048]{2,1,0:T(8,128)(2,1)S(1)} %collective-permute-done.3.other), custom_call_target="tpu_custom_call" | custom-call | flops 805306368 | bytes 8388608 | tf_op jit(solution)/shard_map/pallas_call | solution.py:375
  18.4 0.4 collective-permute-start.4
  18.8 1.8 %collective-permute-done.2.other = bf16[4,64,2048]{2,1,0:T(8,128)(2,1)S(1)} collective-permute-done((bf16[4,64,2048]{2,1,0:T(8,128)(2,1)S(1)}, bf16[4,64,2048]{2,1,0:T(8,128)(2,1)S(1)}, u32[]{:S(2)}, u32[]{:S(2)}) %collective-permute-start.2) | collective-permute-done | bytes 1048608 | tf_op jit(solution)/shard_map/ppermute | solution.py:274
  20.6 2.1 %shard_map.49 = (f32[256,256]{1,0:T(8,128)S(1)}, bf16[256,256]{1,0:T(8,128)(2,1)S(1)}) custom-call(s32[4,4,4]{2,1,0:T(4,128)S(1)} %copy-done.1, bf16[768,4096]{1,0:T(8,128)(2,1)S(1)} %get-tuple-element.27.y_all, bf16[768,2048]{1,0:T(8,128)(2,1)S(1)} %get-tuple-element.28.v_high, bf16[4,64,2048]{2,1,0:T(8,128)(2,1)S(1)} %collective-permute-done.2.other), custom_call_target="tpu_custom_call" | custom-call | flops 805306368 | bytes 8388608 | tf_op jit(solution)/shard_map/pallas_call | solution.py:375
  22.7 3.6 %collective-permute-start.5 = (bf16[256,256]{1,0:T(8,128)(2,1)S(1)}, bf16[256,256]{1,0:T(8,128)(2,1)S(1)}, u32[]{:S(2)}, u32[]{:S(2)}) collective-permute-start(bf16[256,256]{1,0:T(8,128)(2,1)S(1)} %get-tuple-element.29.after), channel_id=1, source_target_pairs={{8,16},{16,8},{9,17},{17,9},{10,18},{18,10},{11,19},{19,11},{12,20... | collective-permute-start | bytes 393224 | tf_op jit(solution)/shard_map/ppermute | solution.py:274
  26.3 2.8 %shard_map.50.middle = f32[256,256]{1,0:T(8,128)S(1)} custom-call(s32[4,4,4]{2,1,0:T(4,128)S(1)} %copy-done.1, bf16[768,4096]{1,0:T(8,128)(2,1)S(1)} %get-tuple-element.27.y_all, bf16[1,4,64,4096]{3,2,1,0:T(8,128)(2,1)S(1)} %copy-done, bf16[256,256]{1,0:T(8,128)(2,1)S(1)} %get-tuple-element.29.after), custom_call_target="tpu_custom_call" | custom-call | flops 1610612736 | bytes 8388608 | tf_op jit(solution)/shard_map/pallas_call | solution.py:389
  29.2 0.0 collective-permute-done.4.got_even
  29.2 0.0 collective-permute-done.5.got_odd
  29.2 0.1 shard_map.52
  29.3 15.2 %all_to_all.5 = bf16[8,32,768]{2,1,0:T(8,128)(2,1)S(1)} all-to-all(bf16[8,32,768]{2,1,0:T(8,128)(2,1)S(1)} %bitcast.1), channel_id=1, replica_groups=mesh['grp'=4,'mem'=8] {'mem'}, dimensions={0} | all-to-all | bytes 786432 | tf_op jit(solution)/shard_map/all_to_all | solution.py:405
  44.4 0.7 %convert_reduce_fusion = f32[32,768]{1,0:T(8,128)} fusion(bf16[8,32,768]{2,1,0:T(8,128)(2,1)S(1)} %all_to_all.5), kind=kLoop, calls=%fused_computation | loop fusion | flops 368640 | bytes 491520 | tf_op jit(solution)/shard_map/reduce_sum | solution.py:406
  (1 shorter events, 0.0 us)
Async XLA Ops:
  0.0 8.8 %copy-start.1 = (s32[4,4,4]{2,1,0:T(4,128)S(1)}, s32[4,4,4]{2,1,0:T(4,128)}, u32[]{:S(2)}) copy-start(s32[4,4,4]{2,1,0:T(4,128)} %ids.9) | copy-start | bytes 772
  0.0 8.8 %copy-start = (bf16[1,4,64,4096]{3,2,1,0:T(8,128)(2,1)S(1)}, bf16[1,4,64,4096]{3,2,1,0:T(8,128)(2,1)}, u32[]{:S(2)}) copy-start(bf16[1,4,64,4096]{3,2,1,0:T(8,128)(2,1)} %tiles.7) | copy-start | bytes 6291460
  3.5 12.8 %collective-permute-start.3 = (bf16[4,64,2048]{2,1,0:T(8,128)(2,1)S(1)}, bf16[4,64,2048]{2,1,0:T(8,128)(2,1)S(1)}, u32[]{:S(2)}, u32[]{:S(2)}) collective-permute-start(bf16[4,64,2048]{2,1,0:T(8,128)(2,1)S(1)} %get-tuple-element.21.even), channel_id=1, source_target_pairs={{0,8},{16,24},{8,0},{24,16},{1,9},{17,25},{9,1},{25,17},{2,10},{18... | collective-permute-start | bytes 3145736 | tf_op jit(solution)/shard_map/ppermute | solution.py:274
  3.7 16.9 %collective-permute-start.2 = (bf16[4,64,2048]{2,1,0:T(8,128)(2,1)S(1)}, bf16[4,64,2048]{2,1,0:T(8,128)(2,1)S(1)}, u32[]{:S(2)}, u32[]{:S(2)}) collective-permute-start(bf16[4,64,2048]{2,1,0:T(8,128)(2,1)S(1)} %get-tuple-element.22.odd), channel_id=1, source_target_pairs={{8,16},{16,8},{9,17},{17,9},{10,18},{18,10},{11,19},{19,11},{12,20... | collective-permute-start | bytes 3145736 | tf_op jit(solution)/shard_map/ppermute | solution.py:274
  8.1 3.1 %collective-permute-start = (bf16[2,2,4096]{2,1,0:T(2,128)(2,1)S(1)}, bf16[2,2,4096]{2,1,0:T(2,128)(2,1)S(1)}, u32[]{:S(2)}, u32[]{:S(2)}) collective-permute-start(bf16[2,2,4096]{2,1,0:T(2,128)(2,1)S(1)} %get-tuple-element.19), channel_id=1, source_target_pairs={{0,1},{1,0},{2,3},{3,2},{4,5},{5,4},{6,7},{7,6},{9,10},{10,9},{11,... | collective-permute-start | bytes 98312 | tf_op jit(solution)/shard_map/ppermute | solution.py:342
  11.3 1.4 %collective-permute-start.1 = (bf16[2,2,4096]{2,1,0:T(2,128)(2,1)S(1)}, bf16[2,2,4096]{2,1,0:T(2,128)(2,1)S(1)}, u32[]{:S(2)}, u32[]{:S(2)}) collective-permute-start(bf16[2,2,4096]{2,1,0:T(2,128)(2,1)S(1)} %collective-permute-done.fetched), channel_id=1, source_target_pairs={{0,8},{16,24},{8,0},{24,16},{1,9},{17,25},{9,1},{25,17},{2,10},{18... | collective-permute-start | bytes 98312 | tf_op jit(solution)/shard_map/ppermute | solution.py:274
  18.4 10.7 %collective-permute-start.4 = (bf16[256,256]{1,0:T(8,128)(2,1)S(1)}, bf16[256,256]{1,0:T(8,128)(2,1)S(1)}, u32[]{:S(2)}, u32[]{:S(2)}) collective-permute-start(bf16[256,256]{1,0:T(8,128)(2,1)S(1)} %get-tuple-element.32), channel_id=1, source_target_pairs={{0,8},{16,24},{8,0},{24,16},{1,9},{17,25},{9,1},{25,17},{2,10},{18... | collective-permute-start | bytes 393224 | tf_op jit(solution)/shard_map/ppermute | solution.py:274
  22.7 6.5 %collective-permute-start.5 = (bf16[256,256]{1,0:T(8,128)(2,1)S(1)}, bf16[256,256]{1,0:T(8,128)(2,1)S(1)}, u32[]{:S(2)}, u32[]{:S(2)}) collective-permute-start(bf16[256,256]{1,0:T(8,128)(2,1)S(1)} %get-tuple-element.29.after), channel_id=1, source_target_pairs={{8,16},{16,8},{9,17},{17,9},{10,18},{18,10},{11,19},{19,11},{12,20... | collective-permute-start | bytes 393224 | tf_op jit(solution)/shard_map/ppermute | solution.py:274

commit v6 on v5

--- a/solution.py
+++ b/solution.py
@@ -125,7 +125,7 @@
     pltpu.make_async_copy(even, high_part, sem.at[0]).wait()
 
 
-def combined(products, slots, side, ids, left, right, left_on, right_on, total):
+def combined(products, slots, side, ids, left, right, total):
     width = slots * side
 
     def spread(values, owner):
@@ -135,12 +135,12 @@
         return out
 
     owner = lax.broadcasted_iota(jnp.int32, (1, width), 1) // side
-    live = [ids[right, 3, u] * right_on for u in range(slots)]
-    row_block = spread([jnp.where(live[u] > 0, ids[right, 1, u], -1) for u in range(slots)], owner)
+    live = [jnp.where(ids[right, 3, u] > 0, ids[right, 1, u], -1) for u in range(slots)]
+    row_block = spread(live, owner)
     col_block = spread([ids[right, 2, u] for u in range(slots)], owner)
     total[...] = jnp.zeros_like(total)
     for t in range(slots):
-        same = row_block == jnp.where(ids[left, 3, t] * left_on > 0, ids[left, 1, t], -2)
+        same = row_block == jnp.where(ids[left, 3, t] > 0, ids[left, 1, t], -2)
         term = jnp.zeros((side, width), F32)
         for j in range(3):
             at = (t * 3 + j) * side
@@ -229,7 +229,7 @@
     products[...] = lax.dot_general(
         y_all[...], tiles[0].reshape(slots * side, flat), NT, preferred_element_type=F32
     )
-    middle[...] = combined(products, slots, side, ids, group, group, 1, 1, total)
+    middle[...] = combined(products, slots, side, ids, group, group, total)
 
 
 def pair_kernel(odd_is_upper_group, ids, y_all, v_high, other, part, send, total, products):
@@ -239,23 +239,27 @@
     odd_one = is_odd()
     below = odd_one if odd_is_upper_group else jnp.logical_not(odd_one)
     right = jnp.where(below, jnp.maximum(group - 1, 0), jnp.minimum(group + 1, last))
-    right_on = jnp.where(below, group > 0, group < last).astype(jnp.int32)
-
-    @pl.when(below)
-    def _():
-        products[...] = lax.dot_general(
-            y_all[:, :cut], other[...].reshape(slots * side, cut), NT, preferred_element_type=F32
-        )
-
-    @pl.when(jnp.logical_not(below))
-    def _():
-        products[...] = lax.dot_general(
-            v_high[...], other[...].reshape(slots * side, cut), NT, preferred_element_type=F32
-        )
-
-    mine = combined(products, slots, side, ids, group, right, 1, right_on, total)
-    part[...] = mine
-    send[...] = mine.T.astype(BF16)
+    exists = jnp.where(below, group, last - group) > 0
+    partner = other[...].reshape(slots * side, cut)
+
+    @pl.when(exists & below)
+    def _():
+        products[...] = lax.dot_general(y_all[:, :cut], partner, NT, preferred_element_type=F32)
+
+    @pl.when(exists & jnp.logical_not(below))
+    def _():
+        products[...] = lax.dot_general(v_high[...], partner, NT, preferred_element_type=F32)
+
+    @pl.when(exists)
+    def _():
+        mine = combined(products, slots, side, ids, group, right, total)
+        part[...] = mine
+        send[...] = mine.T.astype(BF16)
+
+    @pl.when(jnp.logical_not(exists))
+    def _():
+        part[...] = jnp.zeros_like(part)
+        send[...] = jnp.zeros_like(send)
 
 
 def band_kernel(middle, even, odd, got_even, got_odd, band):

time: 45.3 us -> 44.3 us (0.978)
  blocking collectives: 15.2 us -> 14.1 us
    all_to_all x1, blocking collectives: 15.2 us -> 14.1 us  [body(): lax.all_to_all(band.reshape(members, width // members, 3 * width), 'mem',...]
  transfers between devices with their start and end apart: 6 -> 6, of which waited for: 2 -> 2; matrix products, arithmetic and copies ran while one was open for 0% -> 0% of each run, Pallas kernels for 29% -> 30%
where the time goes in v6:
time: 44.3 us; the launch traced here: 44.1 us
  Pallas kernels  16.7 us (38%)
  blocking collectives  14.1 us (32%)
  starting transfers between devices  9.87 us (22%)
  waiting for transfers between devices  2.58 us (6%)
  other arithmetic  0.69 us (2%)
    all_to_all x1, blocking collectives, body(): lax.all_to_all(band.reshape(members, width // members, 3 * width), 'mem',...  14.1 us
    ppermute x5, starting transfers between devices, swapped(): return lax.ppermute(block, 'grp', pairs + [(b, a) for a, b in pairs])  9.2 us
    pallas_call x2, Pallas kernels, coupled(): pl.pallas_call(functools.partial(pair_kernel, odd_is_upper_group), in_spe...  4.26 us
    pallas_call x1, Pallas kernels, body(): pl.pallas_call(functools.partial(prepare_kernel, rows), in_specs=[SCALAR]...  3.62 us
    pallas_call x1, Pallas kernels, body(): pl.pallas_call(send_kernel, in_specs=[anywhere] * 4, out_specs=[WHOLE] *...  3.52 us
    pallas_call x1, Pallas kernels, body(): pl.pallas_call(middle_kernel, in_specs=[SCALAR, WHOLE, WHOLE, pl.BlockSpe...  2.82 us
    ppermute x5, waiting for transfers between devices, swapped(): return lax.ppermute(block, 'grp', pairs + [(b, a) for a, b in pairs])  2.57 us
    pallas_call x1, Pallas kernels, body(): pl.pallas_call(functools.partial(half_kernel, rows), in_specs=[SCALAR, WH...  2.44 us
  transfers between devices with their start and end apart: 6, of which 2 were waited for; matrix products, arithmetic and copies ran while one was open for 0% of the time, Pallas kernels for 30%

profile of v6, /device:TPU:1, one launch (start us, length us, event | category | flops | bytes accessed | tf_op | source)
XLA Modules:
  0.0 44.1 jit_solution(1663201429853041742)
XLA Ops:
  0.0 0.0 copy-start
  0.0 3.5 %shard_map.46 = (bf16[4,64,2048]{2,1,0:T(8,128)(2,1)S(1)}, bf16[4,64,2048]{2,1,0:T(8,128)(2,1)S(1)}, bf16[2,2,4096]{2,1,0:T(2,128)(2,1)S(1)}, bf16[2,2,4096]{2,1...) custom-call(bf16[48,4096]{1,0:T(8,128)(2,1)} %occ_in.1, s32[4,4,4]{2,1,0:T(4,128)} %ids.9, ...), custom_call_target="tpu_custom_call" | custom-call | tf_op jit(solution)/shard_map/pallas_call | solution.py:307
  3.5 0.1 collective-permute-start.3
  3.7 4.5 %collective-permute-start.2 = (bf16[4,64,2048]{2,1,0:T(8,128)(2,1)S(1)}, bf16[4,64,2048]{2,1,0:T(8,128)(2,1)S(1)}, u32[]{:S(2)}, u32[]{:S(2)}) collective-permute-start(bf16[4,64,2048]{2,1,0:T(8,128)(2,1)S(1)} %get-tuple-element.22.odd), channel_id=1, source_target_pairs={{8,16},{16,8},{9,17},{17,9},{10,18},{18,10},{11,19},{19,11},{12,20... | collective-permute-start | bytes 3145736 | tf_op jit(solution)/shard_map/ppermute | solution.py:278
  8.1 0.7 %collective-permute-start = (bf16[2,2,4096]{2,1,0:T(2,128)(2,1)S(1)}, bf16[2,2,4096]{2,1,0:T(2,128)(2,1)S(1)}, u32[]{:S(2)}, u32[]{:S(2)}) collective-permute-start(bf16[2,2,4096]{2,1,0:T(2,128)(2,1)S(1)} %get-tuple-element.19), channel_id=1, source_target_pairs={{0,1},{1,0},{2,3},{3,2},{4,5},{5,4},{6,7},{7,6},{9,10},{10,9},{11,... | collective-permute-start | bytes 98312 | tf_op jit(solution)/shard_map/ppermute | solution.py:346
  8.8 0.0 copy-done.1
  8.8 0.0 copy-done
  8.8 2.4 %shard_map.47.half = bf16[4,64,4096]{2,1,0:T(8,128)(2,1)S(1)} custom-call(s32[4,4,4]{2,1,0:T(4,128)S(1)} %copy-done.1, bf16[2,2,32,64]{3,2,1,0:T(8,128)(2,1)S(1)} %get-tuple-element.20.green, bf16[1,4,64,4096]{3,2,1,0:T(8,128)(2,1)S(1)} %copy-done, bf16[4,64,2048]{2,1,0:T(8,128)(2,1)S(1)} %get-tuple-element.21.even, ...), custom_call_target="tpu_custom_call" | custom-call | flops 1610612736 | bytes 4194304 | tf_op jit(solution)/shard_map/pallas_call | solution.py:348
  11.3 0.0 collective-permute-done.fetched
  11.3 0.6 %collective-permute-start.1 = (bf16[2,2,4096]{2,1,0:T(2,128)(2,1)S(1)}, bf16[2,2,4096]{2,1,0:T(2,128)(2,1)S(1)}, u32[]{:S(2)}, u32[]{:S(2)}) collective-permute-start(bf16[2,2,4096]{2,1,0:T(2,128)(2,1)S(1)} %collective-permute-done.fetched), channel_id=1, source_target_pairs={{0,8},{16,24},{8,0},{24,16},{1,9},{17,25},{9,1},{25,17},{2,10},{18... | collective-permute-start | bytes 98312 | tf_op jit(solution)/shard_map/ppermute | solution.py:278
  11.8 0.9 %collective-permute-done.1.passed = bf16[2,2,4096]{2,1,0:T(2,128)(2,1)S(1)} collective-permute-done((bf16[2,2,4096]{2,1,0:T(2,128)(2,1)S(1)}, bf16[2,2,4096]{2,1,0:T(2,128)(2,1)S(1)}, u32[]{:S(2)}, u32[]{:S(2)}) %collective-permute-start.1) | collective-permute-done | bytes 32800 | tf_op jit(solution)/shard_map/ppermute | solution.py:278
  12.7 3.6 %shard_map.48 = (bf16[768,4096]{1,0:T(8,128)(2,1)S(1)}, bf16[768,2048]{1,0:T(8,128)(2,1)S(1)}) custom-call(s32[4,4,4]{2,1,0:T(4,128)S(1)} %copy-done.1, bf16[2,2,4096]{2,1,0:T(2,128)(2,1)S(1)} %collective-permute-done.fetched, bf16[2,2,4096]{2,1,0:T(2,128)(2,1)S(1)} %collective-permute-done.1.passed, bf16[2,2,4096]{2,1,0:T(2,128)(2,1)S(1)} %get-tuple-element.24.near, ...), custom_call_target="tpu_custom_call" | custom-call | flops 2415919104 | bytes 10485760 | tf_op jit(solution)/shard_map/pallas_call | solution.py:361
  16.3 0.0 collective-permute-done.3.other
  16.3 2.1 %shard_map.51 = (f32[256,256]{1,0:T(8,128)S(1)}, bf16[256,256]{1,0:T(8,128)(2,1)S(1)}) custom-call(s32[4,4,4]{2,1,0:T(4,128)S(1)} %copy-done.1, bf16[768,4096]{1,0:T(8,128)(2,1)S(1)} %get-tuple-element.27.y_all, bf16[768,2048]{1,0:T(8,128)(2,1)S(1)} %get-tuple-element.28.v_high, bf16[4,64,2048]{2,1,0:T(8,128)(2,1)S(1)} %collective-permute-done.3.other), custom_call_target="tpu_custom_call" | custom-call | flops 805306368 | bytes 8388608 | tf_op jit(solution)/shard_map/pallas_call | solution.py:379
  18.5 0.4 collective-permute-start.4
  18.9 1.7 %collective-permute-done.2.other = bf16[4,64,2048]{2,1,0:T(8,128)(2,1)S(1)} collective-permute-done((bf16[4,64,2048]{2,1,0:T(8,128)(2,1)S(1)}, bf16[4,64,2048]{2,1,0:T(8,128)(2,1)S(1)}, u32[]{:S(2)}, u32[]{:S(2)}) %collective-permute-start.2) | collective-permute-done | bytes 1048608 | tf_op jit(solution)/shard_map/ppermute | solution.py:278
  20.6 2.1 %shard_map.49 = (f32[256,256]{1,0:T(8,128)S(1)}, bf16[256,256]{1,0:T(8,128)(2,1)S(1)}) custom-call(s32[4,4,4]{2,1,0:T(4,128)S(1)} %copy-done.1, bf16[768,4096]{1,0:T(8,128)(2,1)S(1)} %get-tuple-element.27.y_all, bf16[768,2048]{1,0:T(8,128)(2,1)S(1)} %get-tuple-element.28.v_high, bf16[4,64,2048]{2,1,0:T(8,128)(2,1)S(1)} %collective-permute-done.2.other), custom_call_target="tpu_custom_call" | custom-call | flops 805306368 | bytes 8388608 | tf_op jit(solution)/shard_map/pallas_call | solution.py:379
  22.7 3.6 %collective-permute-start.5 = (bf16[256,256]{1,0:T(8,128)(2,1)S(1)}, bf16[256,256]{1,0:T(8,128)(2,1)S(1)}, u32[]{:S(2)}, u32[]{:S(2)}) collective-permute-start(bf16[256,256]{1,0:T(8,128)(2,1)S(1)} %get-tuple-element.29.after), channel_id=1, source_target_pairs={{8,16},{16,8},{9,17},{17,9},{10,18},{18,10},{11,19},{19,11},{12,20... | collective-permute-start | bytes 393224 | tf_op jit(solution)/shard_map/ppermute | solution.py:278
  26.4 2.8 %shard_map.50.middle = f32[256,256]{1,0:T(8,128)S(1)} custom-call(s32[4,4,4]{2,1,0:T(4,128)S(1)} %copy-done.1, bf16[768,4096]{1,0:T(8,128)(2,1)S(1)} %get-tuple-element.27.y_all, bf16[1,4,64,4096]{3,2,1,0:T(8,128)(2,1)S(1)} %copy-done, bf16[256,256]{1,0:T(8,128)(2,1)S(1)} %get-tuple-element.29.after), custom_call_target="tpu_custom_call" | custom-call | flops 1610612736 | bytes 8388608 | tf_op jit(solution)/shard_map/pallas_call | solution.py:393
  29.2 0.0 collective-permute-done.4.got_even
  29.2 0.0 collective-permute-done.5.got_odd
  29.2 0.1 shard_map.52
  29.3 14.1 %all_to_all.5 = bf16[8,32,768]{2,1,0:T(8,128)(2,1)S(1)} all-to-all(bf16[8,32,768]{2,1,0:T(8,128)(2,1)S(1)} %bitcast.1), channel_id=1, replica_groups=mesh['grp'=4,'mem'=8] {'mem'}, dimensions={0} | all-to-all | bytes 786432 | tf_op jit(solution)/shard_map/all_to_all | solution.py:409
  43.4 0.7 %convert_reduce_fusion = f32[32,768]{1,0:T(8,128)} fusion(bf16[8,32,768]{2,1,0:T(8,128)(2,1)S(1)} %all_to_all.5), kind=kLoop, calls=%fused_computation | loop fusion | flops 368640 | bytes 491520 | tf_op jit(solution)/shard_map/reduce_sum | solution.py:410
  (1 shorter events, 0.0 us)
Async XLA Ops:
  0.0 8.8 %copy-start.1 = (s32[4,4,4]{2,1,0:T(4,128)S(1)}, s32[4,4,4]{2,1,0:T(4,128)}, u32[]{:S(2)}) copy-start(s32[4,4,4]{2,1,0:T(4,128)} %ids.9) | copy-start | bytes 772
  0.0 8.8 %copy-start = (bf16[1,4,64,4096]{3,2,1,0:T(8,128)(2,1)S(1)}, bf16[1,4,64,4096]{3,2,1,0:T(8,128)(2,1)}, u32[]{:S(2)}) copy-start(bf16[1,4,64,4096]{3,2,1,0:T(8,128)(2,1)} %tiles.7) | copy-start | bytes 6291460
  3.5 12.8 %collective-permute-start.3 = (bf16[4,64,2048]{2,1,0:T(8,128)(2,1)S(1)}, bf16[4,64,2048]{2,1,0:T(8,128)(2,1)S(1)}, u32[]{:S(2)}, u32[]{:S(2)}) collective-permute-start(bf16[4,64,2048]{2,1,0:T(8,128)(2,1)S(1)} %get-tuple-element.21.even), channel_id=1, source_target_pairs={{0,8},{16,24},{8,0},{24,16},{1,9},{17,25},{9,1},{25,17},{2,10},{18... | collective-permute-start | bytes 3145736 | tf_op jit(solution)/shard_map/ppermute | solution.py:278
  3.7 16.9 %collective-permute-start.2 = (bf16[4,64,2048]{2,1,0:T(8,128)(2,1)S(1)}, bf16[4,64,2048]{2,1,0:T(8,128)(2,1)S(1)}, u32[]{:S(2)}, u32[]{:S(2)}) collective-permute-start(bf16[4,64,2048]{2,1,0:T(8,128)(2,1)S(1)} %get-tuple-element.22.odd), channel_id=1, source_target_pairs={{8,16},{16,8},{9,17},{17,9},{10,18},{18,10},{11,19},{19,11},{12,20... | collective-permute-start | bytes 3145736 | tf_op jit(solution)/shard_map/ppermute | solution.py:278
  8.1 3.1 %collective-permute-start = (bf16[2,2,4096]{2,1,0:T(2,128)(2,1)S(1)}, bf16[2,2,4096]{2,1,0:T(2,128)(2,1)S(1)}, u32[]{:S(2)}, u32[]{:S(2)}) collective-permute-start(bf16[2,2,4096]{2,1,0:T(2,128)(2,1)S(1)} %get-tuple-element.19), channel_id=1, source_target_pairs={{0,1},{1,0},{2,3},{3,2},{4,5},{5,4},{6,7},{7,6},{9,10},{10,9},{11,... | collective-permute-start | bytes 98312 | tf_op jit(solution)/shard_map/ppermute | solution.py:346
  11.3 1.4 %collective-permute-start.1 = (bf16[2,2,4096]{2,1,0:T(2,128)(2,1)S(1)}, bf16[2,2,4096]{2,1,0:T(2,128)(2,1)S(1)}, u32[]{:S(2)}, u32[]{:S(2)}) collective-permute-start(bf16[2,2,4096]{2,1,0:T(2,128)(2,1)S(1)} %collective-permute-done.fetched), channel_id=1, source_target_pairs={{0,8},{16,24},{8,0},{24,16},{1,9},{17,25},{9,1},{25,17},{2,10},{18... | collective-permute-start | bytes 98312 | tf_op jit(solution)/shard_map/ppermute | solution.py:278
  18.5 10.7 %collective-permute-start.4 = (bf16[256,256]{1,0:T(8,128)(2,1)S(1)}, bf16[256,256]{1,0:T(8,128)(2,1)S(1)}, u32[]{:S(2)}, u32[]{:S(2)}) collective-permute-start(bf16[256,256]{1,0:T(8,128)(2,1)S(1)} %get-tuple-element.32), channel_id=1, source_target_pairs={{0,8},{16,24},{8,0},{24,16},{1,9},{17,25},{9,1},{25,17},{2,10},{18... | collective-permute-start | bytes 393224 | tf_op jit(solution)/shard_map/ppermute | solution.py:278
  22.7 6.5 %collective-permute-start.5 = (bf16[256,256]{1,0:T(8,128)(2,1)S(1)}, bf16[256,256]{1,0:T(8,128)(2,1)S(1)}, u32[]{:S(2)}, u32[]{:S(2)}) collective-permute-start(bf16[256,256]{1,0:T(8,128)(2,1)S(1)} %get-tuple-element.29.after), channel_id=1, source_target_pairs={{8,16},{16,8},{9,17},{17,9},{10,18},{18,10},{11,19},{19,11},{12,20... | collective-permute-start | bytes 393224 | tf_op jit(solution)/shard_map/ppermute | solution.py:278

commit v7 on v6

--- a/solution.py
+++ b/solution.py
@@ -45,8 +45,8 @@
 
 
 def send_kernel(
-    occ_in, ids_in, tiles, virt, even, odd, send_row, near, far, green, held,
-    occ, ids, rows_in, rows_out, sem
+    occ_in, ids_in, tiles, virt, even, odd, send_row, near, far, lows, held,
+    occ, ids, green, rows_in, rows_out, sem
 ):
     slots, side, flat = held.shape
     lanes, cut = 2 * side, even.shape[2]
@@ -88,7 +88,9 @@
     ids_copy.wait()
     for t in range(slots):
         fetch[t].wait()
-        block = green[(ids[group, 1, t] != first).astype(jnp.int32), 1]
+        end = (ids[group, 1, t] != first).astype(jnp.int32)
+        lows[t] = green[end, 0]
+        block = green[end, 1]
 
         def result(at, done):
             raw = held[t, :, at]
@@ -100,11 +102,11 @@
         copy.wait()
 
 
-def half_kernel(rows, ids, green, tiles, even, odd, half, rows_in, rows_out, sem):
+def half_kernel(rows, ids_in, lows, tiles, even, odd, half, pick, masks, left, place, ids, rows_in, rows_out, sem):
     slots, side, flat = half.shape
     cut = even.shape[2]
-    group = lax.axis_index("grp")
-    first = lax.axis_index("mem") * rows
+    ids_copy = pltpu.make_async_copy(ids_in, ids, sem.at[1])
+    ids_copy.start()
     high_part = half.at[:, :, pl.ds(cut, flat - cut)]
 
     @pl.when(is_odd())
@@ -116,46 +118,85 @@
         pltpu.make_async_copy(odd, high_part, sem.at[0]).start()
 
     for t in range(slots):
-        block = green[(ids[group, 1, t] != first).astype(jnp.int32), 0]
 
         def result(at, done):
             half[t, :, at] = done
 
-        go_rows(block, tiles.at[0, t], rows_in, rows_out, result)
+        go_rows(lows[t], tiles.at[t], rows_in, rows_out, result)
+    ids_copy.wait()
+    choose(rows, ids, slots, side, pick, masks, left, place)
     pltpu.make_async_copy(even, high_part, sem.at[0]).wait()
 
 
-def combined(products, slots, side, ids, left, right, total):
+def choose(rows, ids, slots, side, pick, masks, left, place):
     width = slots * side
-
-    def spread(values, owner):
+    group = lax.axis_index("grp")
+    last = lax.axis_size("grp") - 1
+    first = lax.axis_index("mem") * rows
+    count = rows * lax.axis_size("mem")
+
+    def stacked(lines, size):
+        lines = lines + [jnp.zeros_like(lines[0])] * (size - len(lines))
+        return jnp.concatenate(lines, axis=0)
+
+    line = lax.broadcasted_iota(jnp.int32, (1, pick.shape[1]), 1)
+    wanted = []
+    for t in range(slots):
+        a, b = ids[group, 1, t], ids[group, 2, t]
+        at = 2 * (jnp.where(a == first, 2, 6) + b - a)
+        wanted += [at - 1, at, jnp.where(b + 1 < count, at + 1, -1)]
+    pick[...] = stacked([(line == w).astype(F32) for w in wanted], pick.shape[0]).astype(BF16)
+
+    def spread(values):
         out = jnp.full(owner.shape, values[0], jnp.int32)
         for u in range(1, slots):
             out = jnp.where(owner == u, values[u], out)
         return out
 
     owner = lax.broadcasted_iota(jnp.int32, (1, width), 1) // side
-    live = [jnp.where(ids[right, 3, u] > 0, ids[right, 1, u], -1) for u in range(slots)]
-    row_block = spread(live, owner)
-    col_block = spread([ids[right, 2, u] for u in range(slots)], owner)
-    total[...] = jnp.zeros_like(total)
-    for t in range(slots):
-        same = row_block == jnp.where(ids[left, 3, t] > 0, ids[left, 1, t], -2)
-        term = jnp.zeros((side, width), F32)
-        for j in range(3):
-            at = (t * 3 + j) * side
-            match = (same & (col_block == ids[left, 2, t] + (j - 1))).astype(F32)
-            term = term + products[at : at + side, :] * match
-        total[ids[left, 0, t]] += term
     ahead = lax.broadcasted_iota(jnp.int32, (side, RIB * side), 1)
     ahead = ahead - lax.broadcasted_iota(jnp.int32, (side, RIB * side), 0)
-    place = [(ahead == ids[right, 0, u] * side).astype(F32).astype(BF16) for u in range(slots)]
-    place = jnp.concatenate(place, axis=0)
-    summed = total[...].reshape(RIB * side, width)
+    step = jnp.where(is_odd(), -1, 1)
+    for k, right in enumerate((group, group + step, group - step)):
+        right = jnp.clip(right, 0, last)
+        row_block = spread([jnp.where(ids[right, 3, u] > 0, ids[right, 1, u], -1) for u in range(slots)])
+        col_block = spread([ids[right, 2, u] for u in range(slots)])
+        lines = []
+        for t in range(slots):
+            same = row_block == jnp.where(ids[group, 3, t] > 0, ids[group, 1, t], -2)
+            for j in range(3):
+                lines.append((same & (col_block == ids[group, 2, t] + (j - 1))).astype(F32))
+        masks[k] = stacked(lines, masks.shape[1])
+        for u in range(slots):
+            place[k, u * side : (u + 1) * side, :] = (ahead == ids[right, 0, u] * side).astype(F32).astype(BF16)
+    lines = []
+    for p in range(RIB):
+        for t in range(slots):
+            lines.append(jnp.full((1, width), (ids[group, 0, t] == p).astype(F32), F32))
+    left[...] = stacked(lines, left.shape[0])
+
+
+def combined(products, slots, side, k, masks, left, place):
+    terms = []
+    for t in range(slots):
+        term = None
+        for j in range(3):
+            at = t * 3 + j
+            block = products[at * side : (at + 1) * side, :] * masks[k, at : at + 1, :]
+            term = block if term is None else term + block
+        terms.append(term)
+    lines = []
+    for p in range(RIB):
+        line = None
+        for t in range(slots):
+            block = terms[t] * left[p * slots + t : p * slots + t + 1, :]
+            line = block if line is None else line + block
+        lines.append(line)
+    summed = jnp.concatenate(lines, axis=0)
     coarse = summed.astype(BF16)
     fine = (summed - coarse.astype(F32)).astype(BF16)
-    return jnp.dot(coarse, place, preferred_element_type=F32) + jnp.dot(
-        fine, place, preferred_element_type=F32
+    return jnp.dot(coarse, place[k], preferred_element_type=F32) + jnp.dot(
+        fine, place[k], preferred_element_type=F32
     )
 
 
@@ -163,12 +204,9 @@
 NN = (((1,), (0,)), ((), ()))
 
 
-def prepare_kernel(rows, ids, fetched, passed, near, far, half, tiles, y_all, v_high, table, mats):
+def prepare_kernel(pick, fetched, passed, near, far, half, tiles, y_all, v_high, table, mats):
     slots, side, flat = half.shape
     cut = flat - v_high.shape[1]
-    group = lax.axis_index("grp")
-    first = lax.axis_index("mem") * rows
-    count = rows * lax.axis_size("mem")
     copies = WIDE // side
     own = lax.broadcasted_iota(jnp.int32, (WIDE, WIDE), 0) // side
     own = own == lax.broadcasted_iota(jnp.int32, (WIDE, WIDE), 1) // side
@@ -190,23 +228,18 @@
     even_row = lax.rem(lax.broadcasted_iota(jnp.int32, (side, lanes), 0), 2) == 0
     straight = even_row == (lax.broadcasted_iota(jnp.int32, (side, lanes), 1) < side)
 
-    def spread(row, keep=None):
-        line = table[pl.ds(row, 1), :]
-        if keep is not None:
-            line = line * keep
+    table[...] = jnp.dot(pick[...], table[...].astype(BF16), preferred_element_type=F32)
+
+    def spread(row):
+        line = table[row : row + 1, :]
         block = jnp.concatenate([line[:, h * lanes : (h + 1) * lanes] for h in range(pairs)], axis=0)
         block = jnp.dot(line_of, block.astype(BF16), preferred_element_type=F32)
         block = jnp.where(straight, block, pltpu.roll(block, side, 1)).astype(BF16)
         row = jnp.concatenate([block] * (copies // 2), axis=1)
         return jnp.concatenate([row] * copies, axis=0) * own
 
-    for t in range(slots):
-        a, b = ids[group, 1, t], ids[group, 2, t]
-        at = jnp.where(a == first, 2, 6) + b - a
-        keep = (b + 1 < count).astype(F32)
-        mats[t * 3] = spread(2 * at - 1)
-        mats[t * 3 + 1] = spread(2 * at)
-        mats[t * 3 + 2] = spread(2 * at + 1, keep)
+    for k in range(slots * 3):
+        mats[k] = spread(k)
 
     def transform(source, low, result, dims):
         lanes = result.shape[1]
@@ -220,25 +253,23 @@
                     result[at, k * WIDE : (k + 1) * WIDE] = y[k * side : (k + 1) * side]
 
     transform(half, 0, y_all, (NT, NN, NN))
-    transform(tiles.at[0], cut, v_high, (NT, NT, NN))
-
-
-def middle_kernel(ids, y_all, tiles, after, middle, total, products):
-    slots, side, flat = tiles.shape[1:]
-    group = lax.axis_index("grp")
+    transform(tiles, cut, v_high, (NT, NT, NN))
+
+
+def middle_kernel(masks, left, place, y_all, tiles, after, middle, products):
+    slots, side, flat = tiles.shape
     products[...] = lax.dot_general(
-        y_all[...], tiles[0].reshape(slots * side, flat), NT, preferred_element_type=F32
+        y_all[...], tiles[...].reshape(slots * side, flat), NT, preferred_element_type=F32
     )
-    middle[...] = combined(products, slots, side, ids, group, group, total)
-
-
-def pair_kernel(odd_is_upper_group, ids, y_all, v_high, other, part, send, total, products):
+    middle[...] = combined(products, slots, side, 0, masks, left, place)
+
+
+def pair_kernel(odd_is_upper_group, masks, left, place, y_all, v_high, other, part, send, products):
     slots, side, cut = other.shape
     group = lax.axis_index("grp")
     last = lax.axis_size("grp") - 1
     odd_one = is_odd()
     below = odd_one if odd_is_upper_group else jnp.logical_not(odd_one)
-    right = jnp.where(below, jnp.maximum(group - 1, 0), jnp.minimum(group + 1, last))
     exists = jnp.where(below, group, last - group) > 0
     partner = other[...].reshape(slots * side, cut)
 
@@ -252,7 +283,7 @@
 
     @pl.when(exists)
     def _():
-        mine = combined(products, slots, side, ids, group, right, total)
+        mine = combined(products, slots, side, 1 if odd_is_upper_group else 2, masks, left, place)
         part[...] = mine
         send[...] = mine.T.astype(BF16)
 
@@ -291,7 +322,6 @@
 
 
 WHOLE = pl.BlockSpec(memory_space=pltpu.VMEM)
-SCALAR = pl.BlockSpec(memory_space=pltpu.SMEM)
 
 
 def body(tiles, tile_ids, occ_blocks, virt_blocks):
@@ -304,22 +334,23 @@
     anywhere = pl.BlockSpec(memory_space=pltpu.HBM)
     pitch = side + 8
     strided = [pltpu.VMEM((flat // (2 * side) * pitch, 2 * side), F32)] * 2
-    even, odd, send_row, near, far, green = pl.pallas_call(
+    even, odd, send_row, near, far, lows, held = pl.pallas_call(
         send_kernel,
         in_specs=[anywhere] * 4,
-        out_specs=[WHOLE] * 2 + [anywhere] * 3 + [WHOLE],
+        out_specs=[WHOLE] * 2 + [anywhere] * 3 + [WHOLE] * 2,
         out_shape=[
             jax.ShapeDtypeStruct((slots, side, cut), BF16),
             jax.ShapeDtypeStruct((slots, side, cut), BF16),
             jax.ShapeDtypeStruct((2, 2, flat), BF16),
             jax.ShapeDtypeStruct((2, 2, flat), BF16),
             jax.ShapeDtypeStruct((3, 2, flat), BF16),
-            jax.ShapeDtypeStruct((2, 2, side // 2, side), BF16),
+            jax.ShapeDtypeStruct((slots, side // 2, side), BF16),
+            jax.ShapeDtypeStruct((slots, side, flat), BF16),
         ],
         scratch_shapes=[
-            pltpu.VMEM((slots, side, flat), BF16),
             pltpu.VMEM(occ_blocks.shape, BF16),
             pltpu.SMEM(tile_ids.shape, jnp.int32),
+            pltpu.VMEM((2, 2, side // 2, side), BF16),
             *strided,
             pltpu.SemaphoreType.DMA((slots + 6,)),
         ],
@@ -328,16 +359,6 @@
     got_odd = swapped(odd, 1)
     got_even = swapped(even, 0)
 
-    macs = slots * slots * 3 * side * side * flat
-    half = pl.pallas_call(
-        functools.partial(half_kernel, rows),
-        in_specs=[SCALAR, WHOLE, WHOLE] + [pl.BlockSpec(memory_space=pl.ANY)] * 2,
-        out_specs=WHOLE,
-        out_shape=pltpu.VMEM((slots, side, flat), BF16),
-        scratch_shapes=[*strided, pltpu.SemaphoreType.DMA((1,))],
-        compiler_params=params(12),
-        cost_estimate=pl.CostEstimate(flops=2 * macs, bytes_accessed=4 * slots * side * flat, transcendentals=0),
-    )(tile_ids, green, tiles, even, odd)
     route = []
     for g in range(lax.axis_size("grp")):
         for m in range(g % 2, members - 1, 2):
@@ -345,22 +366,27 @@
             route += [(a, b), (b, a)]
     fetched = lax.ppermute(send_row, ("grp", "mem"), route)
     macs = slots * slots * 3 * side * side * flat
-    half = pl.pallas_call(
+    picks = -(-slots * 3 // 8) * 8
+    half, pick, masks, left, place = pl.pallas_call(
         functools.partial(half_kernel, rows),
-        in_specs=[SCALAR, WHOLE, WHOLE] + [pl.BlockSpec(memory_space=pl.ANY)] * 2,
-        out_specs=WHOLE,
-        out_shape=pltpu.VMEM((slots, side, flat), BF16),
-        scratch_shapes=[*strided, pltpu.SemaphoreType.DMA((1,))],
+        in_specs=[anywhere, WHOLE, WHOLE] + [pl.BlockSpec(memory_space=pl.ANY)] * 2,
+        out_specs=[WHOLE] * 5,
+        out_shape=[
+            pltpu.VMEM((slots, side, flat), BF16),
+            pltpu.VMEM((picks, 16), BF16),
+            pltpu.VMEM((3, picks, slots * side), F32),
+            pltpu.VMEM((-(-RIB * slots // 8) * 8, slots * side), F32),
+            pltpu.VMEM((3, slots * side, width), BF16),
+        ],
+        scratch_shapes=[pltpu.SMEM(tile_ids.shape, jnp.int32), *strided, pltpu.SemaphoreType.DMA((2,))],
         compiler_params=params(12),
         cost_estimate=pl.CostEstimate(flops=2 * macs, bytes_accessed=4 * slots * side * flat, transcendentals=0),
-    )(tile_ids, green, tiles, even, odd)
-    forward = [(i, i + 1) for i in range(members - 1)]
-    backward = [(b, a) for a, b in forward]
+    )(in_hbm(tile_ids), lows, held, even, odd)
     fetched, half = lax.optimization_barrier((fetched, half))
     passed = swapped(fetched, 0)
     y_all, v_high = pl.pallas_call(
-        functools.partial(prepare_kernel, rows),
-        in_specs=[SCALAR] + [WHOLE] * 6,
+        prepare_kernel,
+        in_specs=[WHOLE] * 7,
         out_specs=[WHOLE, WHOLE],
         out_shape=[
             pltpu.VMEM((slots * 3 * side, flat), BF16),
@@ -369,22 +395,19 @@
         scratch_shapes=[pltpu.VMEM((16, flat), F32), pltpu.VMEM((slots * 3, WIDE, WIDE), BF16)],
         compiler_params=params(20),
         cost_estimate=pl.CostEstimate(flops=3 * macs, bytes_accessed=10 * slots * side * flat, transcendentals=0),
-    )(tile_ids, fetched, passed, near, far, half, tiles)
-    found = [
-        pltpu.VMEM((RIB, side, slots * side), F32),
-        pltpu.VMEM((slots * 3 * side, slots * side), F32),
-    ]
+    )(pick, fetched, passed, near, far, half, held)
+    found = [pltpu.VMEM((slots * 3 * side, slots * side), F32)]
 
     def coupled(got, odd_is_upper_group):
         return pl.pallas_call(
             functools.partial(pair_kernel, odd_is_upper_group),
-            in_specs=[SCALAR] + [WHOLE] * 3,
+            in_specs=[WHOLE] * 6,
             out_specs=[WHOLE] * 2,
             out_shape=[pltpu.VMEM((width, width), F32), pltpu.VMEM((width, width), BF16)],
             scratch_shapes=found,
             compiler_params=params(20),
             cost_estimate=pl.CostEstimate(flops=macs, bytes_accessed=8 * slots * side * flat, transcendentals=0),
-        )(tile_ids, y_all, v_high, got)
+        )(masks, left, place, y_all, v_high, got)
 
     part_even, out_even = coupled(got_even, True)
     back_even = swapped(out_even, 0)
@@ -392,13 +415,13 @@
     back_odd = swapped(out_odd, 1)
     middle = pl.pallas_call(
         middle_kernel,
-        in_specs=[SCALAR, WHOLE, WHOLE, pl.BlockSpec(memory_space=pl.ANY)],
+        in_specs=[WHOLE] * 5 + [pl.BlockSpec(memory_space=pl.ANY)],
         out_specs=WHOLE,
         out_shape=pltpu.VMEM((width, width), F32),
         scratch_shapes=found,
         compiler_params=params(20),
         cost_estimate=pl.CostEstimate(flops=2 * macs, bytes_accessed=8 * slots * side * flat, transcendentals=0),
-    )(tile_ids, y_all, tiles, out_odd)
+    )(masks, left, place, y_all, held, out_odd)
     band = pl.pallas_call(
         band_kernel,
         in_specs=[WHOLE] * 5,

time: 44.3 us -> 43.7 us (0.986)
  Pallas kernels: 16.7 us -> 13.5 us
  waiting for transfers between devices: 2.58 us -> 4.83 us
  blocking collectives: 14.1 us -> 14.6 us
    ppermute x5, waiting for transfers between devices: 2.57 us -> 4.83 us  [swapped(): return lax.ppermute(block, 'grp', pairs + [(b, a) for a, b in pairs])]
    pallas_call x3, Pallas kernels: 8.88 us -> 7.19 us  [the longest x1 3.08 us: body(): pl.pallas_call(prepare_kernel, in_specs=[WHOLE] * 7, out_specs=[WHOLE, WH...]
    pallas_call x2, Pallas kernels: 4.26 us -> 2.85 us  [coupled(): pl.pallas_call(functools.partial(pair_kernel, odd_is_upper_group), in_spe...]
    all_to_all x1, blocking collectives: 14.1 us -> 14.6 us  [body(): lax.all_to_all(band.reshape(members, width // members, 3 * width), 'mem',...]
  transfers between devices with their start and end apart: 6 -> 6, of which waited for: 2 -> 3; matrix products, arithmetic and copies ran while one was open for 0% -> 0% of each run, Pallas kernels for 30% -> 23%
where the time goes in v7:
time: 43.7 us; the launch traced here: 43.5 us
  blocking collectives  14.6 us (33%)
  Pallas kernels  13.5 us (31%)
  starting transfers between devices  9.82 us (22%)
  waiting for transfers between devices  4.83 us (11%)
  other arithmetic  0.69 us (2%)
    all_to_all x1, blocking collectives, body(): lax.all_to_all(band.reshape(members, width // members, 3 * width), 'mem',...  14.6 us
    ppermute x5, starting transfers between devices, swapped(): return lax.ppermute(block, 'grp', pairs + [(b, a) for a, b in pairs])  9.16 us
    ppermute x5, waiting for transfers between devices, swapped(): return lax.ppermute(block, 'grp', pairs + [(b, a) for a, b in pairs])  4.83 us
    pallas_call x1, Pallas kernels, body(): pl.pallas_call(send_kernel, in_specs=[anywhere] * 4, out_specs=[WHOLE] *...  3.41 us
    pallas_call x1, Pallas kernels, body(): pl.pallas_call(prepare_kernel, in_specs=[WHOLE] * 7, out_specs=[WHOLE, WH...  3.08 us
    pallas_call x2, Pallas kernels, coupled(): pl.pallas_call(functools.partial(pair_kernel, odd_is_upper_group), in_spe...  2.85 us
    pallas_call x1, Pallas kernels, body(): pl.pallas_call(middle_kernel, in_specs=[WHOLE] * 5 + [pl.BlockSpec(memory...  2.18 us
    pallas_call x1, Pallas kernels, body(): pl.pallas_call(functools.partial(half_kernel, rows), in_specs=[anywhere,...  1.93 us
  transfers between devices with their start and end apart: 6, of which 3 were waited for; matrix products, arithmetic and copies ran while one was open for 0% of the time, Pallas kernels for 23%

profile of v7, /device:TPU:1, one launch (start us, length us, event | category | flops | bytes accessed | tf_op | source)
XLA Modules:
  0.0 43.5 jit_solution(7430418975675130722)
XLA Ops:
  0.0 3.4 %shard_map.46 = (bf16[4,64,2048]{2,1,0:T(8,128)(2,1)S(1)}, bf16[4,64,2048]{2,1,0:T(8,128)(2,1)S(1)}, bf16[2,2,4096]{2,1,0:T(2,128)(2,1)S(1)}, bf16[2,2,4096]{2,1...) custom-call(bf16[48,4096]{1,0:T(8,128)(2,1)} %occ_in.1, ...), custom_call_target="tpu_custom_call" | custom-call | tf_op jit(solution)/shard_map/pallas_call | solution.py:337
  3.4 0.1 collective-permute-start.3
  3.5 4.5 %collective-permute-start.2 = (bf16[4,64,2048]{2,1,0:T(8,128)(2,1)S(1)}, bf16[4,64,2048]{2,1,0:T(8,128)(2,1)S(1)}, u32[]{:S(2)}, u32[]{:S(2)}) collective-permute-start(bf16[4,64,2048]{2,1,0:T(8,128)(2,1)S(1)} %get-tuple-element.28.odd), channel_id=1, source_target_pairs={{8,16},{16,8},{9,17},{17,9},{10,18},{18,10},{11,19},{19,11},{12,20... | collective-permute-start | bytes 3145736 | tf_op jit(solution)/shard_map/ppermute | solution.py:309
  8.0 0.7 %collective-permute-start = (bf16[2,2,4096]{2,1,0:T(2,128)(2,1)S(1)}, bf16[2,2,4096]{2,1,0:T(2,128)(2,1)S(1)}, u32[]{:S(2)}, u32[]{:S(2)}) collective-permute-start(bf16[2,2,4096]{2,1,0:T(2,128)(2,1)S(1)} %get-tuple-element.33), channel_id=1, source_target_pairs={{0,1},{1,0},{2,3},{3,2},{4,5},{5,4},{6,7},{7,6},{9,10},{10,9},{11,... | collective-permute-start | bytes 98312 | tf_op jit(solution)/shard_map/ppermute | solution.py:367
  8.7 1.9 %shard_map.47 = (bf16[4,64,4096]{2,1,0:T(8,128)(2,1)S(1)}, bf16[16,16]{1,0:T(8,128)(2,1)S(1)}, f32[3,16,256]{2,1,0:T(8,128)S(1)}, f32[16,256]{1,0:T(8,128)S(1)}, bf16[3,256,256]{2,1,0:T(8,128)(2,1)S(1)}) custom-call(s32[4,4,4]{2,1,0:T(4,128)} %ids_in.3, bf16[4,32,64]{2,1,0:T(8,128)(2,1)S(1)} %get-tuple-element.25.lows, ...), custom_call_target="tpu_custom_call" | custom-call | flops 1610612736 | bytes 4194304 | tf_op jit(solution)/shard_map/pallas_call | solution.py:370
  10.6 0.0 collective-permute-done.fetched
  10.6 0.5 %collective-permute-start.1 = (bf16[2,2,4096]{2,1,0:T(2,128)(2,1)S(1)}, bf16[2,2,4096]{2,1,0:T(2,128)(2,1)S(1)}, u32[]{:S(2)}, u32[]{:S(2)}) collective-permute-start(bf16[2,2,4096]{2,1,0:T(2,128)(2,1)S(1)} %collective-permute-done.fetched), channel_id=1, source_target_pairs={{0,8},{16,24},{8,0},{24,16},{1,9},{17,25},{9,1},{25,17},{2,10},{18... | collective-permute-start | bytes 98312 | tf_op jit(solution)/shard_map/ppermute | solution.py:309
  11.1 0.9 %collective-permute-done.1.passed = bf16[2,2,4096]{2,1,0:T(2,128)(2,1)S(1)} collective-permute-done((bf16[2,2,4096]{2,1,0:T(2,128)(2,1)S(1)}, bf16[2,2,4096]{2,1,0:T(2,128)(2,1)S(1)}, u32[]{:S(2)}, u32[]{:S(2)}) %collective-permute-start.1) | collective-permute-done | bytes 32800 | tf_op jit(solution)/shard_map/ppermute | solution.py:309
  12.0 3.1 %shard_map.48 = (bf16[768,4096]{1,0:T(8,128)(2,1)S(1)}, bf16[768,2048]{1,0:T(8,128)(2,1)S(1)}) custom-call(bf16[16,16]{1,0:T(8,128)(2,1)S(1)} %get-tuple-element.32.pick, bf16[2,2,4096]{2,1,0:T(2,128)(2,1)S(1)} %collective-permute-done.fetched, bf16[2,2,4096]{2,1,0:T(2,128)(2,1)S(1)} %collective-permute-done.1.passed, ...), custom_call_target="tpu_custom_call" | custom-call | flops 2415919104 | bytes 10485760 | tf_op jit(solution)/shard_map/pallas_call | solution.py:387
  15.1 0.0 collective-permute-done.3.other
  15.1 1.4 %shard_map.51 = (f32[256,256]{1,0:T(8,128)S(1)}, bf16[256,256]{1,0:T(8,128)(2,1)S(1)}) custom-call(f32[3,16,256]{2,1,0:T(8,128)S(1)} %get-tuple-element.29.masks, f32[16,256]{1,0:T(8,128)S(1)} %get-tuple-element.30.left, bf16[3,256,256]{2,1,0:T(8,128)(2,1)S(1)} %get-tuple-element.31.place, bf16[768,4096]{1,0:T(8,128)(2,1)S(1)} %get-tuple-element.39.y_all, ...), custom_call_target="tpu_custom_call" | custom-call | flops 805306368 | bytes 8388608 | tf_op jit(solution)/shard_map/pallas_call | solution.py:402
  16.5 0.4 collective-permute-start.4
  16.9 3.5 %collective-permute-done.2.other = bf16[4,64,2048]{2,1,0:T(8,128)(2,1)S(1)} collective-permute-done((bf16[4,64,2048]{2,1,0:T(8,128)(2,1)S(1)}, bf16[4,64,2048]{2,1,0:T(8,128)(2,1)S(1)}, u32[]{:S(2)}, u32[]{:S(2)}) %collective-permute-start.2) | collective-permute-done | bytes 1048608 | tf_op jit(solution)/shard_map/ppermute | solution.py:309
  20.5 1.4 %shard_map.49 = (f32[256,256]{1,0:T(8,128)S(1)}, bf16[256,256]{1,0:T(8,128)(2,1)S(1)}) custom-call(f32[3,16,256]{2,1,0:T(8,128)S(1)} %get-tuple-element.29.masks, f32[16,256]{1,0:T(8,128)S(1)} %get-tuple-element.30.left, bf16[3,256,256]{2,1,0:T(8,128)(2,1)S(1)} %get-tuple-element.31.place, bf16[768,4096]{1,0:T(8,128)(2,1)S(1)} %get-tuple-element.39.y_all, ...), custom_call_target="tpu_custom_call" | custom-call | flops 805306368 | bytes 8388608 | tf_op jit(solution)/shard_map/pallas_call | solution.py:402
  21.9 3.6 %collective-permute-start.5 = (bf16[256,256]{1,0:T(8,128)(2,1)S(1)}, bf16[256,256]{1,0:T(8,128)(2,1)S(1)}, u32[]{:S(2)}, u32[]{:S(2)}) collective-permute-start(bf16[256,256]{1,0:T(8,128)(2,1)S(1)} %get-tuple-element.41.after), channel_id=1, source_target_pairs={{8,16},{16,8},{9,17},{17,9},{10,18},{18,10},{11,19},{19,11},{12,20... | collective-permute-start | bytes 393224 | tf_op jit(solution)/shard_map/ppermute | solution.py:309
  25.6 2.2 %shard_map.50.middle = f32[256,256]{1,0:T(8,128)S(1)} custom-call(f32[3,16,256]{2,1,0:T(8,128)S(1)} %get-tuple-element.29.masks, f32[16,256]{1,0:T(8,128)S(1)} %get-tuple-element.30.left, bf16[3,256,256]{2,1,0:T(8,128)(2,1)S(1)} %get-tuple-element.31.place, bf16[768,4096]{1,0:T(8,128)(2,1)S(1)} %get-tuple-element.39.y_all, ...), custom_call_target="tpu_custom_call" | custom-call | flops 1610612736 | bytes 8388608 | tf_op jit(solution)/shard_map/pallas_call | solution.py:416
  27.8 0.0 collective-permute-done.4.got_even
  27.8 0.4 collective-permute-done.5.got_odd
  28.2 0.1 shard_map.52
  28.3 14.6 %all_to_all.5 = bf16[8,32,768]{2,1,0:T(8,128)(2,1)S(1)} all-to-all(bf16[8,32,768]{2,1,0:T(8,128)(2,1)S(1)} %bitcast.1), channel_id=1, replica_groups=mesh['grp'=4,'mem'=8] {'mem'}, dimensions={0} | all-to-all | bytes 786432 | tf_op jit(solution)/shard_map/all_to_all | solution.py:432
  42.8 0.7 %convert_reduce_fusion = f32[32,768]{1,0:T(8,128)} fusion(bf16[8,32,768]{2,1,0:T(8,128)(2,1)S(1)} %all_to_all.5), kind=kLoop, calls=%fused_computation | loop fusion | flops 368640 | bytes 491520 | tf_op jit(solution)/shard_map/reduce_sum | solution.py:433
Async XLA Ops:
  3.4 11.7 %collective-permute-start.3 = (bf16[4,64,2048]{2,1,0:T(8,128)(2,1)S(1)}, bf16[4,64,2048]{2,1,0:T(8,128)(2,1)S(1)}, u32[]{:S(2)}, u32[]{:S(2)}) collective-permute-start(bf16[4,64,2048]{2,1,0:T(8,128)(2,1)S(1)} %get-tuple-element.27.even), channel_id=1, source_target_pairs={{0,8},{16,24},{8,0},{24,16},{1,9},{17,25},{9,1},{25,17},{2,10},{18... | collective-permute-start | bytes 3145736 | tf_op jit(solution)/shard_map/ppermute | solution.py:309
  3.5 16.9 %collective-permute-start.2 = (bf16[4,64,2048]{2,1,0:T(8,128)(2,1)S(1)}, bf16[4,64,2048]{2,1,0:T(8,128)(2,1)S(1)}, u32[]{:S(2)}, u32[]{:S(2)}) collective-permute-start(bf16[4,64,2048]{2,1,0:T(8,128)(2,1)S(1)} %get-tuple-element.28.odd), channel_id=1, source_target_pairs={{8,16},{16,8},{9,17},{17,9},{10,18},{18,10},{11,19},{19,11},{12,20... | collective-permute-start | bytes 3145736 | tf_op jit(solution)/shard_map/ppermute | solution.py:309
  8.0 2.6 %collective-permute-start = (bf16[2,2,4096]{2,1,0:T(2,128)(2,1)S(1)}, bf16[2,2,4096]{2,1,0:T(2,128)(2,1)S(1)}, u32[]{:S(2)}, u32[]{:S(2)}) collective-permute-start(bf16[2,2,4096]{2,1,0:T(2,128)(2,1)S(1)} %get-tuple-element.33), channel_id=1, source_target_pairs={{0,1},{1,0},{2,3},{3,2},{4,5},{5,4},{6,7},{7,6},{9,10},{10,9},{11,... | collective-permute-start | bytes 98312 | tf_op jit(solution)/shard_map/ppermute | solution.py:367
  10.6 1.4 %collective-permute-start.1 = (bf16[2,2,4096]{2,1,0:T(2,128)(2,1)S(1)}, bf16[2,2,4096]{2,1,0:T(2,128)(2,1)S(1)}, u32[]{:S(2)}, u32[]{:S(2)}) collective-permute-start(bf16[2,2,4096]{2,1,0:T(2,128)(2,1)S(1)} %collective-permute-done.fetched), channel_id=1, source_target_pairs={{0,8},{16,24},{8,0},{24,16},{1,9},{17,25},{9,1},{25,17},{2,10},{18... | collective-permute-start | bytes 98312 | tf_op jit(solution)/shard_map/ppermute | solution.py:309
  16.5 11.2 %collective-permute-start.4 = (bf16[256,256]{1,0:T(8,128)(2,1)S(1)}, bf16[256,256]{1,0:T(8,128)(2,1)S(1)}, u32[]{:S(2)}, u32[]{:S(2)}) collective-permute-start(bf16[256,256]{1,0:T(8,128)(2,1)S(1)} %get-tuple-element.44), channel_id=1, source_target_pairs={{0,8},{16,24},{8,0},{24,16},{1,9},{17,25},{9,1},{25,17},{2,10},{18... | collective-permute-start | bytes 393224 | tf_op jit(solution)/shard_map/ppermute | solution.py:309
  21.9 6.3 %collective-permute-start.5 = (bf16[256,256]{1,0:T(8,128)(2,1)S(1)}, bf16[256,256]{1,0:T(8,128)(2,1)S(1)}, u32[]{:S(2)}, u32[]{:S(2)}) collective-permute-start(bf16[256,256]{1,0:T(8,128)(2,1)S(1)} %get-tuple-element.41.after), channel_id=1, source_target_pairs={{8,16},{16,8},{9,17},{17,9},{10,18},{18,10},{11,19},{19,11},{12,20... | collective-permute-start | bytes 393224 | tf_op jit(solution)/shard_map/ppermute | solution.py:309

commit v8 on v7

--- a/solution.py
+++ b/solution.py
@@ -26,7 +26,7 @@
     lanes = 2 * side
     high = source.shape[1] // lanes
     some = block.shape[0] // 2
-    pitch = rows_in.shape[0] // high
+    pitch = side + 8
     low = lax.broadcasted_iota(jnp.int32, (some, lanes), 1) < side
     for h in range(high):
         rows_in[h * pitch : h * pitch + side, :] = source[:, h * lanes : (h + 1) * lanes].astype(F32)
@@ -57,15 +57,13 @@
     first_in.start()
     ids_copy.start()
     fetch = [pltpu.make_async_copy(tiles.at[0, t], held.at[t], sem.at[t]) for t in range(slots)]
-    for copy in fetch:
+    for copy in fetch[:2]:
         copy.start()
     start = jnp.where(sends_up(), rows - 2, 0)
     row_copy = pltpu.make_async_copy(virt.at[pl.ds(start, 2)], send_row, sem.at[slots])
     near_copy = pltpu.make_async_copy(virt.at[pl.ds(0, 2)], near, sem.at[slots + 4])
     far_copy = pltpu.make_async_copy(virt.at[pl.ds(rows - 3, 3)], far, sem.at[slots + 5])
     edges = [row_copy, near_copy, far_copy]
-    for copy in edges:
-        copy.start()
     group = lax.axis_index("grp")
     first = lax.axis_index("mem") * rows
     odd_one = is_odd()
@@ -88,6 +86,8 @@
     ids_copy.wait()
     for t in range(slots):
         fetch[t].wait()
+        for copy in fetch[t + 2 : t + 3] if t + 2 < slots else edges if t + 2 == slots else []:
+            copy.start()
         end = (ids[group, 1, t] != first).astype(jnp.int32)
         lows[t] = green[end, 0]
         block = green[end, 1]
@@ -333,7 +333,7 @@
 
     anywhere = pl.BlockSpec(memory_space=pltpu.HBM)
     pitch = side + 8
-    strided = [pltpu.VMEM((flat // (2 * side) * pitch, 2 * side), F32)] * 2
+    strided = [pltpu.VMEM(((flat // (2 * side) + 1) * pitch, 2 * side), F32)] * 2
     even, odd, send_row, near, far, lows, held = pl.pallas_call(
         send_kernel,
         in_specs=[anywhere] * 4,

time: 43.7 us -> 43.8 us (level)
  no operation moved by 1% of the time
where the time goes in v8:
time: 43.8 us; the launch traced here: 43.5 us
  blocking collectives  14.6 us (33%)
  Pallas kernels  13.5 us (31%)
  starting transfers between devices  9.82 us (22%)
  waiting for transfers between devices  4.84 us (11%)
  other arithmetic  0.69 us (2%)
    all_to_all x1, blocking collectives, body(): lax.all_to_all(band.reshape(members, width // members, 3 * width), 'mem',...  14.6 us
    ppermute x5, starting transfers between devices, swapped(): return lax.ppermute(block, 'grp', pairs + [(b, a) for a, b in pairs])  9.16 us
    ppermute x5, waiting for transfers between devices, swapped(): return lax.ppermute(block, 'grp', pairs + [(b, a) for a, b in pairs])  4.83 us
    pallas_call x1, Pallas kernels, body(): pl.pallas_call(send_kernel, in_specs=[anywhere] * 4, out_specs=[WHOLE] *...  3.41 us
    pallas_call x1, Pallas kernels, body(): pl.pallas_call(prepare_kernel, in_specs=[WHOLE] * 7, out_specs=[WHOLE, WH...  3.08 us
    pallas_call x2, Pallas kernels, coupled(): pl.pallas_call(functools.partial(pair_kernel, odd_is_upper_group), in_spe...  2.85 us
    pallas_call x1, Pallas kernels, body(): pl.pallas_call(middle_kernel, in_specs=[WHOLE] * 5 + [pl.BlockSpec(memory...  2.18 us
    pallas_call x1, Pallas kernels, body(): pl.pallas_call(functools.partial(half_kernel, rows), in_specs=[anywhere,...  1.92 us
  transfers between devices with their start and end apart: 6, of which 3 were waited for; matrix products, arithmetic and copies ran while one was open for 0% of the time, Pallas kernels for 23%

profile of v8, /device:TPU:1, one launch (start us, length us, event | category | flops | bytes accessed | tf_op | source)
XLA Modules:
  0.0 43.5 jit_solution(10736922757668687790)
XLA Ops:
  0.0 3.4 %shard_map.46 = (bf16[4,64,2048]{2,1,0:T(8,128)(2,1)S(1)}, bf16[4,64,2048]{2,1,0:T(8,128)(2,1)S(1)}, bf16[2,2,4096]{2,1,0:T(2,128)(2,1)S(1)}, bf16[2,2,4096]{2,1...) custom-call(bf16[48,4096]{1,0:T(8,128)(2,1)} %occ_in.1, ...), custom_call_target="tpu_custom_call" | custom-call | tf_op jit(solution)/shard_map/pallas_call | solution.py:337
  3.4 0.1 collective-permute-start.3
  3.5 4.5 %collective-permute-start.2 = (bf16[4,64,2048]{2,1,0:T(8,128)(2,1)S(1)}, bf16[4,64,2048]{2,1,0:T(8,128)(2,1)S(1)}, u32[]{:S(2)}, u32[]{:S(2)}) collective-permute-start(bf16[4,64,2048]{2,1,0:T(8,128)(2,1)S(1)} %get-tuple-element.28.odd), channel_id=1, source_target_pairs={{8,16},{16,8},{9,17},{17,9},{10,18},{18,10},{11,19},{19,11},{12,20... | collective-permute-start | bytes 3145736 | tf_op jit(solution)/shard_map/ppermute | solution.py:309
  8.0 0.7 %collective-permute-start = (bf16[2,2,4096]{2,1,0:T(2,128)(2,1)S(1)}, bf16[2,2,4096]{2,1,0:T(2,128)(2,1)S(1)}, u32[]{:S(2)}, u32[]{:S(2)}) collective-permute-start(bf16[2,2,4096]{2,1,0:T(2,128)(2,1)S(1)} %get-tuple-element.33), channel_id=1, source_target_pairs={{0,1},{1,0},{2,3},{3,2},{4,5},{5,4},{6,7},{7,6},{9,10},{10,9},{11,... | collective-permute-start | bytes 98312 | tf_op jit(solution)/shard_map/ppermute | solution.py:367
  8.7 1.9 %shard_map.47 = (bf16[4,64,4096]{2,1,0:T(8,128)(2,1)S(1)}, bf16[16,16]{1,0:T(8,128)(2,1)S(1)}, f32[3,16,256]{2,1,0:T(8,128)S(1)}, f32[16,256]{1,0:T(8,128)S(1)}, bf16[3,256,256]{2,1,0:T(8,128)(2,1)S(1)}) custom-call(s32[4,4,4]{2,1,0:T(4,128)} %ids_in.3, bf16[4,32,64]{2,1,0:T(8,128)(2,1)S(1)} %get-tuple-element.25.lows, ...), custom_call_target="tpu_custom_call" | custom-call | flops 1610612736 | bytes 4194304 | tf_op jit(solution)/shard_map/pallas_call | solution.py:370
  10.6 0.0 collective-permute-done.fetched
  10.6 0.5 %collective-permute-start.1 = (bf16[2,2,4096]{2,1,0:T(2,128)(2,1)S(1)}, bf16[2,2,4096]{2,1,0:T(2,128)(2,1)S(1)}, u32[]{:S(2)}, u32[]{:S(2)}) collective-permute-start(bf16[2,2,4096]{2,1,0:T(2,128)(2,1)S(1)} %collective-permute-done.fetched), channel_id=1, source_target_pairs={{0,8},{16,24},{8,0},{24,16},{1,9},{17,25},{9,1},{25,17},{2,10},{18... | collective-permute-start | bytes 98312 | tf_op jit(solution)/shard_map/ppermute | solution.py:309
  11.1 0.9 %collective-permute-done.1.passed = bf16[2,2,4096]{2,1,0:T(2,128)(2,1)S(1)} collective-permute-done((bf16[2,2,4096]{2,1,0:T(2,128)(2,1)S(1)}, bf16[2,2,4096]{2,1,0:T(2,128)(2,1)S(1)}, u32[]{:S(2)}, u32[]{:S(2)}) %collective-permute-start.1) | collective-permute-done | bytes 32800 | tf_op jit(solution)/shard_map/ppermute | solution.py:309
  12.0 3.1 %shard_map.48 = (bf16[768,4096]{1,0:T(8,128)(2,1)S(1)}, bf16[768,2048]{1,0:T(8,128)(2,1)S(1)}) custom-call(bf16[16,16]{1,0:T(8,128)(2,1)S(1)} %get-tuple-element.32.pick, bf16[2,2,4096]{2,1,0:T(2,128)(2,1)S(1)} %collective-permute-done.fetched, bf16[2,2,4096]{2,1,0:T(2,128)(2,1)S(1)} %collective-permute-done.1.passed, ...), custom_call_target="tpu_custom_call" | custom-call | flops 2415919104 | bytes 10485760 | tf_op jit(solution)/shard_map/pallas_call | solution.py:387
  15.1 0.0 collective-permute-done.3.other
  15.1 1.4 %shard_map.51 = (f32[256,256]{1,0:T(8,128)S(1)}, bf16[256,256]{1,0:T(8,128)(2,1)S(1)}) custom-call(f32[3,16,256]{2,1,0:T(8,128)S(1)} %get-tuple-element.29.masks, f32[16,256]{1,0:T(8,128)S(1)} %get-tuple-element.30.left, bf16[3,256,256]{2,1,0:T(8,128)(2,1)S(1)} %get-tuple-element.31.place, bf16[768,4096]{1,0:T(8,128)(2,1)S(1)} %get-tuple-element.39.y_all, ...), custom_call_target="tpu_custom_call" | custom-call | flops 805306368 | bytes 8388608 | tf_op jit(solution)/shard_map/pallas_call | solution.py:402
  16.5 0.4 collective-permute-start.4
  16.9 3.5 %collective-permute-done.2.other = bf16[4,64,2048]{2,1,0:T(8,128)(2,1)S(1)} collective-permute-done((bf16[4,64,2048]{2,1,0:T(8,128)(2,1)S(1)}, bf16[4,64,2048]{2,1,0:T(8,128)(2,1)S(1)}, u32[]{:S(2)}, u32[]{:S(2)}) %collective-permute-start.2) | collective-permute-done | bytes 1048608 | tf_op jit(solution)/shard_map/ppermute | solution.py:309
  20.5 1.4 %shard_map.49 = (f32[256,256]{1,0:T(8,128)S(1)}, bf16[256,256]{1,0:T(8,128)(2,1)S(1)}) custom-call(f32[3,16,256]{2,1,0:T(8,128)S(1)} %get-tuple-element.29.masks, f32[16,256]{1,0:T(8,128)S(1)} %get-tuple-element.30.left, bf16[3,256,256]{2,1,0:T(8,128)(2,1)S(1)} %get-tuple-element.31.place, bf16[768,4096]{1,0:T(8,128)(2,1)S(1)} %get-tuple-element.39.y_all, ...), custom_call_target="tpu_custom_call" | custom-call | flops 805306368 | bytes 8388608 | tf_op jit(solution)/shard_map/pallas_call | solution.py:402
  21.9 3.6 %collective-permute-start.5 = (bf16[256,256]{1,0:T(8,128)(2,1)S(1)}, bf16[256,256]{1,0:T(8,128)(2,1)S(1)}, u32[]{:S(2)}, u32[]{:S(2)}) collective-permute-start(bf16[256,256]{1,0:T(8,128)(2,1)S(1)} %get-tuple-element.41.after), channel_id=1, source_target_pairs={{8,16},{16,8},{9,17},{17,9},{10,18},{18,10},{11,19},{19,11},{12,20... | collective-permute-start | bytes 393224 | tf_op jit(solution)/shard_map/ppermute | solution.py:309
  25.6 2.2 %shard_map.50.middle = f32[256,256]{1,0:T(8,128)S(1)} custom-call(f32[3,16,256]{2,1,0:T(8,128)S(1)} %get-tuple-element.29.masks, f32[16,256]{1,0:T(8,128)S(1)} %get-tuple-element.30.left, bf16[3,256,256]{2,1,0:T(8,128)(2,1)S(1)} %get-tuple-element.31.place, bf16[768,4096]{1,0:T(8,128)(2,1)S(1)} %get-tuple-element.39.y_all, ...), custom_call_target="tpu_custom_call" | custom-call | flops 1610612736 | bytes 8388608 | tf_op jit(solution)/shard_map/pallas_call | solution.py:416
  27.8 0.0 collective-permute-done.4.got_even
  27.8 0.4 collective-permute-done.5.got_odd
  28.2 0.1 shard_map.52
  28.3 14.6 %all_to_all.5 = bf16[8,32,768]{2,1,0:T(8,128)(2,1)S(1)} all-to-all(bf16[8,32,768]{2,1,0:T(8,128)(2,1)S(1)} %bitcast.1), channel_id=1, replica_groups=mesh['grp'=4,'mem'=8] {'mem'}, dimensions={0} | all-to-all | bytes 786432 | tf_op jit(solution)/shard_map/all_to_all | solution.py:432
  42.8 0.7 %convert_reduce_fusion = f32[32,768]{1,0:T(8,128)} fusion(bf16[8,32,768]{2,1,0:T(8,128)(2,1)S(1)} %all_to_all.5), kind=kLoop, calls=%fused_computation | loop fusion | flops 368640 | bytes 491520 | tf_op jit(solution)/shard_map/reduce_sum | solution.py:433
Async XLA Ops:
  3.4 11.7 %collective-permute-start.3 = (bf16[4,64,2048]{2,1,0:T(8,128)(2,1)S(1)}, bf16[4,64,2048]{2,1,0:T(8,128)(2,1)S(1)}, u32[]{:S(2)}, u32[]{:S(2)}) collective-permute-start(bf16[4,64,2048]{2,1,0:T(8,128)(2,1)S(1)} %get-tuple-element.27.even), channel_id=1, source_target_pairs={{0,8},{16,24},{8,0},{24,16},{1,9},{17,25},{9,1},{25,17},{2,10},{18... | collective-permute-start | bytes 3145736 | tf_op jit(solution)/shard_map/ppermute | solution.py:309
  3.5 16.9 %collective-permute-start.2 = (bf16[4,64,2048]{2,1,0:T(8,128)(2,1)S(1)}, bf16[4,64,2048]{2,1,0:T(8,128)(2,1)S(1)}, u32[]{:S(2)}, u32[]{:S(2)}) collective-permute-start(bf16[4,64,2048]{2,1,0:T(8,128)(2,1)S(1)} %get-tuple-element.28.odd), channel_id=1, source_target_pairs={{8,16},{16,8},{9,17},{17,9},{10,18},{18,10},{11,19},{19,11},{12,20... | collective-permute-start | bytes 3145736 | tf_op jit(solution)/shard_map/ppermute | solution.py:309
  8.0 2.6 %collective-permute-start = (bf16[2,2,4096]{2,1,0:T(2,128)(2,1)S(1)}, bf16[2,2,4096]{2,1,0:T(2,128)(2,1)S(1)}, u32[]{:S(2)}, u32[]{:S(2)}) collective-permute-start(bf16[2,2,4096]{2,1,0:T(2,128)(2,1)S(1)} %get-tuple-element.33), channel_id=1, source_target_pairs={{0,1},{1,0},{2,3},{3,2},{4,5},{5,4},{6,7},{7,6},{9,10},{10,9},{11,... | collective-permute-start | bytes 98312 | tf_op jit(solution)/shard_map/ppermute | solution.py:367
  10.6 1.4 %collective-permute-start.1 = (bf16[2,2,4096]{2,1,0:T(2,128)(2,1)S(1)}, bf16[2,2,4096]{2,1,0:T(2,128)(2,1)S(1)}, u32[]{:S(2)}, u32[]{:S(2)}) collective-permute-start(bf16[2,2,4096]{2,1,0:T(2,128)(2,1)S(1)} %collective-permute-done.fetched), channel_id=1, source_target_pairs={{0,8},{16,24},{8,0},{24,16},{1,9},{17,25},{9,1},{25,17},{2,10},{18... | collective-permute-start | bytes 98312 | tf_op jit(solution)/shard_map/ppermute | solution.py:309
  16.5 11.2 %collective-permute-start.4 = (bf16[256,256]{1,0:T(8,128)(2,1)S(1)}, bf16[256,256]{1,0:T(8,128)(2,1)S(1)}, u32[]{:S(2)}, u32[]{:S(2)}) collective-permute-start(bf16[256,256]{1,0:T(8,128)(2,1)S(1)} %get-tuple-element.44), channel_id=1, source_target_pairs={{0,8},{16,24},{8,0},{24,16},{1,9},{17,25},{9,1},{25,17},{2,10},{18... | collective-permute-start | bytes 393224 | tf_op jit(solution)/shard_map/ppermute | solution.py:309
  21.9 6.3 %collective-permute-start.5 = (bf16[256,256]{1,0:T(8,128)(2,1)S(1)}, bf16[256,256]{1,0:T(8,128)(2,1)S(1)}, u32[]{:S(2)}, u32[]{:S(2)}) collective-permute-start(bf16[256,256]{1,0:T(8,128)(2,1)S(1)} %get-tuple-element.41.after), channel_id=1, source_target_pairs={{8,16},{16,8},{9,17},{17,9},{10,18},{18,10},{11,19},{19,11},{12,20... | collective-permute-start | bytes 393224 | tf_op jit(solution)/shard_map/ppermute | solution.py:309

commit v9 on v8

--- a/solution.py
+++ b/solution.py
@@ -253,7 +253,10 @@
                     result[at, k * WIDE : (k + 1) * WIDE] = y[k * side : (k + 1) * side]
 
     transform(half, 0, y_all, (NT, NN, NN))
-    transform(tiles, cut, v_high, (NT, NT, NN))
+
+    @pl.when(lax.axis_index("grp") < lax.axis_size("grp") - 1)
+    def _():
+        transform(tiles, cut, v_high, (NT, NT, NN))
 
 
 def middle_kernel(masks, left, place, y_all, tiles, after, middle, products):

time: 43.8 us -> 43.8 us (level)
  transfers between devices with their start and end apart: 6 -> 6, of which waited for: 3 -> 3; matrix products, arithmetic and copies ran while one was open for 0% -> 0% of each run, Pallas kernels for 23% -> 24%
where the time goes in v9:
time: 43.8 us; the launch traced here: 43.5 us
  blocking collectives  14.6 us (33%)
  Pallas kernels  13.8 us (32%)
  starting transfers between devices  9.82 us (22%)
  waiting for transfers between devices  4.6 us (11%)
  other arithmetic  0.69 us (2%)
    all_to_all x1, blocking collectives, body(): lax.all_to_all(band.reshape(members, width // members, 3 * width), 'mem',...  14.6 us
    ppermute x5, starting transfers between devices, swapped(): return lax.ppermute(block, 'grp', pairs + [(b, a) for a, b in pairs])  9.16 us
    ppermute x5, waiting for transfers between devices, swapped(): return lax.ppermute(block, 'grp', pairs + [(b, a) for a, b in pairs])  4.6 us
    pallas_call x1, Pallas kernels, body(): pl.pallas_call(send_kernel, in_specs=[anywhere] * 4, out_specs=[WHOLE] *...  3.41 us
    pallas_call x1, Pallas kernels, body(): pl.pallas_call(prepare_kernel, in_specs=[WHOLE] * 7, out_specs=[WHOLE, WH...  3.32 us
    pallas_call x2, Pallas kernels, coupled(): pl.pallas_call(functools.partial(pair_kernel, odd_is_upper_group), in_spe...  2.85 us
    pallas_call x1, Pallas kernels, body(): pl.pallas_call(middle_kernel, in_specs=[WHOLE] * 5 + [pl.BlockSpec(memory...  2.18 us
    pallas_call x1, Pallas kernels, body(): pl.pallas_call(functools.partial(half_kernel, rows), in_specs=[anywhere,...  1.92 us
  transfers between devices with their start and end apart: 6, of which 3 were waited for; matrix products, arithmetic and copies ran while one was open for 0% of the time, Pallas kernels for 24%

profile of v9, /device:TPU:1, one launch (start us, length us, event | category | flops | bytes accessed | tf_op | source)
XLA Modules:
  0.0 43.5 jit_solution(839293189956857615)
XLA Ops:
  0.0 3.4 %shard_map.46 = (bf16[4,64,2048]{2,1,0:T(8,128)(2,1)S(1)}, bf16[4,64,2048]{2,1,0:T(8,128)(2,1)S(1)}, bf16[2,2,4096]{2,1,0:T(2,128)(2,1)S(1)}, bf16[2,2,4096]{2,1...) custom-call(bf16[48,4096]{1,0:T(8,128)(2,1)} %occ_in.1, ...), custom_call_target="tpu_custom_call" | custom-call | tf_op jit(solution)/shard_map/pallas_call | solution.py:340
  3.4 0.1 collective-permute-start.3
  3.5 4.5 %collective-permute-start.2 = (bf16[4,64,2048]{2,1,0:T(8,128)(2,1)S(1)}, bf16[4,64,2048]{2,1,0:T(8,128)(2,1)S(1)}, u32[]{:S(2)}, u32[]{:S(2)}) collective-permute-start(bf16[4,64,2048]{2,1,0:T(8,128)(2,1)S(1)} %get-tuple-element.28.odd), channel_id=1, source_target_pairs={{8,16},{16,8},{9,17},{17,9},{10,18},{18,10},{11,19},{19,11},{12,20... | collective-permute-start | bytes 3145736 | tf_op jit(solution)/shard_map/ppermute | solution.py:312
  8.0 0.7 %collective-permute-start = (bf16[2,2,4096]{2,1,0:T(2,128)(2,1)S(1)}, bf16[2,2,4096]{2,1,0:T(2,128)(2,1)S(1)}, u32[]{:S(2)}, u32[]{:S(2)}) collective-permute-start(bf16[2,2,4096]{2,1,0:T(2,128)(2,1)S(1)} %get-tuple-element.33), channel_id=1, source_target_pairs={{0,1},{1,0},{2,3},{3,2},{4,5},{5,4},{6,7},{7,6},{9,10},{10,9},{11,... | collective-permute-start | bytes 98312 | tf_op jit(solution)/shard_map/ppermute | solution.py:370
  8.7 1.9 %shard_map.47 = (bf16[4,64,4096]{2,1,0:T(8,128)(2,1)S(1)}, bf16[16,16]{1,0:T(8,128)(2,1)S(1)}, f32[3,16,256]{2,1,0:T(8,128)S(1)}, f32[16,256]{1,0:T(8,128)S(1)}, bf16[3,256,256]{2,1,0:T(8,128)(2,1)S(1)}) custom-call(s32[4,4,4]{2,1,0:T(4,128)} %ids_in.3, bf16[4,32,64]{2,1,0:T(8,128)(2,1)S(1)} %get-tuple-element.25.lows, ...), custom_call_target="tpu_custom_call" | custom-call | flops 1610612736 | bytes 4194304 | tf_op jit(solution)/shard_map/pallas_call | solution.py:373
  10.6 0.0 collective-permute-done.fetched
  10.6 0.5 %collective-permute-start.1 = (bf16[2,2,4096]{2,1,0:T(2,128)(2,1)S(1)}, bf16[2,2,4096]{2,1,0:T(2,128)(2,1)S(1)}, u32[]{:S(2)}, u32[]{:S(2)}) collective-permute-start(bf16[2,2,4096]{2,1,0:T(2,128)(2,1)S(1)} %collective-permute-done.fetched), channel_id=1, source_target_pairs={{0,8},{16,24},{8,0},{24,16},{1,9},{17,25},{9,1},{25,17},{2,10},{18... | collective-permute-start | bytes 98312 | tf_op jit(solution)/shard_map/ppermute | solution.py:312
  11.1 0.9 %collective-permute-done.1.passed = bf16[2,2,4096]{2,1,0:T(2,128)(2,1)S(1)} collective-permute-done((bf16[2,2,4096]{2,1,0:T(2,128)(2,1)S(1)}, bf16[2,2,4096]{2,1,0:T(2,128)(2,1)S(1)}, u32[]{:S(2)}, u32[]{:S(2)}) %collective-permute-start.1) | collective-permute-done | bytes 32800 | tf_op jit(solution)/shard_map/ppermute | solution.py:312
  12.0 3.3 %shard_map.48 = (bf16[768,4096]{1,0:T(8,128)(2,1)S(1)}, bf16[768,2048]{1,0:T(8,128)(2,1)S(1)}) custom-call(bf16[16,16]{1,0:T(8,128)(2,1)S(1)} %get-tuple-element.32.pick, bf16[2,2,4096]{2,1,0:T(2,128)(2,1)S(1)} %collective-permute-done.fetched, bf16[2,2,4096]{2,1,0:T(2,128)(2,1)S(1)} %collective-permute-done.1.passed, ...), custom_call_target="tpu_custom_call" | custom-call | flops 2415919104 | bytes 10485760 | tf_op jit(solution)/shard_map/pallas_call | solution.py:390
  15.3 0.0 collective-permute-done.3.other
  15.3 1.4 %shard_map.51 = (f32[256,256]{1,0:T(8,128)S(1)}, bf16[256,256]{1,0:T(8,128)(2,1)S(1)}) custom-call(f32[3,16,256]{2,1,0:T(8,128)S(1)} %get-tuple-element.29.masks, f32[16,256]{1,0:T(8,128)S(1)} %get-tuple-element.30.left, bf16[3,256,256]{2,1,0:T(8,128)(2,1)S(1)} %get-tuple-element.31.place, bf16[768,4096]{1,0:T(8,128)(2,1)S(1)} %get-tuple-element.39.y_all, ...), custom_call_target="tpu_custom_call" | custom-call | flops 805306368 | bytes 8388608 | tf_op jit(solution)/shard_map/pallas_call | solution.py:405
  16.8 0.4 collective-permute-start.4
  17.2 3.3 %collective-permute-done.2.other = bf16[4,64,2048]{2,1,0:T(8,128)(2,1)S(1)} collective-permute-done((bf16[4,64,2048]{2,1,0:T(8,128)(2,1)S(1)}, bf16[4,64,2048]{2,1,0:T(8,128)(2,1)S(1)}, u32[]{:S(2)}, u32[]{:S(2)}) %collective-permute-start.2) | collective-permute-done | bytes 1048608 | tf_op jit(solution)/shard_map/ppermute | solution.py:312
  20.5 1.4 %shard_map.49 = (f32[256,256]{1,0:T(8,128)S(1)}, bf16[256,256]{1,0:T(8,128)(2,1)S(1)}) custom-call(f32[3,16,256]{2,1,0:T(8,128)S(1)} %get-tuple-element.29.masks, f32[16,256]{1,0:T(8,128)S(1)} %get-tuple-element.30.left, bf16[3,256,256]{2,1,0:T(8,128)(2,1)S(1)} %get-tuple-element.31.place, bf16[768,4096]{1,0:T(8,128)(2,1)S(1)} %get-tuple-element.39.y_all, ...), custom_call_target="tpu_custom_call" | custom-call | flops 805306368 | bytes 8388608 | tf_op jit(solution)/shard_map/pallas_call | solution.py:405
  21.9 3.6 %collective-permute-start.5 = (bf16[256,256]{1,0:T(8,128)(2,1)S(1)}, bf16[256,256]{1,0:T(8,128)(2,1)S(1)}, u32[]{:S(2)}, u32[]{:S(2)}) collective-permute-start(bf16[256,256]{1,0:T(8,128)(2,1)S(1)} %get-tuple-element.41.after), channel_id=1, source_target_pairs={{8,16},{16,8},{9,17},{17,9},{10,18},{18,10},{11,19},{19,11},{12,20... | collective-permute-start | bytes 393224 | tf_op jit(solution)/shard_map/ppermute | solution.py:312
  25.6 2.2 %shard_map.50.middle = f32[256,256]{1,0:T(8,128)S(1)} custom-call(f32[3,16,256]{2,1,0:T(8,128)S(1)} %get-tuple-element.29.masks, f32[16,256]{1,0:T(8,128)S(1)} %get-tuple-element.30.left, bf16[3,256,256]{2,1,0:T(8,128)(2,1)S(1)} %get-tuple-element.31.place, bf16[768,4096]{1,0:T(8,128)(2,1)S(1)} %get-tuple-element.39.y_all, ...), custom_call_target="tpu_custom_call" | custom-call | flops 1610612736 | bytes 8388608 | tf_op jit(solution)/shard_map/pallas_call | solution.py:419
  27.8 0.0 collective-permute-done.4.got_even
  27.8 0.4 collective-permute-done.5.got_odd
  28.2 0.1 shard_map.52
  28.3 14.6 %all_to_all.5 = bf16[8,32,768]{2,1,0:T(8,128)(2,1)S(1)} all-to-all(bf16[8,32,768]{2,1,0:T(8,128)(2,1)S(1)} %bitcast.1), channel_id=1, replica_groups=mesh['grp'=4,'mem'=8] {'mem'}, dimensions={0} | all-to-all | bytes 786432 | tf_op jit(solution)/shard_map/all_to_all | solution.py:435
  42.8 0.7 %convert_reduce_fusion = f32[32,768]{1,0:T(8,128)} fusion(bf16[8,32,768]{2,1,0:T(8,128)(2,1)S(1)} %all_to_all.5), kind=kLoop, calls=%fused_computation | loop fusion | flops 368640 | bytes 491520 | tf_op jit(solution)/shard_map/reduce_sum | solution.py:436
Async XLA Ops:
  3.4 11.9 %collective-permute-start.3 = (bf16[4,64,2048]{2,1,0:T(8,128)(2,1)S(1)}, bf16[4,64,2048]{2,1,0:T(8,128)(2,1)S(1)}, u32[]{:S(2)}, u32[]{:S(2)}) collective-permute-start(bf16[4,64,2048]{2,1,0:T(8,128)(2,1)S(1)} %get-tuple-element.27.even), channel_id=1, source_target_pairs={{0,8},{16,24},{8,0},{24,16},{1,9},{17,25},{9,1},{25,17},{2,10},{18... | collective-permute-start | bytes 3145736 | tf_op jit(solution)/shard_map/ppermute | solution.py:312
  3.5 16.9 %collective-permute-start.2 = (bf16[4,64,2048]{2,1,0:T(8,128)(2,1)S(1)}, bf16[4,64,2048]{2,1,0:T(8,128)(2,1)S(1)}, u32[]{:S(2)}, u32[]{:S(2)}) collective-permute-start(bf16[4,64,2048]{2,1,0:T(8,128)(2,1)S(1)} %get-tuple-element.28.odd), channel_id=1, source_target_pairs={{8,16},{16,8},{9,17},{17,9},{10,18},{18,10},{11,19},{19,11},{12,20... | collective-permute-start | bytes 3145736 | tf_op jit(solution)/shard_map/ppermute | solution.py:312
  8.0 2.6 %collective-permute-start = (bf16[2,2,4096]{2,1,0:T(2,128)(2,1)S(1)}, bf16[2,2,4096]{2,1,0:T(2,128)(2,1)S(1)}, u32[]{:S(2)}, u32[]{:S(2)}) collective-permute-start(bf16[2,2,4096]{2,1,0:T(2,128)(2,1)S(1)} %get-tuple-element.33), channel_id=1, source_target_pairs={{0,1},{1,0},{2,3},{3,2},{4,5},{5,4},{6,7},{7,6},{9,10},{10,9},{11,... | collective-permute-start | bytes 98312 | tf_op jit(solution)/shard_map/ppermute | solution.py:370
  10.6 1.4 %collective-permute-start.1 = (bf16[2,2,4096]{2,1,0:T(2,128)(2,1)S(1)}, bf16[2,2,4096]{2,1,0:T(2,128)(2,1)S(1)}, u32[]{:S(2)}, u32[]{:S(2)}) collective-permute-start(bf16[2,2,4096]{2,1,0:T(2,128)(2,1)S(1)} %collective-permute-done.fetched), channel_id=1, source_target_pairs={{0,8},{16,24},{8,0},{24,16},{1,9},{17,25},{9,1},{25,17},{2,10},{18... | collective-permute-start | bytes 98312 | tf_op jit(solution)/shard_map/ppermute | solution.py:312
  16.8 11.0 %collective-permute-start.4 = (bf16[256,256]{1,0:T(8,128)(2,1)S(1)}, bf16[256,256]{1,0:T(8,128)(2,1)S(1)}, u32[]{:S(2)}, u32[]{:S(2)}) collective-permute-start(bf16[256,256]{1,0:T(8,128)(2,1)S(1)} %get-tuple-element.44), channel_id=1, source_target_pairs={{0,8},{16,24},{8,0},{24,16},{1,9},{17,25},{9,1},{25,17},{2,10},{18... | collective-permute-start | bytes 393224 | tf_op jit(solution)/shard_map/ppermute | solution.py:312
  21.9 6.3 %collective-permute-start.5 = (bf16[256,256]{1,0:T(8,128)(2,1)S(1)}, bf16[256,256]{1,0:T(8,128)(2,1)S(1)}, u32[]{:S(2)}, u32[]{:S(2)}) collective-permute-start(bf16[256,256]{1,0:T(8,128)(2,1)S(1)} %get-tuple-element.41.after), channel_id=1, source_target_pairs={{8,16},{16,8},{9,17},{17,9},{10,18},{18,10},{11,19},{19,11},{12,20... | collective-permute-start | bytes 393224 | tf_op jit(solution)/shard_map/ppermute | solution.py:312
